TPU v7x, 256 devices: a whole 4x4x8 slice. The times are simulated.
256 devices in a mesh: cp: 32 (over y, z), tp: 8 (over x, core).
Axes of the slice: x: 4, y: 4, z: 8, core: 2. Of those that a mesh axis runs over, the one named last changes fastest.
Arguments:
- queries: bfloat16 [12288, 4096], P('cp', 'tp'), may hold values from -36 to 36
- keys: bfloat16 [12288, 1024], P('cp', 'tp'), may hold values from -6 to 6
- values: bfloat16 [12288, 1024], P('cp', 'tp'), may hold values from -18 to 18
- doc_lengths: int32 [4], replicated, may hold values from 1 to 4096, 8192 in all
- shard_starts: int32 [32], replicated, may hold values from 0 to 8000, as said below
- norm_gain: float32 [4096], replicated, may hold values from 0.1 to 1.9
- ffn_weight: bfloat16 [4096, 14336], P('cp', 'tp'), may hold values from -0.09375 to 0.09375
Outputs:
- ffn_out: bfloat16 [8192, 14336], P('cp', 'tp')
Inputs may be any that keep to these rules, and one draw needn't show every extreme that they name: `doc_lengths`: each of the 4 documents has at least one token; the longest has exactly 4096. shard_starts[0] = 0, the last start is exactly 64 past its index times 256, and shard_starts[c] differs from c * 256 by at most 64, so every shard holds 128 to 384 tokens, at most 64 of them owned by index c - 1 and at most 64 by index c + 1 of cp; in every draw some shard holds exactly 384 tokens and hands exactly 64 to each of those two owners.
All inputs are finite; a program needn't handle non-finite values.
Results may differ from a plain program's by a relative error of at most 0.017.
Values may be sent and summed in bfloat16 or wider, within the bound.
No kernel may reach another device: no remote copies, remote signals or barrier semaphores. Data moves between devices by JAX's collectives and lax.ppermute only.
A program may use at most 128 MiB of HBM per device.

v0:
```python
import functools

import jax
import jax.numpy as jnp
from jax import lax
from jax.experimental import pallas as pl
from jax.experimental.pallas import tpu as pltpu
from jax.sharding import Mesh, PartitionSpec as P

HD = 128
TOK = 256
CAP = 384
QUARTER = TOK // 4
FEATURES = 4096
TOKENS = 8192
NY, NZ, NX, NC = 4, 8, 4, 2
HEADS_HERE = 4
HERE = 4
NEAR = 3
NORM_EPS = 1e-05
MASKED = -1e30
LOG2E = 1.4426950408889634
EXP2_SCALE = HD ** (-0.5) * LOG2E
VMEM = pl.BlockSpec(memory_space=pltpu.VMEM)
SMEM = pl.BlockSpec(memory_space=pltpu.SMEM)
ROWS, COLUMNS, TALL = ("yp", "yb", "z"), ("x", "c"), ("yp", "yb")


def shift(block, axis, distance):
    count = lax.axis_size(axis)
    return lax.ppermute(block, axis, [(i, (i + distance) % count) for i in range(count)])


def here():
    y = lax.axis_index("yp") * 2 + lax.axis_index("yb")
    return y, lax.axis_index("z"), lax.axis_index("x"), lax.axis_index("c")


def shift_both(block, across, distance):
    pairs = [(b, i) for b in range(2) for i in range(NX)]
    to = lambda b, i: (b ^ across) * NX + (i + distance) % NX
    return lax.ppermute(block, ("yb", "x"), [(b * NX + i, to(b, i)) for b, i in pairs])


def z_ring(block):
    up, down = [block], [block]
    for _ in range(3):
        up.append(shift(up[-1], "z", 1))
        down.append(shift(down[-1], "z", -1))
    near = jnp.concatenate([shift(up[3], "z", 1), up[3], up[2]], axis=0)
    return near, jnp.concatenate([up[1], block, *down[1:]], axis=0)


def bf16(*shape):
    return jax.ShapeDtypeStruct(shape, jnp.bfloat16)


def f32(*shape):
    return jax.ShapeDtypeStruct(shape, jnp.float32)


def limit(mib):
    return pltpu.CompilerParams(vmem_limit_bytes=mib << 20)


def extent(starts):
    y, z, _, _ = here()
    mine = y * NZ + z
    after = jnp.where(mine == NY * NZ - 1, TOKENS, starts[jnp.minimum(mine + 1, NY * NZ - 1)])
    return starts[mine] - mine * TOK, after - mine * TOK


def cut_kernel(starts, q, k, v, up, down):
    first, _ = extent(starts)
    row = lax.broadcasted_iota(jnp.int32, (QUARTER, CAP), 0)
    slot = lax.broadcasted_iota(jnp.int32, (QUARTER, CAP), 1)
    last = (slot == row + TOK - first).astype(jnp.bfloat16)
    at = 0
    for ref in (q, k, v):
        wide = ref.shape[1]
        up[:, at : at + wide] = jnp.dot(last, ref[...], preferred_element_type=jnp.float32).astype(jnp.bfloat16)
        down[:, at : at + wide] = ref[:QUARTER]
        at += wide


def align_kernel(starts, q, k, v, low, high, q_out, kv_out):
    first, end = extent(starts)
    row = lax.broadcasted_iota(jnp.int32, (TOK, 1), 0)
    slot = lax.broadcasted_iota(jnp.int32, (TOK, CAP), 1)
    near = lax.broadcasted_iota(jnp.int32, (TOK, QUARTER), 1)
    own = ((slot == row - first) & (row >= first) & (row < end)).astype(jnp.bfloat16)
    from_low = ((near == row) & (row < first)).astype(jnp.bfloat16)
    from_high = ((near == row - end) & (row >= end)).astype(jnp.bfloat16)
    at = 0
    for ref, out, place in ((q, q_out, 0), (k, kv_out, 0), (v, kv_out, HD)):
        wide = ref.shape[1]
        total = jnp.dot(own, ref[...], preferred_element_type=jnp.float32)
        total += jnp.dot(from_low, low[:, at : at + wide], preferred_element_type=jnp.float32)
        total += jnp.dot(from_high, high[:, at : at + wide], preferred_element_type=jnp.float32)
        out[:, place : place + wide] = total.astype(jnp.bfloat16)
        at += wide


def cut(starts, q, k, v):
    wide = q.shape[1] + k.shape[1] + v.shape[1]
    return pl.pallas_call(
        cut_kernel,
        out_shape=(bf16(QUARTER, wide),) * 2,
        in_specs=[SMEM] + [VMEM] * 3,
        out_specs=(VMEM,) * 2,
        compiler_params=limit(16),
    )(starts, q, k, v)


def align(starts, q, k, v, up, down):
    count = NY * NZ
    low = lax.ppermute(up, ROWS, [(i, (i + 1) % count) for i in range(count)])
    high = lax.ppermute(down, ROWS, [(i, (i - 1) % count) for i in range(count)])
    return pl.pallas_call(
        align_kernel,
        out_shape=(bf16(TOK, q.shape[1]), bf16(TOK, 2 * HD)),
        in_specs=[SMEM] + [VMEM] * 5,
        out_specs=(VMEM,) * 2,
        compiler_params=limit(16),
    )(starts, q, k, v, low, high)


def attention_kernel(back, parts, place, lengths, q_ref, *refs):
    blocks, refs = refs[:parts], refs[parts:]
    if back:
        old_stats, old_sums, *refs = refs
    if back == 2:
        out_ref, stats, sums = refs
    else:
        stats, sums = refs
    y, z = place() if callable(place) else place
    ends, total = [], 0
    for i in range(4):
        total += lengths[i]
        ends.append(total)
    mine = y * NZ + z
    query = mine * TOK + lax.broadcasted_iota(jnp.int32, (1, TOK), 1)

    def start_of(token):
        start = token * 0
        for end in ends:
            start = jnp.maximum(start, jnp.where(end <= token, end, 0))
        return start

    starts = start_of(query)
    lowest = start_of(mine * TOK) // TOK
    clear = (start_of(mine * TOK + TOK - 1) + TOK - 1) // TOK

    def step(ref, row, block, masked, opening):
        key, value = ref[pl.ds(row, TOK), :HD], ref[pl.ds(row, TOK), HD:]
        heads = range(HEADS_HERE)
        scores = [
            lax.dot_general(
                key, q_ref[:, h * HD : (h + 1) * HD], (((1,), (1,)), ((), ())), preferred_element_type=jnp.float32
            )
            for h in heads
        ]
        if masked:
            ids = block * TOK + lax.broadcasted_iota(jnp.int32, (TOK, 1), 0)
            allowed = (ids >= starts) & (ids <= query)
            scores = [jnp.where(allowed, s, MASKED) for s in scores]
        tops = [jnp.max(s, axis=0, keepdims=True) * EXP2_SCALE for s in scores]
        if not opening:
            was = [stats[h : h + 1] for h in heads]
            tops = [jnp.maximum(a, b) for a, b in zip(tops, was)]
            fading = [jnp.exp2(a - b) for a, b in zip(was, tops)]
        weights = [jnp.exp2(s * EXP2_SCALE - t) for s, t in zip(scores, tops)]
        mass = [jnp.sum(w, axis=0, keepdims=True) for w in weights]
        added = [
            lax.dot_general(
                value, w.astype(jnp.bfloat16), (((0,), (0,)), ((), ())), preferred_element_type=jnp.float32
            )
            for w in weights
        ]
        if not opening:
            mass = [m + stats[4 + h : 5 + h] * f for h, m, f in zip(heads, mass, fading)]
            added = [a + sums[h] * f for h, a, f in zip(heads, added, fading)]
        for h in heads:
            stats[h : h + 1] = tops[h]
            stats[4 + h : 5 + h] = mass[h]
            sums[h] = added[h]

    if back:
        stats[...] = old_stats[...]
        sums[...] = old_sums[...]
    else:
        step(blocks[1], (HERE - NEAR) * TOK, mine, True, True)
    before = 0
    for ref in blocks:

        def body(i, _, ref=ref, before=before):
            block = (y - back) * NZ + lax.rem(z + before + i - HERE + NZ, NZ)
            needed = (block >= lowest) & (block < mine)
            row = pl.multiple_of(i * TOK, TOK)

            @pl.when(needed & (block < clear))
            def _():
                step(ref, row, block, True, False)

            @pl.when(needed & (block >= clear))
            def _():
                step(ref, row, block, False, False)

            return 0

        lax.fori_loop(0, ref.shape[0] // TOK, body, 0)
        before += ref.shape[0] // TOK
    if back == 2:
        for h in range(HEADS_HERE):
            out_ref[:, h * HD : (h + 1) * HD] = (sums[h] / stats[4 + h : 5 + h]).T.astype(jnp.bfloat16)


def attention(back, lengths, q, blocks, state, place=lambda: here()[:2]):
    shapes = [f32(2 * HEADS_HERE, TOK), f32(HEADS_HERE, HD, TOK)]
    kwargs = {}
    if back == 2:
        kwargs["scratch_shapes"] = [pltpu.VMEM(s.shape, s.dtype) for s in shapes]
        shapes = [bf16(TOK, HEADS_HERE * HD)]
    work = 8 * HEADS_HERE * TOK * TOK
    return pl.pallas_call(
        functools.partial(attention_kernel, back, len(blocks), place),
        out_shape=tuple(shapes),
        in_specs=[SMEM] + [VMEM] * (1 + len(blocks) + len(state)),
        out_specs=(VMEM,) * len(shapes),
        compiler_params=limit(32),
        cost_estimate=pl.CostEstimate(flops=4 * work * HD, bytes_accessed=4 << 20, transcendentals=work),
        **kwargs,
    )(lengths, q, *blocks, *state)


def gate_kernel(gain, mine, other, weight, out, rows):
    y, _, x, c = here()
    squares = jnp.zeros((TOK, HD), jnp.float32)
    for side, pieces in enumerate((mine, other)):
        for i in range(NX):
            tp = lax.rem(x + (0, 3, 1, 2)[i], NX) * NC + (c if side == 0 else 1 - c)
            for j in range(HEADS_HERE):
                head = tp * HEADS_HERE + j
                part = pieces[i * TOK : (i + 1) * TOK, j * HD : (j + 1) * HD].astype(jnp.float32)
                squares += part * part
                scaled = (part * gain[:, pl.ds(pl.multiple_of(head * HD, HD), HD)]).astype(jnp.bfloat16)
                away = lax.rem(head // NZ - y + NY, NY)
                slot = jnp.where(away == 0, 0, jnp.where(away == 3, 1, away + 1))
                place = lax.rem(head, NZ) * NY + slot
                rows[:, pl.ds(pl.multiple_of(place * HD, HD), HD)] = scaled
    inv = lax.rsqrt(jnp.sum(squares, axis=1, keepdims=True) / FEATURES + NORM_EPS)

    def columns(i, _):
        at = pl.ds(pl.multiple_of(i * HD, HD), HD)
        value = jnp.dot(rows[...], weight[:, at], preferred_element_type=jnp.float32) * inv
        out[:, at] = (value / (1.0 + jnp.exp(-value))).astype(jnp.bfloat16)
        return 0

    lax.fori_loop(0, out.shape[1] // HD, columns, 0)


def gate(gain, mine, other, weight):
    columns = weight.shape[1]
    return pl.pallas_call(
        gate_kernel,
        out_shape=bf16(TOK, columns),
        in_specs=[VMEM] * 4,
        out_specs=VMEM,
        scratch_shapes=[pltpu.VMEM((TOK, FEATURES), jnp.bfloat16)],
        compiler_params=limit(24),
        cost_estimate=pl.CostEstimate(
            flops=2 * TOK * FEATURES * columns, bytes_accessed=2 * FEATURES * columns, transcendentals=TOK * columns
        ),
    )(gain, mine, other, weight)


def join_kernel(home, back, out):
    columns = home.shape[1]
    odd = lax.rem(here()[0], 2)
    out[:, pl.ds(pl.multiple_of(odd * columns, HD), columns)] = home[...]
    out[:, pl.ds(pl.multiple_of((1 - odd) * columns, HD), columns)] = back[...]


def join(home, back):
    return pl.pallas_call(
        join_kernel,
        out_shape=bf16(TOK, 2 * home.shape[1]),
        in_specs=[VMEM] * 2,
        out_specs=VMEM,
        compiler_params=limit(8),
    )(home, back)


def on_device(queries, keys, values, doc_lengths, shard_starts, norm_gain, ffn_weight):
    half = ffn_weight.shape[1] // 2
    odd = lax.axis_index("yb") == 1

    with jax.named_scope("rows_to_owners"):
        up, down = cut(shard_starts, queries, keys, values)
        odd, up, down = lax.optimization_barrier((odd, up, down))
        q, kv = align(shard_starts, queries, keys, values, up, down)

    with jax.named_scope("weight_rows"):
        left, right = ffn_weight[:, :half], ffn_weight[:, half:]
        theirs, mine = jnp.where(odd, left, right), jnp.where(odd, right, left)
        parts = [mine, shift(theirs, TALL, 1), shift(theirs, TALL, -1), shift(mine, TALL, 2)]
        *parts, kv = lax.optimization_barrier((*parts, kv))
        weight = lax.all_gather(jnp.concatenate(parts, axis=0), "z", axis=0, tiled=True)

    with jax.named_scope("keys_and_values"):
        near, far = z_ring(kv)
        near1, far3 = shift(near, TALL, 1), shift(far, TALL, -1)
        far1 = shift(far, TALL, 1)
        near2, far2 = shift(near1, TALL, 1), shift(far3, TALL, -1)

    with jax.named_scope("attention"):
        state = attention(0, doc_lengths, q, [near, far], ())
        state = attention(1, doc_lengths, q, [near1, far1], state)
        (attended,) = attention(2, doc_lengths, q, [near2, far2], state)

    gain = norm_gain.reshape(1, FEATURES)
    with jax.named_scope("features_of_the_pair"):
        pieces = [shift_both(attended, 1, d) for d in (0, 1, -1, 2)]
        own = [attended] + [shift(attended, "x", d) for d in (1, -1, 2)]
        mine = jnp.concatenate(pieces, axis=0)
        away = gate(gain, mine, shift(mine, "c", 1), weight)

    with jax.named_scope("features"):
        *own, away = lax.optimization_barrier((*own, away))
        mine = jnp.concatenate(own, axis=0)
        home = gate(gain, mine, shift(mine, "c", 1), weight)
        return join(home, shift(away, "yb", 1))


def solution(mesh):
    fine = Mesh(mesh.devices.reshape(NY // 2, 2, NZ, NX, NC), ("yp", "yb", "z", "x", "c"))
    return jax.shard_map(
        on_device,
        mesh=fine,
        in_specs=(P(ROWS, COLUMNS), P(ROWS, COLUMNS), P(ROWS, COLUMNS), P(), P(), P(), P(ROWS, COLUMNS)),
        out_specs=P(ROWS, COLUMNS),
        check_vma=False,
    )
```

profile of v0, /device:TPU:1, one launch (start us, length us, event | category | flops | bytes accessed | tf_op | source)
XLA Modules:
  0.0 161.3 jit_solution(14721514672384949773)
XLA Ops:
  11.9 2.2 %collective-permute-start.2 = (bf16[128,896]{1,0:T(8,128)(2,1)S(1)}, bf16[128,896]{1,0:T(8,128)(2,1)S(1)}, u32[]{:S(2)}, u32[]{:S(2)}) collective-permute-start(bf16[128,896]{1,0:T(8,128)(2,1)S(1)} %get-tuple-element.47), channel_id=1, source_target_pairs={{0,64},{64,128},{128,192},{192,0},{1,65},{65,129},{129,193},{193,1... | collective-permute-start | bytes 688136 | tf_op jit(solution)/shard_map/weight_rows/ppermute | solution.py:31
  14.1 1.5 collective-permute-start.3
  15.6 1.6 collective-permute-start.4
  17.1 1.6 %collective-permute-start = (bf16[64,768]{1,0:T(8,128)(2,1)S(1)}, bf16[64,768]{1,0:T(8,128)(2,1)S(1)}, u32[]{:S(2)}, u32[]{:S(2)}) collective-permute-start(bf16[64,768]{1,0:T(8,128)(2,1)S(1)} %get-tuple-element.28), channel_id=1, source_target_pairs={{0,8},{8,16},{16,24},{24,32},{32,40},{40,48},{48,56},{56,64},{64,7... | collective-permute-start | bytes 294920 | tf_op jit(solution)/shard_map/rows_to_owners/ppermute | solution.py:117
  18.8 4.4 %collective-permute-start.1 = (bf16[64,768]{1,0:T(8,128)(2,1)S(1)}, bf16[64,768]{1,0:T(8,128)(2,1)S(1)}, u32[]{:S(2)}, u32[]{:S(2)}) collective-permute-start(bf16[64,768]{1,0:T(8,128)(2,1)S(1)} %get-tuple-element.29), channel_id=1, source_target_pairs={{0,248},{8,0},{16,8},{24,16},{32,24},{40,32},{48,40},{56,48},{64,5... | collective-permute-start | bytes 294920 | tf_op jit(solution)/shard_map/rows_to_owners/ppermute | solution.py:118
  23.2 2.7 %collective-permute-done.low = bf16[64,768]{1,0:T(8,128)(2,1)S(1)} collective-permute-done((bf16[64,768]{1,0:T(8,128)(2,1)S(1)}, bf16[64,768]{1,0:T(8,128)(2,1)S(1)}, u32[]{:S(2)}, u32[]{:S(2)}) %collective-permute-start) | collective-permute-done | bytes 98336 | tf_op jit(solution)/shard_map/rows_to_owners/ppermute | solution.py:117
  27.1 1.6 collective-permute-done.4
  29.7 3.6 %collective-permute-start.11 = (bf16[256,256]{1,0:T(8,128)(2,1)S(1)}, bf16[256,256]{1,0:T(8,128)(2,1)S(1)}, u32[]{:S(2)}, u32[]{:S(2)}) collective-permute-start(bf16[256,256]{1,0:T(8,128)(2,1)S(1)} %get-tuple-element.33), channel_id=1, source_target_pairs={{0,56},{8,0},{16,8},{24,16},{32,24},{40,32},{48,40},{56,48},{1,57}... | collective-permute-start | bytes 393224 | tf_op jit(solution)/shard_map/keys_and_values/ppermute | solution.py:31
  33.3 1.9 %collective-permute-done.11 = bf16[256,256]{1,0:T(8,128)(2,1)S(1)} collective-permute-done((bf16[256,256]{1,0:T(8,128)(2,1)S(1)}, bf16[256,256]{1,0:T(8,128)(2,1)S(1)}, u32[]{:S(2)}, u32[]{:S(2)}) %collective-permute-start.11) | collective-permute-done | bytes 131104 | tf_op jit(solution)/shard_map/keys_and_values/ppermute | solution.py:31
  35.2 3.1 %collective-permute-start.12 = (bf16[256,256]{1,0:T(8,128)(2,1)S(1)}, bf16[256,256]{1,0:T(8,128)(2,1)S(1)}, u32[]{:S(2)}, u32[]{:S(2)}) collective-permute-start(bf16[256,256]{1,0:T(8,128)(2,1)S(1)} %collective-permute-done.11), channel_id=1, source_target_pairs={{0,56},{8,0},{16,8},{24,16},{32,24},{40,32},{48,40},{56,48},{1,57}... | collective-permute-start | bytes 393224 | tf_op jit(solution)/shard_map/keys_and_values/ppermute | solution.py:31
  38.4 1.8 %collective-permute-done.12 = bf16[256,256]{1,0:T(8,128)(2,1)S(1)} collective-permute-done((bf16[256,256]{1,0:T(8,128)(2,1)S(1)}, bf16[256,256]{1,0:T(8,128)(2,1)S(1)}, u32[]{:S(2)}, u32[]{:S(2)}) %collective-permute-start.12) | collective-permute-done | bytes 131104 | tf_op jit(solution)/shard_map/keys_and_values/ppermute | solution.py:31
  40.3 3.1 %collective-permute-start.13 = (bf16[256,256]{1,0:T(8,128)(2,1)S(1)}, bf16[256,256]{1,0:T(8,128)(2,1)S(1)}, u32[]{:S(2)}, u32[]{:S(2)}) collective-permute-start(bf16[256,256]{1,0:T(8,128)(2,1)S(1)} %collective-permute-done.12), channel_id=1, source_target_pairs={{0,56},{8,0},{16,8},{24,16},{32,24},{40,32},{48,40},{56,48},{1,57}... | collective-permute-start | bytes 393224 | tf_op jit(solution)/shard_map/keys_and_values/ppermute | solution.py:31
  43.5 5.1 %collective-permute-done.13 = bf16[256,256]{1,0:T(8,128)(2,1)S(1)} collective-permute-done((bf16[256,256]{1,0:T(8,128)(2,1)S(1)}, bf16[256,256]{1,0:T(8,128)(2,1)S(1)}, u32[]{:S(2)}, u32[]{:S(2)}) %collective-permute-start.13) | collective-permute-done | bytes 131104 | tf_op jit(solution)/shard_map/keys_and_values/ppermute | solution.py:31
  48.5 3.5 %collective-permute-start.14 = (bf16[1280,256]{1,0:T(8,128)(2,1)S(1)}, bf16[1280,256]{1,0:T(8,128)(2,1)S(1)}, u32[]{:S(2)}, u32[]{:S(2)}) collective-permute-start(bf16[1280,256]{1,0:T(8,128)(2,1)S(1)} %constant_dynamic-update-slice_fusion.3.refs_1_), channel_id=1, source_target_pairs={{0,192},{64,0},{128,64},{192,128},{1,193},{65,1},{129,65},{193,129... | collective-permute-start | bytes 1966088 | tf_op jit(solution)/shard_map/keys_and_values/ppermute | solution.py:31
  52.3 9.8 %collective-permute-done.8 = bf16[256,256]{1,0:T(8,128)(2,1)S(1)} collective-permute-done((bf16[256,256]{1,0:T(8,128)(2,1)S(1)}, bf16[256,256]{1,0:T(8,128)(2,1)S(1)}, u32[]{:S(2)}, u32[]{:S(2)}) %collective-permute-start.8) | collective-permute-done | bytes 131104 | tf_op jit(solution)/shard_map/keys_and_values/ppermute | solution.py:31
  62.2 2.5 %collective-permute-start.9 = (bf16[768,256]{1,0:T(8,128)(2,1)S(1)}, bf16[768,256]{1,0:T(8,128)(2,1)S(1)}, u32[]{:S(2)}, u32[]{:S(2)}) collective-permute-start(bf16[768,256]{1,0:T(8,128)(2,1)S(1)} %constant_dynamic-update-slice_fusion.refs_0_), channel_id=1, source_target_pairs={{0,64},{64,128},{128,192},{192,0},{1,65},{65,129},{129,193},{193,1... | collective-permute-start | bytes 1179656 | tf_op jit(solution)/shard_map/keys_and_values/ppermute | solution.py:31
  65.0 2.4 %collective-permute-start.15 = (bf16[1280,256]{1,0:T(8,128)(2,1)S(1)}, bf16[1280,256]{1,0:T(8,128)(2,1)S(1)}, u32[]{:S(2)}, u32[]{:S(2)}) collective-permute-start(bf16[1280,256]{1,0:T(8,128)(2,1)S(1)} %collective-permute-done.14), channel_id=1, source_target_pairs={{0,192},{64,0},{128,64},{192,128},{1,193},{65,1},{129,65},{193,129... | collective-permute-start | bytes 1966088 | tf_op jit(solution)/shard_map/keys_and_values/ppermute | solution.py:31
  67.4 3.4 %collective-permute-done.9.refs_0_ = bf16[768,256]{1,0:T(8,128)(2,1)S(1)} collective-permute-done((bf16[768,256]{1,0:T(8,128)(2,1)S(1)}, bf16[768,256]{1,0:T(8,128)(2,1)S(1)}, u32[]{:S(2)}, u32[]{:S(2)}) %collective-permute-start.9) | collective-permute-done | bytes 393248 | tf_op jit(solution)/shard_map/keys_and_values/ppermute | solution.py:31
  71.7 1.4 attention.3
  73.1 6.7 %collective-permute-done.16.refs_1_ = bf16[1280,256]{1,0:T(8,128)(2,1)S(1)} collective-permute-done((bf16[1280,256]{1,0:T(8,128)(2,1)S(1)}, bf16[1280,256]{1,0:T(8,128)(2,1)S(1)}, u32[]{:S(2)}, u32[]{:S(2)}) %collective-permute-start.16) | collective-permute-done | bytes 655392 | tf_op jit(solution)/shard_map/keys_and_values/ppermute | solution.py:31
  80.6 7.7 %collective-permute-done.10.refs_0_ = bf16[768,256]{1,0:T(8,128)(2,1)S(1)} collective-permute-done((bf16[768,256]{1,0:T(8,128)(2,1)S(1)}, bf16[768,256]{1,0:T(8,128)(2,1)S(1)}, u32[]{:S(2)}, u32[]{:S(2)}) %collective-permute-start.10) | collective-permute-done | bytes 393248 | tf_op jit(solution)/shard_map/keys_and_values/ppermute | solution.py:31
  91.7 2.2 %collective-permute-start.22 = (bf16[256,512]{1,0:T(8,128)(2,1)S(1)}, bf16[256,512]{1,0:T(8,128)(2,1)S(1)}, u32[]{:S(2)}, u32[]{:S(2)}) collective-permute-start(bf16[256,512]{1,0:T(8,128)(2,1)S(1)} %attention.5), channel_id=1, source_target_pairs={{0,70},{2,64},{4,66},{6,68},{64,6},{66,0},{68,2},{70,4},{1,71},{3,... | collective-permute-start | bytes 786440 | tf_op jit(solution)/shard_map/features_of_the_pair/ppermute | solution.py:42
  93.9 1.7 %collective-permute-start.23 = (bf16[256,512]{1,0:T(8,128)(2,1)S(1)}, bf16[256,512]{1,0:T(8,128)(2,1)S(1)}, u32[]{:S(2)}, u32[]{:S(2)}) collective-permute-start(bf16[256,512]{1,0:T(8,128)(2,1)S(1)} %attention.5), channel_id=1, source_target_pairs={{0,68},{2,70},{4,64},{6,66},{64,4},{66,6},{68,0},{70,2},{1,69},{3,... | collective-permute-start | bytes 786440 | tf_op jit(solution)/shard_map/features_of_the_pair/ppermute | solution.py:42
  95.6 9.4 %collective-permute-done.20 = bf16[256,512]{1,0:T(8,128)(2,1)S(1)} collective-permute-done((bf16[256,512]{1,0:T(8,128)(2,1)S(1)}, bf16[256,512]{1,0:T(8,128)(2,1)S(1)}, u32[]{:S(2)}, u32[]{:S(2)}) %collective-permute-start.20) | collective-permute-done | bytes 262176 | tf_op jit(solution)/shard_map/features_of_the_pair/ppermute | solution.py:42
  105.1 20.2 %collective-permute-start.24 = (bf16[1024,512]{1,0:T(8,128)(2,1)S(1)}, bf16[1024,512]{1,0:T(8,128)(2,1)S(1)}, u32[]{:S(2)}, u32[]{:S(2)}) collective-permute-start(bf16[1024,512]{1,0:T(8,128)(2,1)S(1)} %constant_dynamic-update-slice_fusion.8.mine), channel_id=1, source_target_pairs={{0,1},{1,0},{2,3},{3,2},{4,5},{5,4},{6,7},{7,6},{8,9},{9,8},{10,11... | collective-permute-start | bytes 3145736 | tf_op jit(solution)/shard_map/features_of_the_pair/ppermute | solution.py:31
  126.1 1.9 %collective-permute-start.18 = (bf16[256,512]{1,0:T(8,128)(2,1)S(1)}, bf16[256,512]{1,0:T(8,128)(2,1)S(1)}, u32[]{:S(2)}, u32[]{:S(2)}) collective-permute-start(bf16[256,512]{1,0:T(8,128)(2,1)S(1)} %attention.5), channel_id=1, source_target_pairs={{0,6},{2,0},{4,2},{6,4},{1,7},{3,1},{5,3},{7,5},{8,14},{10,8},{12,... | collective-permute-start | bytes 786440 | tf_op jit(solution)/shard_map/features_of_the_pair/ppermute | solution.py:31
  128.5 3.1 %copy-done = bf16[4096,896]{1,0:T(8,128)(2,1)S(1)} copy-done((bf16[4096,896]{1,0:T(8,128)(2,1)S(1)}, bf16[4096,896]{1,0:T(8,128)(2,1)}, u32[]{:S(2)}) %copy-start) | copy-done | bytes 7340056
  131.6 6.1 %features_of_the_pair.1 = bf16[256,896]{1,0:T(8,128)(2,1)S(1)} custom-call(f32[1,4096]{1,0:T(1,128)S(1)} %bitcast.1, bf16[1024,512]{1,0:T(8,128)(2,1)S(1)} %constant_dynamic-update-slice_fusion.8.mine, bf16[1024,512]{1,0:T(8,128)(2,1)S(1)} %collective-permute-done.24.other, bf16[4096,896]{1,0:T(8,128)(2,1)S(1)} %copy-done), custom_call_target="tpu_custom_call" | custom-call | flops 1879048192 | bytes 7340032 | tf_op jit(solution)/shard_map/features_of_the_pair/pallas_call | solution.py:264
  137.8 2.2 %collective-permute-done.19 = bf16[256,512]{1,0:T(8,128)(2,1)S(1)} collective-permute-done((bf16[256,512]{1,0:T(8,128)(2,1)S(1)}, bf16[256,512]{1,0:T(8,128)(2,1)S(1)}, u32[]{:S(2)}, u32[]{:S(2)}) %collective-permute-start.19) | collective-permute-done | bytes 262176 | tf_op jit(solution)/shard_map/features_of_the_pair/ppermute | solution.py:31
  141.3 1.4 collective-permute-start.26
  143.6 6.1 %features.2.home = bf16[256,896]{1,0:T(8,128)(2,1)S(1)} custom-call(f32[1,4096]{1,0:T(1,128)S(1)} %bitcast.2, bf16[1024,512]{1,0:T(8,128)(2,1)S(1)} %constant_dynamic-update-slice_fusion.12.mine, bf16[1024,512]{1,0:T(8,128)(2,1)S(1)} %collective-permute-done.25.other, bf16[4096,896]{1,0:T(8,128)(2,1)S(1)} %copy-done.1), custom_call_target="tpu_custom_call" | custom-call | flops 1879048192 | bytes 7340032 | tf_op jit(solution)/shard_map/features/pallas_call | solution.py:264
  149.8 3.6 %collective-permute-done.26.back = bf16[256,896]{1,0:T(8,128)(2,1)S(1)} collective-permute-done((bf16[256,896]{1,0:T(8,128)(2,1)S(1)}, bf16[256,896]{1,0:T(8,128)(2,1)S(1)}, u32[]{:S(2)}, u32[]{:S(2)}) %collective-permute-start.26) | collective-permute-done | bytes 458784 | tf_op jit(solution)/shard_map/features/ppermute | solution.py:31
  (67 shorter events, 18.1 us)
Async XLA Ops:
  6.5 122.0 %all-gather.2.cloned.1.call-start = ((), (), s32[]{:S(2)}) async-start(), calls=%async_computation | async-start | bytes 8257536 | tf_op jit(solution)/shard_map/weight_rows/all_gather | solution.py:308
  11.9 15.2 %collective-permute-start.2 = (bf16[128,896]{1,0:T(8,128)(2,1)S(1)}, bf16[128,896]{1,0:T(8,128)(2,1)S(1)}, u32[]{:S(2)}, u32[]{:S(2)}) collective-permute-start(bf16[128,896]{1,0:T(8,128)(2,1)S(1)} %get-tuple-element.47), channel_id=1, source_target_pairs={{0,64},{64,128},{128,192},{192,0},{1,65},{65,129},{129,193},{193,1... | collective-permute-start | bytes 688136 | tf_op jit(solution)/shard_map/weight_rows/ppermute | solution.py:31
  14.1 13.1 %collective-permute-start.3 = (bf16[128,896]{1,0:T(8,128)(2,1)S(1)}, bf16[128,896]{1,0:T(8,128)(2,1)S(1)}, u32[]{:S(2)}, u32[]{:S(2)}) collective-permute-start(bf16[128,896]{1,0:T(8,128)(2,1)S(1)} %get-tuple-element.47), channel_id=1, source_target_pairs={{0,192},{64,0},{128,64},{192,128},{1,193},{65,1},{129,65},{193,129... | collective-permute-start | bytes 688136 | tf_op jit(solution)/shard_map/weight_rows/ppermute | solution.py:31
  15.6 13.1 %collective-permute-start.4 = (bf16[128,896]{1,0:T(8,128)(2,1)S(1)}, bf16[128,896]{1,0:T(8,128)(2,1)S(1)}, u32[]{:S(2)}, u32[]{:S(2)}) collective-permute-start(bf16[128,896]{1,0:T(8,128)(2,1)S(1)} %get-tuple-element.38), channel_id=1, source_target_pairs={{0,128},{64,192},{128,0},{192,64},{1,129},{65,193},{129,1},{193,65... | collective-permute-start | bytes 688136 | tf_op jit(solution)/shard_map/weight_rows/ppermute | solution.py:31
  17.1 8.8 %collective-permute-start = (bf16[64,768]{1,0:T(8,128)(2,1)S(1)}, bf16[64,768]{1,0:T(8,128)(2,1)S(1)}, u32[]{:S(2)}, u32[]{:S(2)}) collective-permute-start(bf16[64,768]{1,0:T(8,128)(2,1)S(1)} %get-tuple-element.28), channel_id=1, source_target_pairs={{0,8},{8,16},{16,24},{24,32},{32,40},{40,48},{48,56},{56,64},{64,7... | collective-permute-start | bytes 294920 | tf_op jit(solution)/shard_map/rows_to_owners/ppermute | solution.py:117
  18.8 7.2 %collective-permute-start.1 = (bf16[64,768]{1,0:T(8,128)(2,1)S(1)}, bf16[64,768]{1,0:T(8,128)(2,1)S(1)}, u32[]{:S(2)}, u32[]{:S(2)}) collective-permute-start(bf16[64,768]{1,0:T(8,128)(2,1)S(1)} %get-tuple-element.29), channel_id=1, source_target_pairs={{0,248},{8,0},{16,8},{24,16},{32,24},{40,32},{48,40},{56,48},{64,5... | collective-permute-start | bytes 294920 | tf_op jit(solution)/shard_map/rows_to_owners/ppermute | solution.py:118
  29.7 42.0 %copy-start.7 = (s32[4]{0:T(128)S(1)}, s32[4]{0:T(128)}, u32[]{:S(2)}) copy-start(s32[4]{0:T(128)} %lengths.5) | copy-start | bytes 52
  29.7 5.5 %collective-permute-start.11 = (bf16[256,256]{1,0:T(8,128)(2,1)S(1)}, bf16[256,256]{1,0:T(8,128)(2,1)S(1)}, u32[]{:S(2)}, u32[]{:S(2)}) collective-permute-start(bf16[256,256]{1,0:T(8,128)(2,1)S(1)} %get-tuple-element.33), channel_id=1, source_target_pairs={{0,56},{8,0},{16,8},{24,16},{32,24},{40,32},{48,40},{56,48},{1,57}... | collective-permute-start | bytes 393224 | tf_op jit(solution)/shard_map/keys_and_values/ppermute | solution.py:31
  33.3 5.0 %collective-permute-start.5 = (bf16[256,256]{1,0:T(8,128)(2,1)S(1)}, bf16[256,256]{1,0:T(8,128)(2,1)S(1)}, u32[]{:S(2)}, u32[]{:S(2)}) collective-permute-start(bf16[256,256]{1,0:T(8,128)(2,1)S(1)} %get-tuple-element.33), channel_id=1, source_target_pairs={{0,8},{8,16},{16,24},{24,32},{32,40},{40,48},{48,56},{56,0},{1,9},... | collective-permute-start | bytes 393224 | tf_op jit(solution)/shard_map/keys_and_values/ppermute | solution.py:31
  35.2 5.0 %collective-permute-start.12 = (bf16[256,256]{1,0:T(8,128)(2,1)S(1)}, bf16[256,256]{1,0:T(8,128)(2,1)S(1)}, u32[]{:S(2)}, u32[]{:S(2)}) collective-permute-start(bf16[256,256]{1,0:T(8,128)(2,1)S(1)} %collective-permute-done.11), channel_id=1, source_target_pairs={{0,56},{8,0},{16,8},{24,16},{32,24},{40,32},{48,40},{56,48},{1,57}... | collective-permute-start | bytes 393224 | tf_op jit(solution)/shard_map/keys_and_values/ppermute | solution.py:31
  38.3 5.1 %collective-permute-start.6 = (bf16[256,256]{1,0:T(8,128)(2,1)S(1)}, bf16[256,256]{1,0:T(8,128)(2,1)S(1)}, u32[]{:S(2)}, u32[]{:S(2)}) collective-permute-start(bf16[256,256]{1,0:T(8,128)(2,1)S(1)} %collective-permute-done.5), channel_id=1, source_target_pairs={{0,8},{8,16},{16,24},{24,32},{32,40},{40,48},{48,56},{56,0},{1,9},... | collective-permute-start | bytes 393224 | tf_op jit(solution)/shard_map/keys_and_values/ppermute | solution.py:31
  40.3 8.3 %collective-permute-start.13 = (bf16[256,256]{1,0:T(8,128)(2,1)S(1)}, bf16[256,256]{1,0:T(8,128)(2,1)S(1)}, u32[]{:S(2)}, u32[]{:S(2)}) collective-permute-start(bf16[256,256]{1,0:T(8,128)(2,1)S(1)} %collective-permute-done.12), channel_id=1, source_target_pairs={{0,56},{8,0},{16,8},{24,16},{32,24},{40,32},{48,40},{56,48},{1,57}... | collective-permute-start | bytes 393224 | tf_op jit(solution)/shard_map/keys_and_values/ppermute | solution.py:31
  43.4 8.8 %collective-permute-start.7 = (bf16[256,256]{1,0:T(8,128)(2,1)S(1)}, bf16[256,256]{1,0:T(8,128)(2,1)S(1)}, u32[]{:S(2)}, u32[]{:S(2)}) collective-permute-start(bf16[256,256]{1,0:T(8,128)(2,1)S(1)} %collective-permute-done.6), channel_id=1, source_target_pairs={{0,8},{8,16},{16,24},{24,32},{32,40},{40,48},{48,56},{56,0},{1,9},... | collective-permute-start | bytes 393224 | tf_op jit(solution)/shard_map/keys_and_values/ppermute | solution.py:31
  48.5 16.4 %collective-permute-start.14 = (bf16[1280,256]{1,0:T(8,128)(2,1)S(1)}, bf16[1280,256]{1,0:T(8,128)(2,1)S(1)}, u32[]{:S(2)}, u32[]{:S(2)}) collective-permute-start(bf16[1280,256]{1,0:T(8,128)(2,1)S(1)} %constant_dynamic-update-slice_fusion.3.refs_1_), channel_id=1, source_target_pairs={{0,192},{64,0},{128,64},{192,128},{1,193},{65,1},{129,65},{193,129... | collective-permute-start | bytes 1966088 | tf_op jit(solution)/shard_map/keys_and_values/ppermute | solution.py:31
  52.3 9.8 %collective-permute-start.8 = (bf16[256,256]{1,0:T(8,128)(2,1)S(1)}, bf16[256,256]{1,0:T(8,128)(2,1)S(1)}, u32[]{:S(2)}, u32[]{:S(2)}) collective-permute-start(bf16[256,256]{1,0:T(8,128)(2,1)S(1)} %collective-permute-done.7), channel_id=1, source_target_pairs={{0,8},{8,16},{16,24},{24,32},{32,40},{40,48},{48,56},{56,0},{1,9},... | collective-permute-start | bytes 393224 | tf_op jit(solution)/shard_map/keys_and_values/ppermute | solution.py:31
  62.2 8.6 %collective-permute-start.9 = (bf16[768,256]{1,0:T(8,128)(2,1)S(1)}, bf16[768,256]{1,0:T(8,128)(2,1)S(1)}, u32[]{:S(2)}, u32[]{:S(2)}) collective-permute-start(bf16[768,256]{1,0:T(8,128)(2,1)S(1)} %constant_dynamic-update-slice_fusion.refs_0_), channel_id=1, source_target_pairs={{0,64},{64,128},{128,192},{192,0},{1,65},{65,129},{129,193},{193,1... | collective-permute-start | bytes 1179656 | tf_op jit(solution)/shard_map/keys_and_values/ppermute | solution.py:31
  64.7 15.2 %collective-permute-start.16 = (bf16[1280,256]{1,0:T(8,128)(2,1)S(1)}, bf16[1280,256]{1,0:T(8,128)(2,1)S(1)}, u32[]{:S(2)}, u32[]{:S(2)}) collective-permute-start(bf16[1280,256]{1,0:T(8,128)(2,1)S(1)} %constant_dynamic-update-slice_fusion.3.refs_1_), channel_id=1, source_target_pairs={{0,64},{64,128},{128,192},{192,0},{1,65},{65,129},{129,193},{193,1... | collective-permute-start | bytes 1966088 | tf_op jit(solution)/shard_map/keys_and_values/ppermute | solution.py:31
  65.0 23.3 %collective-permute-start.15 = (bf16[1280,256]{1,0:T(8,128)(2,1)S(1)}, bf16[1280,256]{1,0:T(8,128)(2,1)S(1)}, u32[]{:S(2)}, u32[]{:S(2)}) collective-permute-start(bf16[1280,256]{1,0:T(8,128)(2,1)S(1)} %collective-permute-done.14), channel_id=1, source_target_pairs={{0,192},{64,0},{128,64},{192,128},{1,193},{65,1},{129,65},{193,129... | collective-permute-start | bytes 1966088 | tf_op jit(solution)/shard_map/keys_and_values/ppermute | solution.py:31
  70.7 17.6 %collective-permute-start.10 = (bf16[768,256]{1,0:T(8,128)(2,1)S(1)}, bf16[768,256]{1,0:T(8,128)(2,1)S(1)}, u32[]{:S(2)}, u32[]{:S(2)}) collective-permute-start(bf16[768,256]{1,0:T(8,128)(2,1)S(1)} %collective-permute-done.9.refs_0_), channel_id=1, source_target_pairs={{0,64},{64,128},{128,192},{192,0},{1,65},{65,129},{129,193},{193,1... | collective-permute-start | bytes 1179656 | tf_op jit(solution)/shard_map/keys_and_values/ppermute | solution.py:31
  89.2 39.3 %copy-start.5 = (f32[4096]{0:T(1024)S(1)}, f32[4096]{0:T(1024)}, u32[]{:S(2)}) copy-start(f32[4096]{0:T(1024)} %param.12) | copy-start | bytes 49156
  89.2 15.8 %collective-permute-start.20 = (bf16[256,512]{1,0:T(8,128)(2,1)S(1)}, bf16[256,512]{1,0:T(8,128)(2,1)S(1)}, u32[]{:S(2)}, u32[]{:S(2)}) collective-permute-start(bf16[256,512]{1,0:T(8,128)(2,1)S(1)} %attention.5), channel_id=1, source_target_pairs={{0,64},{2,66},{4,68},{6,70},{64,0},{66,2},{68,4},{70,6},{1,65},{3,... | collective-permute-start | bytes 786440 | tf_op jit(solution)/shard_map/features_of_the_pair/ppermute | solution.py:42
  90.3 14.6 %collective-permute-start.21 = (bf16[256,512]{1,0:T(8,128)(2,1)S(1)}, bf16[256,512]{1,0:T(8,128)(2,1)S(1)}, u32[]{:S(2)}, u32[]{:S(2)}) collective-permute-start(bf16[256,512]{1,0:T(8,128)(2,1)S(1)} %attention.5), channel_id=1, source_target_pairs={{0,66},{2,68},{4,70},{6,64},{64,2},{66,4},{68,6},{70,0},{1,67},{3,... | collective-permute-start | bytes 786440 | tf_op jit(solution)/shard_map/features_of_the_pair/ppermute | solution.py:42
  91.7 13.3 %collective-permute-start.22 = (bf16[256,512]{1,0:T(8,128)(2,1)S(1)}, bf16[256,512]{1,0:T(8,128)(2,1)S(1)}, u32[]{:S(2)}, u32[]{:S(2)}) collective-permute-start(bf16[256,512]{1,0:T(8,128)(2,1)S(1)} %attention.5), channel_id=1, source_target_pairs={{0,70},{2,64},{4,66},{6,68},{64,6},{66,0},{68,2},{70,4},{1,71},{3,... | collective-permute-start | bytes 786440 | tf_op jit(solution)/shard_map/features_of_the_pair/ppermute | solution.py:42
  93.9 11.1 %collective-permute-start.23 = (bf16[256,512]{1,0:T(8,128)(2,1)S(1)}, bf16[256,512]{1,0:T(8,128)(2,1)S(1)}, u32[]{:S(2)}, u32[]{:S(2)}) collective-permute-start(bf16[256,512]{1,0:T(8,128)(2,1)S(1)} %attention.5), channel_id=1, source_target_pairs={{0,68},{2,70},{4,64},{6,66},{64,4},{66,6},{68,0},{70,2},{1,69},{3,... | collective-permute-start | bytes 786440 | tf_op jit(solution)/shard_map/features_of_the_pair/ppermute | solution.py:42
  105.1 23.4 %collective-permute-start.24 = (bf16[1024,512]{1,0:T(8,128)(2,1)S(1)}, bf16[1024,512]{1,0:T(8,128)(2,1)S(1)}, u32[]{:S(2)}, u32[]{:S(2)}) collective-permute-start(bf16[1024,512]{1,0:T(8,128)(2,1)S(1)} %constant_dynamic-update-slice_fusion.8.mine), channel_id=1, source_target_pairs={{0,1},{1,0},{2,3},{3,2},{4,5},{5,4},{6,7},{7,6},{8,9},{9,8},{10,11... | collective-permute-start | bytes 3145736 | tf_op jit(solution)/shard_map/features_of_the_pair/ppermute | solution.py:31
  125.3 12.5 %collective-permute-start.17 = (bf16[256,512]{1,0:T(8,128)(2,1)S(1)}, bf16[256,512]{1,0:T(8,128)(2,1)S(1)}, u32[]{:S(2)}, u32[]{:S(2)}) collective-permute-start(bf16[256,512]{1,0:T(8,128)(2,1)S(1)} %attention.5), channel_id=1, source_target_pairs={{0,2},{2,4},{4,6},{6,0},{1,3},{3,5},{5,7},{7,1},{8,10},{10,12},{12... | collective-permute-start | bytes 786440 | tf_op jit(solution)/shard_map/features_of_the_pair/ppermute | solution.py:31
  126.1 11.7 %collective-permute-start.18 = (bf16[256,512]{1,0:T(8,128)(2,1)S(1)}, bf16[256,512]{1,0:T(8,128)(2,1)S(1)}, u32[]{:S(2)}, u32[]{:S(2)}) collective-permute-start(bf16[256,512]{1,0:T(8,128)(2,1)S(1)} %attention.5), channel_id=1, source_target_pairs={{0,6},{2,0},{4,2},{6,4},{1,7},{3,1},{5,3},{7,5},{8,14},{10,8},{12,... | collective-permute-start | bytes 786440 | tf_op jit(solution)/shard_map/features_of_the_pair/ppermute | solution.py:31
  127.9 12.1 %collective-permute-start.19 = (bf16[256,512]{1,0:T(8,128)(2,1)S(1)}, bf16[256,512]{1,0:T(8,128)(2,1)S(1)}, u32[]{:S(2)}, u32[]{:S(2)}) collective-permute-start(bf16[256,512]{1,0:T(8,128)(2,1)S(1)} %attention.5), channel_id=1, source_target_pairs={{0,4},{2,6},{4,0},{6,2},{1,5},{3,7},{5,1},{7,3},{8,12},{10,14},{12... | collective-permute-start | bytes 786440 | tf_op jit(solution)/shard_map/features_of_the_pair/ppermute | solution.py:31
  128.5 3.1 %copy-start = (bf16[4096,896]{1,0:T(8,128)(2,1)S(1)}, bf16[4096,896]{1,0:T(8,128)(2,1)}, u32[]{:S(2)}) copy-start(bf16[4096,896]{1,0:T(8,128)(2,1)} %all-gather.2.cloned.1.call-done.weight) | copy-start | bytes 22020100
  131.6 12.0 %copy-start.1 = (bf16[4096,896]{1,0:T(8,128)(2,1)S(1)}, bf16[4096,896]{1,0:T(8,128)(2,1)}, u32[]{:S(2)}) copy-start(bf16[4096,896]{1,0:T(8,128)(2,1)} %all-gather.2.cloned.1.call-done.weight) | copy-start | bytes 22020100
  140.1 3.5 %collective-permute-start.25 = (bf16[1024,512]{1,0:T(8,128)(2,1)S(1)}, bf16[1024,512]{1,0:T(8,128)(2,1)S(1)}, u32[]{:S(2)}, u32[]{:S(2)}) collective-permute-start(bf16[1024,512]{1,0:T(8,128)(2,1)S(1)} %constant_dynamic-update-slice_fusion.12.mine), channel_id=1, source_target_pairs={{0,1},{1,0},{2,3},{3,2},{4,5},{5,4},{6,7},{7,6},{8,9},{9,8},{10,11... | collective-permute-start | bytes 3145736 | tf_op jit(solution)/shard_map/features/ppermute | solution.py:31
  141.3 12.1 %collective-permute-start.26 = (bf16[256,896]{1,0:T(8,128)(2,1)S(1)}, bf16[256,896]{1,0:T(8,128)(2,1)S(1)}, u32[]{:S(2)}, u32[]{:S(2)}) collective-permute-start(bf16[256,896]{1,0:T(8,128)(2,1)S(1)} %features_of_the_pair.1), channel_id=1, source_target_pairs={{0,64},{64,0},{1,65},{65,1},{2,66},{66,2},{3,67},{67,3},{4,68},{68... | collective-permute-start | bytes 1376264 | tf_op jit(solution)/shard_map/features/ppermute | solution.py:31
  (4 other events, 3.4 us)
Sparse Core Ops, SparseCore 0:
  29.8 92.5 all-gather.1
where the time goes:
time: 162 us; the launch traced here: 161 us
  starting transfers between devices  63.2 us (39%)
  waiting for transfers between devices  57.3 us (35%)
  Pallas kernels  18.2 us (11%)
  between operations  13.7 us (8%)
  local copies, waits for them, and re-layouts  6.76 us (4%)
  other arithmetic  2.1 us (1%)
    ppermute x21, starting transfers between devices, shift(): lax.ppermute(block, axis, [(i, (i + distance) % count) for i in range(cou...  50.8 us
    ppermute x21, waiting for transfers between devices, shift(): lax.ppermute(block, axis, [(i, (i + distance) % count) for i in range(cou...  45.2 us
    pallas_call x2, Pallas kernels, gate(): pl.pallas_call(gate_kernel, out_shape=bf16(TOK, columns), in_specs=[VMEM]...  12.3 us
    ppermute x4, waiting for transfers between devices, shift_both(): lax.ppermute(block, ('yb', 'x'), [(b * NX + i, to(b, i)) for b, i in pairs])  9.38 us
    unnamed x28, local copies, waits for them, and re-layouts  6.7 us
    ppermute x4, starting transfers between devices, shift_both(): lax.ppermute(block, ('yb', 'x'), [(b * NX + i, to(b, i)) for b, i in pairs])  6.39 us
    ppermute x1, starting transfers between devices, align(): lax.ppermute(down, ROWS, [(i, (i - 1) % count) for i in range(count)])  4.43 us
  transfers between devices with their start and end apart: 28, of which 15 were waited for; matrix products, arithmetic and copies ran while one was open for 0% of the time, Pallas kernels for 10%

commit v1 on v0

--- a/solution.py
+++ b/solution.py
@@ -15,13 +15,15 @@
 TOKENS = 8192
 NY, NZ, NX, NC = 4, 8, 4, 2
 HEADS_HERE = 4
-HERE = 4
-NEAR = 3
+HERE = 2
+FAR = 5
+PARTS = 4
 NORM_EPS = 1e-05
 MASKED = -1e30
 LOG2E = 1.4426950408889634
 EXP2_SCALE = HD ** (-0.5) * LOG2E
 VMEM = pl.BlockSpec(memory_space=pltpu.VMEM)
+HBM = pl.BlockSpec(memory_space=pltpu.HBM)
 SMEM = pl.BlockSpec(memory_space=pltpu.SMEM)
 ROWS, COLUMNS, TALL = ("yp", "yb", "z"), ("x", "c"), ("yp", "yb")
 
@@ -42,13 +44,11 @@
     return lax.ppermute(block, ("yb", "x"), [(b * NX + i, to(b, i)) for b, i in pairs])
 
 
-def z_ring(block):
-    up, down = [block], [block]
-    for _ in range(3):
-        up.append(shift(up[-1], "z", 1))
-        down.append(shift(down[-1], "z", -1))
-    near = jnp.concatenate([shift(up[3], "z", 1), up[3], up[2]], axis=0)
-    return near, jnp.concatenate([up[1], block, *down[1:]], axis=0)
+def z_blocks(block):
+    up1, down1, up2, down2 = (shift(block, "z", d) for d in (1, -1, 2, -2))
+    far = jnp.concatenate([up2, up1, block, down1, down2], axis=0)
+    up2, down2, far = lax.optimization_barrier((up2, down2, far))
+    return far, jnp.concatenate([shift(down2, "z", -1), shift(up2, "z", 2), shift(up2, "z", 1)], axis=0)
 
 
 def bf16(*shape):
@@ -70,17 +70,26 @@
     return starts[mine] - mine * TOK, after - mine * TOK
 
 
-def cut_kernel(starts, q, k, v, up, down):
+def open_kernel(starts, q, k, v, weight, up, down, theirs, mine, last, sems):
     first, _ = extent(starts)
-    row = lax.broadcasted_iota(jnp.int32, (QUARTER, CAP), 0)
-    slot = lax.broadcasted_iota(jnp.int32, (QUARTER, CAP), 1)
-    last = (slot == row + TOK - first).astype(jnp.bfloat16)
-    at = 0
+    half, odd = weight.shape[1] // 2, lax.rem(here()[0], 2)
+    column = lambda side: weight.at[:, pl.ds(pl.multiple_of(side * half, HD), half)]
+    pairs = [(column(1 - odd), theirs), (column(odd), mine)]
+    at, ends = 0, []
     for ref in (q, k, v):
         wide = ref.shape[1]
-        up[:, at : at + wide] = jnp.dot(last, ref[...], preferred_element_type=jnp.float32).astype(jnp.bfloat16)
-        down[:, at : at + wide] = ref[:QUARTER]
+        pairs.append((ref.at[pl.ds(0, QUARTER)], down.at[:, pl.ds(at, wide)]))
+        pairs.append((ref.at[pl.ds(CAP - 3 * QUARTER, 3 * QUARTER)], last.at[:, pl.ds(at, wide)]))
         at += wide
+    copies = [pltpu.make_async_copy(a, b, sems.at[i]) for i, (a, b) in enumerate(pairs)]
+    for copy in copies:
+        copy.start()
+    for copy in copies:
+        copy.wait()
+    row = lax.broadcasted_iota(jnp.int32, (QUARTER, 3 * QUARTER), 0)
+    slot = lax.broadcasted_iota(jnp.int32, (QUARTER, 3 * QUARTER), 1) + CAP - 3 * QUARTER
+    picked = (slot == row + TOK - first).astype(jnp.bfloat16)
+    up[...] = jnp.dot(picked, last[...], preferred_element_type=jnp.float32).astype(jnp.bfloat16)
 
 
 def align_kernel(starts, q, k, v, low, high, q_out, kv_out):
@@ -101,15 +110,17 @@
         at += wide
 
 
-def cut(starts, q, k, v):
+def opening(starts, q, k, v, weight):
     wide = q.shape[1] + k.shape[1] + v.shape[1]
-    return pl.pallas_call(
-        cut_kernel,
-        out_shape=(bf16(QUARTER, wide),) * 2,
-        in_specs=[SMEM] + [VMEM] * 3,
-        out_specs=(VMEM,) * 2,
-        compiler_params=limit(16),
-    )(starts, q, k, v)
+    rows, half = weight.shape[0], weight.shape[1] // 2
+    return pl.pallas_call(
+        open_kernel,
+        out_shape=(bf16(QUARTER, wide),) * 2 + (bf16(rows, half),) * 2,
+        in_specs=[SMEM] + [HBM] * 4,
+        out_specs=(VMEM,) * 4,
+        scratch_shapes=[pltpu.VMEM((3 * QUARTER, wide), jnp.bfloat16), pltpu.SemaphoreType.DMA((8,))],
+        compiler_params=limit(60),
+    )(starts, q, k, v, weight)
 
 
 def align(starts, q, k, v, up, down):
@@ -121,7 +132,7 @@
         out_shape=(bf16(TOK, q.shape[1]), bf16(TOK, 2 * HD)),
         in_specs=[SMEM] + [VMEM] * 5,
         out_specs=(VMEM,) * 2,
-        compiler_params=limit(16),
+        compiler_params=limit(60),
     )(starts, q, k, v, low, high)
 
 
@@ -189,7 +200,7 @@
         stats[...] = old_stats[...]
         sums[...] = old_sums[...]
     else:
-        step(blocks[1], (HERE - NEAR) * TOK, mine, True, True)
+        step(blocks[0], HERE * TOK, mine, True, True)
     before = 0
     for ref in blocks:
 
@@ -233,7 +244,12 @@
     )(lengths, q, *blocks, *state)
 
 
-def gate_kernel(gain, mine, other, weight, out, rows):
+def gate_kernel(gain, mine, other, weight, out, rows, held, total, sems):
+    depth = FEATURES // PARTS
+    parts = [pl.ds(i * depth, depth) for i in range(PARTS)]
+    copies = [pltpu.make_async_copy(weight.at[p], held.at[p], sems.at[i]) for i, p in enumerate(parts)]
+    for copy in copies:
+        copy.start()
     y, _, x, c = here()
     squares = jnp.zeros((TOK, HD), jnp.float32)
     for side, pieces in enumerate((mine, other)):
@@ -249,14 +265,20 @@
                 place = lax.rem(head, NZ) * NY + slot
                 rows[:, pl.ds(pl.multiple_of(place * HD, HD), HD)] = scaled
     inv = lax.rsqrt(jnp.sum(squares, axis=1, keepdims=True) / FEATURES + NORM_EPS)
-
-    def columns(i, _):
-        at = pl.ds(pl.multiple_of(i * HD, HD), HD)
-        value = jnp.dot(rows[...], weight[:, at], preferred_element_type=jnp.float32) * inv
-        out[:, at] = (value / (1.0 + jnp.exp(-value))).astype(jnp.bfloat16)
-        return 0
-
-    lax.fori_loop(0, out.shape[1] // HD, columns, 0)
+    for i, copy in enumerate(copies):
+        copy.wait()
+        term = jnp.dot(
+            rows[:, i * depth : (i + 1) * depth],
+            held[i * depth : (i + 1) * depth],
+            preferred_element_type=jnp.float32,
+        )
+        if i == 0:
+            total[...] = term
+        elif i < PARTS - 1:
+            total[...] += term
+        else:
+            value = (total[...] + term) * inv
+            out[...] = (value / (1.0 + jnp.exp(-value))).astype(jnp.bfloat16)
 
 
 def gate(gain, mine, other, weight):
@@ -264,14 +286,19 @@
     return pl.pallas_call(
         gate_kernel,
         out_shape=bf16(TOK, columns),
-        in_specs=[VMEM] * 4,
+        in_specs=[VMEM] * 3 + [HBM],
         out_specs=VMEM,
-        scratch_shapes=[pltpu.VMEM((TOK, FEATURES), jnp.bfloat16)],
-        compiler_params=limit(24),
+        scratch_shapes=[
+            pltpu.VMEM((TOK, FEATURES), jnp.bfloat16),
+            pltpu.VMEM(weight.shape, weight.dtype),
+            pltpu.VMEM((TOK, columns), jnp.float32),
+            pltpu.SemaphoreType.DMA((PARTS,)),
+        ],
+        compiler_params=limit(28),
         cost_estimate=pl.CostEstimate(
             flops=2 * TOK * FEATURES * columns, bytes_accessed=2 * FEATURES * columns, transcendentals=TOK * columns
         ),
-    )(gain, mine, other, weight)
+    )(gain, mine, other, pltpu.with_memory_space_constraint(weight, pltpu.HBM))
 
 
 def join_kernel(home, back, out):
@@ -292,31 +319,26 @@
 
 
 def on_device(queries, keys, values, doc_lengths, shard_starts, norm_gain, ffn_weight):
-    half = ffn_weight.shape[1] // 2
-    odd = lax.axis_index("yb") == 1
-
     with jax.named_scope("rows_to_owners"):
-        up, down = cut(shard_starts, queries, keys, values)
-        odd, up, down = lax.optimization_barrier((odd, up, down))
+        up, down, theirs, mine = opening(shard_starts, queries, keys, values, ffn_weight)
         q, kv = align(shard_starts, queries, keys, values, up, down)
 
     with jax.named_scope("weight_rows"):
-        left, right = ffn_weight[:, :half], ffn_weight[:, half:]
-        theirs, mine = jnp.where(odd, left, right), jnp.where(odd, right, left)
         parts = [mine, shift(theirs, TALL, 1), shift(theirs, TALL, -1), shift(mine, TALL, 2)]
         *parts, kv = lax.optimization_barrier((*parts, kv))
         weight = lax.all_gather(jnp.concatenate(parts, axis=0), "z", axis=0, tiled=True)
 
     with jax.named_scope("keys_and_values"):
-        near, far = z_ring(kv)
-        near1, far3 = shift(near, TALL, 1), shift(far, TALL, -1)
-        far1 = shift(far, TALL, 1)
-        near2, far2 = shift(near1, TALL, 1), shift(far3, TALL, -1)
+        far, near = z_blocks(kv)
+        far1, far3 = shift(far, TALL, 1), shift(far, TALL, -1)
+        near1, far2 = shift(near, TALL, 1), shift(far3, TALL, -1)
+        state = attention(0, doc_lengths, q, [far, near], ())
+        near1, far1, *state = lax.optimization_barrier((near1, far1, *state))
+        near2 = shift(near1, TALL, 1)
 
     with jax.named_scope("attention"):
-        state = attention(0, doc_lengths, q, [near, far], ())
-        state = attention(1, doc_lengths, q, [near1, far1], state)
-        (attended,) = attention(2, doc_lengths, q, [near2, far2], state)
+        state = attention(1, doc_lengths, q, [far1, near1], state)
+        (attended,) = attention(2, doc_lengths, q, [far2, near2], state)
 
     gain = norm_gain.reshape(1, FEATURES)
     with jax.named_scope("features_of_the_pair"):

time: 162 us -> 148 us (0.914)
  starting transfers between devices: 63.2 us -> 39.9 us
  waiting for transfers between devices: 57.3 us -> 72.2 us
  local copies, waits for them, and re-layouts: 6.76 us -> 1.51 us
    ppermute x21, starting transfers between devices: 50.8 us -> 27.4 us  [shift(): lax.ppermute(block, axis, [(i, (i + distance) % count) for i in range(cou...]
    all_gather x1, waiting for transfers between devices: 0.01 us -> 13 us  [on_device(): lax.all_gather(jnp.concatenate(parts, axis=0), 'z', axis=0, tiled=True)]
    ppermute x4, waiting for transfers between devices: 9.38 us -> 16.6 us  [shift_both(): lax.ppermute(block, ('yb', 'x'), [(b * NX + i, to(b, i)) for b, i in pairs])]
    ppermute x21, waiting for transfers between devices: 45.2 us -> 39.6 us  [shift(): lax.ppermute(block, axis, [(i, (i + distance) % count) for i in range(cou...]
    unnamed x28 -> x24, local copies, waits for them, and re-layouts: 6.7 us -> 1.45 us
    pallas_call x2, Pallas kernels: 12.3 us -> 9.65 us  [gate(): pl.pallas_call(gate_kernel, out_shape=bf16(TOK, columns), in_specs=[VMEM]...]
    pallas_call x1, Pallas kernels: 0.77 us -> 2.76 us  [opening(): pl.pallas_call(open_kernel, out_shape=(bf16(QUARTER, wide),) * 2 + (bf16(...]
  transfers between devices with their start and end apart: 28 -> 28, of which waited for: 15 -> 13; matrix products, arithmetic and copies ran while one was open for 0% -> 0% of each run, Pallas kernels for 10% -> 10%
where the time goes in v1:
time: 148 us
  waiting for transfers between devices  72.2 us (49%)
  starting transfers between devices  39.9 us (27%)
  Pallas kernels  18.9 us (13%)
  between operations  13.7 us (9%)
  other arithmetic  1.97 us (1%)
  local copies, waits for them, and re-layouts  1.51 us (1%)
    ppermute x21, waiting for transfers between devices, shift(): lax.ppermute(block, axis, [(i, (i + distance) % count) for i in range(cou...  39.6 us
    ppermute x21, starting transfers between devices, shift(): lax.ppermute(block, axis, [(i, (i + distance) % count) for i in range(cou...  27.4 us
    ppermute x4, waiting for transfers between devices, shift_both(): lax.ppermute(block, ('yb', 'x'), [(b * NX + i, to(b, i)) for b, i in pairs])  16.6 us
    all_gather x1, waiting for transfers between devices, on_device(): lax.all_gather(jnp.concatenate(parts, axis=0), 'z', axis=0, tiled=True)  13 us
    pallas_call x2, Pallas kernels, gate(): pl.pallas_call(gate_kernel, out_shape=bf16(TOK, columns), in_specs=[VMEM]...  9.65 us
    ppermute x4, starting transfers between devices, shift_both(): lax.ppermute(block, ('yb', 'x'), [(b * NX + i, to(b, i)) for b, i in pairs])  6.37 us
    ppermute x1, starting transfers between devices, align(): lax.ppermute(down, ROWS, [(i, (i - 1) % count) for i in range(count)])  4.43 us
    pallas_call x3, Pallas kernels, attention(): pl.pallas_call(functools.partial(attention_kernel, back, len(blocks), pla...  3.05 us
  transfers between devices with their start and end apart: 28, of which 13 were waited for; matrix products, arithmetic and copies ran while one was open for 0% of the time, Pallas kernels for 10%

profile of v1, /device:TPU:1, one launch (start us, length us, event | category | flops | bytes accessed | tf_op | source)
XLA Modules:
  0.0 148.1 jit_solution(15243896690889034515)
XLA Ops:
  6.5 2.8 %rows_to_owners.2 = (bf16[64,768]{1,0:T(8,128)(2,1)}, bf16[64,768]{1,0:T(8,128)(2,1)}, bf16[128,896]{1,0:T(8,128)(2,1)}, bf16[128,896]{1,0:T(8,128)(2,1)}) custom-call(s32[32]{0:T(128)} %starts.3, bf16[384,512]{1,0:T(8,128)(2,1)} %q.3, bf16[384,128]{1,0:T(8,128)(2,1)} %k.3, bf16[384,128]{1,0:T(8,128)(2,1)} %v.3, bf16[128,1792]{1,0:T(8,128)(2,1)} %weight.1), custom_call_target="tpu_custom_call" | custom-call | tf_op jit(solution)/shard_map/rows_to_owners/pallas_call | solution.py:116
  9.3 2.2 %collective-permute-start.2 = (bf16[128,896]{1,0:T(8,128)(2,1)}, bf16[128,896]{1,0:T(8,128)(2,1)S(1)}, u32[]{:S(2)}, u32[]{:S(2)}) collective-permute-start(bf16[128,896]{1,0:T(8,128)(2,1)} %get-tuple-element.36), channel_id=1, source_target_pairs={{0,64},{64,128},{128,192},{192,0},{1,65},{65,129},{129,193},{193,1... | collective-permute-start | bytes 688136 | tf_op jit(solution)/shard_map/weight_rows/ppermute | solution.py:33
  11.5 1.5 %collective-permute-start.3 = (bf16[128,896]{1,0:T(8,128)(2,1)}, bf16[128,896]{1,0:T(8,128)(2,1)S(1)}, u32[]{:S(2)}, u32[]{:S(2)}) collective-permute-start(bf16[128,896]{1,0:T(8,128)(2,1)} %get-tuple-element.36), channel_id=1, source_target_pairs={{0,192},{64,0},{128,64},{192,128},{1,193},{65,1},{129,65},{193,129... | collective-permute-start | bytes 688136 | tf_op jit(solution)/shard_map/weight_rows/ppermute | solution.py:33
  13.0 1.6 %collective-permute-start.4 = (bf16[128,896]{1,0:T(8,128)(2,1)}, bf16[128,896]{1,0:T(8,128)(2,1)S(1)}, u32[]{:S(2)}, u32[]{:S(2)}) collective-permute-start(bf16[128,896]{1,0:T(8,128)(2,1)} %get-tuple-element.50), channel_id=1, source_target_pairs={{0,128},{64,192},{128,0},{192,64},{1,129},{65,193},{129,1},{193,65... | collective-permute-start | bytes 688136 | tf_op jit(solution)/shard_map/weight_rows/ppermute | solution.py:33
  14.6 1.6 %collective-permute-start = (bf16[64,768]{1,0:T(8,128)(2,1)}, bf16[64,768]{1,0:T(8,128)(2,1)S(1)}, u32[]{:S(2)}, u32[]{:S(2)}) collective-permute-start(bf16[64,768]{1,0:T(8,128)(2,1)} %get-tuple-element.32), channel_id=1, source_target_pairs={{0,8},{8,16},{16,24},{24,32},{32,40},{40,48},{48,56},{56,64},{64,7... | collective-permute-start | bytes 294920 | tf_op jit(solution)/shard_map/rows_to_owners/ppermute | solution.py:128
  16.2 4.4 %collective-permute-start.1 = (bf16[64,768]{1,0:T(8,128)(2,1)}, bf16[64,768]{1,0:T(8,128)(2,1)S(1)}, u32[]{:S(2)}, u32[]{:S(2)}) collective-permute-start(bf16[64,768]{1,0:T(8,128)(2,1)} %get-tuple-element.33), channel_id=1, source_target_pairs={{0,248},{8,0},{16,8},{24,16},{32,24},{40,32},{48,40},{56,48},{64,5... | collective-permute-start | bytes 294920 | tf_op jit(solution)/shard_map/rows_to_owners/ppermute | solution.py:129
  20.7 3.0 %collective-permute-done.low = bf16[64,768]{1,0:T(8,128)(2,1)S(1)} collective-permute-done((bf16[64,768]{1,0:T(8,128)(2,1)}, bf16[64,768]{1,0:T(8,128)(2,1)S(1)}, u32[]{:S(2)}, u32[]{:S(2)}) %collective-permute-start) | collective-permute-done | bytes 98336 | tf_op jit(solution)/shard_map/rows_to_owners/ppermute | solution.py:128
  24.9 2.4 %rows_to_owners.3 = (bf16[256,512]{1,0:T(8,128)(2,1)}, bf16[256,256]{1,0:T(8,128)(2,1)}) custom-call(s32[32]{0:T(128)} %starts.3, bf16[384,512]{1,0:T(8,128)(2,1)} %q.3, bf16[384,128]{1,0:T(8,128)(2,1)} %k.3, bf16[384,128]{1,0:T(8,128)(2,1)} %v.3, bf16[64,768]{1,0:T(8,128)(2,1)} %copy-done.4, bf16[64,768]{1,0:T(8,128)(2,1)} %copy-done.5), custom_call_target="tpu_custom_call" | custom-call | tf_op jit(solution)/shard_map/rows_to_owners/pallas_call | solution.py:130
  27.3 2.0 %pad_maximum_fusion = bf16[512,896]{1,0:T(8,128)(2,1)} fusion(bf16[128,896]{1,0:T(8,128)(2,1)S(1)} %collective-permute-done.4, bf16[128,896]{1,0:T(8,128)(2,1)S(1)} %collective-permute-done.3, bf16[128,896]{1,0:T(8,128)(2,1)S(1)} %collective-permute-done.2, bf16[128,896]{1,0:T(8,128)(2,1)} %get-tuple-element.50), kind=kLoop, calls=%fused_computation | loop fusion | flops 3670016 | bytes 1835008 | tf_op jit(solution)/shard_map/weight_rows/concatenate | solution.py:329
  29.5 3.0 %collective-permute-start.7 = (bf16[256,256]{1,0:T(8,128)(2,1)S(1)}, bf16[256,256]{1,0:T(8,128)(2,1)S(1)}, u32[]{:S(2)}, u32[]{:S(2)}) collective-permute-start(bf16[256,256]{1,0:T(8,128)(2,1)S(1)} %copy-done.3), channel_id=1, source_target_pairs={{0,8},{8,16},{16,24},{24,32},{32,40},{40,48},{48,56},{56,0},{1,9},... | collective-permute-start | bytes 393224 | tf_op jit(solution)/shard_map/keys_and_values/ppermute | solution.py:33
  32.4 2.0 %collective-permute-start.6 = (bf16[256,256]{1,0:T(8,128)(2,1)S(1)}, bf16[256,256]{1,0:T(8,128)(2,1)S(1)}, u32[]{:S(2)}, u32[]{:S(2)}) collective-permute-start(bf16[256,256]{1,0:T(8,128)(2,1)S(1)} %copy-done.3), channel_id=1, source_target_pairs={{0,48},{8,56},{16,0},{24,8},{32,16},{40,24},{48,32},{56,40},{1,49}... | collective-permute-start | bytes 393224 | tf_op jit(solution)/shard_map/keys_and_values/ppermute | solution.py:33
  34.5 1.4 collective-permute-done.5
  35.9 3.4 %collective-permute-done.7 = bf16[256,256]{1,0:T(8,128)(2,1)S(1)} collective-permute-done((bf16[256,256]{1,0:T(8,128)(2,1)S(1)}, bf16[256,256]{1,0:T(8,128)(2,1)S(1)}, u32[]{:S(2)}, u32[]{:S(2)}) %collective-permute-start.7) | collective-permute-done | bytes 131104 | tf_op jit(solution)/shard_map/keys_and_values/ppermute | solution.py:33
  39.4 1.8 %collective-permute-done.6 = bf16[256,256]{1,0:T(8,128)(2,1)S(1)} collective-permute-done((bf16[256,256]{1,0:T(8,128)(2,1)S(1)}, bf16[256,256]{1,0:T(8,128)(2,1)S(1)}, u32[]{:S(2)}, u32[]{:S(2)}) %collective-permute-start.6) | collective-permute-done | bytes 131104 | tf_op jit(solution)/shard_map/keys_and_values/ppermute | solution.py:33
  42.5 2.2 %collective-permute-start.11 = (bf16[256,256]{1,0:T(8,128)(2,1)S(1)}, bf16[256,256]{1,0:T(8,128)(2,1)S(1)}, u32[]{:S(2)}, u32[]{:S(2)}) collective-permute-start(bf16[256,256]{1,0:T(8,128)(2,1)S(1)} %collective-permute-done.6), channel_id=1, source_target_pairs={{0,56},{8,0},{16,8},{24,16},{32,24},{40,32},{48,40},{56,48},{1,57}... | collective-permute-start | bytes 393224 | tf_op jit(solution)/shard_map/keys_and_values/ppermute | solution.py:33
  46.4 3.4 %collective-permute-done.11 = bf16[256,256]{1,0:T(8,128)(2,1)S(1)} collective-permute-done((bf16[256,256]{1,0:T(8,128)(2,1)S(1)}, bf16[256,256]{1,0:T(8,128)(2,1)S(1)}, u32[]{:S(2)}, u32[]{:S(2)}) %collective-permute-start.11) | collective-permute-done | bytes 131104 | tf_op jit(solution)/shard_map/keys_and_values/ppermute | solution.py:33
  49.8 5.7 %collective-permute-done.12 = bf16[256,256]{1,0:T(8,128)(2,1)S(1)} collective-permute-done((bf16[256,256]{1,0:T(8,128)(2,1)S(1)}, bf16[256,256]{1,0:T(8,128)(2,1)S(1)}, u32[]{:S(2)}, u32[]{:S(2)}) %collective-permute-start.12) | collective-permute-done | bytes 131104 | tf_op jit(solution)/shard_map/keys_and_values/ppermute | solution.py:33
  55.5 4.5 %collective-permute-done.13 = bf16[256,256]{1,0:T(8,128)(2,1)S(1)} collective-permute-done((bf16[256,256]{1,0:T(8,128)(2,1)S(1)}, bf16[256,256]{1,0:T(8,128)(2,1)S(1)}, u32[]{:S(2)}, u32[]{:S(2)}) %collective-permute-start.13) | collective-permute-done | bytes 131104 | tf_op jit(solution)/shard_map/keys_and_values/ppermute | solution.py:33
  60.3 2.6 %collective-permute-start.10 = (bf16[1280,256]{1,0:T(8,128)(2,1)S(1)}, bf16[1280,256]{1,0:T(8,128)(2,1)S(1)}, u32[]{:S(2)}, u32[]{:S(2)}) collective-permute-start(bf16[1280,256]{1,0:T(8,128)(2,1)S(1)} %collective-permute-done.9), channel_id=1, source_target_pairs={{0,192},{64,0},{128,64},{192,128},{1,193},{65,1},{129,65},{193,129... | collective-permute-start | bytes 1966088 | tf_op jit(solution)/shard_map/keys_and_values/ppermute | solution.py:33
  62.9 1.4 keys_and_values.1
  64.3 4.1 %collective-permute-done.14.refs_1_ = bf16[768,256]{1,0:T(8,128)(2,1)S(1)} collective-permute-done((bf16[768,256]{1,0:T(8,128)(2,1)S(1)}, bf16[768,256]{1,0:T(8,128)(2,1)S(1)}, u32[]{:S(2)}, u32[]{:S(2)}) %collective-permute-start.14) | collective-permute-done | bytes 393248 | tf_op jit(solution)/shard_map/keys_and_values/ppermute | solution.py:33
  69.2 9.2 %collective-permute-done.16.refs_1_ = bf16[768,256]{1,0:T(8,128)(2,1)S(1)} collective-permute-done((bf16[768,256]{1,0:T(8,128)(2,1)S(1)}, bf16[768,256]{1,0:T(8,128)(2,1)S(1)}, u32[]{:S(2)}, u32[]{:S(2)}) %collective-permute-start.16) | collective-permute-done | bytes 393248 | tf_op jit(solution)/shard_map/keys_and_values/ppermute | solution.py:33
  79.4 2.4 %collective-permute-start.21 = (bf16[256,512]{1,0:T(8,128)(2,1)S(1)}, bf16[256,512]{1,0:T(8,128)(2,1)S(1)}, u32[]{:S(2)}, u32[]{:S(2)}) collective-permute-start(bf16[256,512]{1,0:T(8,128)(2,1)S(1)} %attention.3), channel_id=1, source_target_pairs={{0,66},{2,68},{4,70},{6,64},{64,2},{66,4},{68,6},{70,0},{1,67},{3,... | collective-permute-start | bytes 786440 | tf_op jit(solution)/shard_map/features_of_the_pair/ppermute | solution.py:44
  83.1 2.6 %collective-permute-start.23 = (bf16[256,512]{1,0:T(8,128)(2,1)S(1)}, bf16[256,512]{1,0:T(8,128)(2,1)S(1)}, u32[]{:S(2)}, u32[]{:S(2)}) collective-permute-start(bf16[256,512]{1,0:T(8,128)(2,1)S(1)} %attention.3), channel_id=1, source_target_pairs={{0,68},{2,70},{4,64},{6,66},{64,4},{66,6},{68,0},{70,2},{1,69},{3,... | collective-permute-start | bytes 786440 | tf_op jit(solution)/shard_map/features_of_the_pair/ppermute | solution.py:44
  85.7 16.6 %collective-permute-done.20 = bf16[256,512]{1,0:T(8,128)(2,1)S(1)} collective-permute-done((bf16[256,512]{1,0:T(8,128)(2,1)S(1)}, bf16[256,512]{1,0:T(8,128)(2,1)S(1)}, u32[]{:S(2)}, u32[]{:S(2)}) %collective-permute-start.20) | collective-permute-done | bytes 262176 | tf_op jit(solution)/shard_map/features_of_the_pair/ppermute | solution.py:44
  102.5 2.7 %collective-permute-start.24 = (bf16[1024,512]{1,0:T(8,128)(2,1)S(1)}, bf16[1024,512]{1,0:T(8,128)(2,1)S(1)}, u32[]{:S(2)}, u32[]{:S(2)}) collective-permute-start(bf16[1024,512]{1,0:T(8,128)(2,1)S(1)} %constant_dynamic-update-slice_fusion.8.mine), channel_id=1, source_target_pairs={{0,1},{1,0},{2,3},{3,2},{4,5},{5,4},{6,7},{7,6},{8,9},{9,8},{10,11... | collective-permute-start | bytes 3145736 | tf_op jit(solution)/shard_map/features_of_the_pair/ppermute | solution.py:33
  106.4 1.5 collective-permute-start.18
  107.9 1.5 %collective-permute-start.19 = (bf16[256,512]{1,0:T(8,128)(2,1)S(1)}, bf16[256,512]{1,0:T(8,128)(2,1)S(1)}, u32[]{:S(2)}, u32[]{:S(2)}) collective-permute-start(bf16[256,512]{1,0:T(8,128)(2,1)S(1)} %attention.3), channel_id=1, source_target_pairs={{0,4},{2,6},{4,0},{6,2},{1,5},{3,7},{5,1},{7,3},{8,12},{10,14},{12... | collective-permute-start | bytes 786440 | tf_op jit(solution)/shard_map/features_of_the_pair/ppermute | solution.py:33
  109.4 13.0 %all-gather.2.cloned.1.call-done.weight = bf16[4096,896]{1,0:T(8,128)(2,1)} async-done(((bf16[512,896]{1,0:T(8,128)(2,1)}), bf16[4096,896]{1,0:T(8,128)(2,1)}) %all-gather.2.cloned.1.call-update) | async-done | bytes 7340048 | tf_op jit(solution)/shard_map/weight_rows/all_gather | solution.py:329
  122.4 4.8 %features_of_the_pair.1 = bf16[256,896]{1,0:T(8,128)(2,1)S(1)} custom-call(f32[1,4096]{1,0:T(1,128)S(1)} %bitcast.1, bf16[1024,512]{1,0:T(8,128)(2,1)S(1)} %constant_dynamic-update-slice_fusion.8.mine, bf16[1024,512]{1,0:T(8,128)(2,1)S(1)} %collective-permute-done.24.other, bf16[4096,896]{1,0:T(8,128)(2,1)} %all-gather.2.cloned.1.call-done.weight), custom_call_target="tpu_custom_call" | custom-call | flops 1879048192 | bytes 7340032 | tf_op jit(solution)/shard_map/features_of_the_pair/pallas_call | solution.py:286
  130.4 4.8 %features.2.home = bf16[256,896]{1,0:T(8,128)(2,1)S(1)} custom-call(f32[1,4096]{1,0:T(1,128)S(1)} %bitcast.2, bf16[1024,512]{1,0:T(8,128)(2,1)S(1)} %constant_dynamic-update-slice_fusion.12.mine, bf16[1024,512]{1,0:T(8,128)(2,1)S(1)} %collective-permute-done.25.other, bf16[4096,896]{1,0:T(8,128)(2,1)} %all-gather.2.cloned.1.call-done.weight), custom_call_target="tpu_custom_call" | custom-call | flops 1879048192 | bytes 7340032 | tf_op jit(solution)/shard_map/features/pallas_call | solution.py:286
  135.3 5.0 %collective-permute-done.26.back = bf16[256,896]{1,0:T(8,128)(2,1)S(1)} collective-permute-done((bf16[256,896]{1,0:T(8,128)(2,1)S(1)}, bf16[256,896]{1,0:T(8,128)(2,1)S(1)}, u32[]{:S(2)}, u32[]{:S(2)}) %collective-permute-start.26) | collective-permute-done | bytes 458784 | tf_op jit(solution)/shard_map/features/ppermute | solution.py:33
  (62 shorter events, 13.2 us)
Async XLA Ops:
  6.5 115.9 %all-gather.2.cloned.1.call-start = ((), (), s32[]{:S(2)}) async-start(), calls=%async_computation | async-start | bytes 8257536 | tf_op jit(solution)/shard_map/weight_rows/all_gather | solution.py:329
  9.3 18.0 %collective-permute-start.2 = (bf16[128,896]{1,0:T(8,128)(2,1)}, bf16[128,896]{1,0:T(8,128)(2,1)S(1)}, u32[]{:S(2)}, u32[]{:S(2)}) collective-permute-start(bf16[128,896]{1,0:T(8,128)(2,1)} %get-tuple-element.36), channel_id=1, source_target_pairs={{0,64},{64,128},{128,192},{192,0},{1,65},{65,129},{129,193},{193,1... | collective-permute-start | bytes 688136 | tf_op jit(solution)/shard_map/weight_rows/ppermute | solution.py:33
  11.5 15.8 %collective-permute-start.3 = (bf16[128,896]{1,0:T(8,128)(2,1)}, bf16[128,896]{1,0:T(8,128)(2,1)S(1)}, u32[]{:S(2)}, u32[]{:S(2)}) collective-permute-start(bf16[128,896]{1,0:T(8,128)(2,1)} %get-tuple-element.36), channel_id=1, source_target_pairs={{0,192},{64,0},{128,64},{192,128},{1,193},{65,1},{129,65},{193,129... | collective-permute-start | bytes 688136 | tf_op jit(solution)/shard_map/weight_rows/ppermute | solution.py:33
  13.0 14.3 %collective-permute-start.4 = (bf16[128,896]{1,0:T(8,128)(2,1)}, bf16[128,896]{1,0:T(8,128)(2,1)S(1)}, u32[]{:S(2)}, u32[]{:S(2)}) collective-permute-start(bf16[128,896]{1,0:T(8,128)(2,1)} %get-tuple-element.50), channel_id=1, source_target_pairs={{0,128},{64,192},{128,0},{192,64},{1,129},{65,193},{129,1},{193,65... | collective-permute-start | bytes 688136 | tf_op jit(solution)/shard_map/weight_rows/ppermute | solution.py:33
  14.6 9.0 %collective-permute-start = (bf16[64,768]{1,0:T(8,128)(2,1)}, bf16[64,768]{1,0:T(8,128)(2,1)S(1)}, u32[]{:S(2)}, u32[]{:S(2)}) collective-permute-start(bf16[64,768]{1,0:T(8,128)(2,1)} %get-tuple-element.32), channel_id=1, source_target_pairs={{0,8},{8,16},{16,24},{24,32},{32,40},{40,48},{48,56},{56,64},{64,7... | collective-permute-start | bytes 294920 | tf_op jit(solution)/shard_map/rows_to_owners/ppermute | solution.py:128
  16.2 7.4 %collective-permute-start.1 = (bf16[64,768]{1,0:T(8,128)(2,1)}, bf16[64,768]{1,0:T(8,128)(2,1)S(1)}, u32[]{:S(2)}, u32[]{:S(2)}) collective-permute-start(bf16[64,768]{1,0:T(8,128)(2,1)} %get-tuple-element.33), channel_id=1, source_target_pairs={{0,248},{8,0},{16,8},{24,16},{32,24},{40,32},{48,40},{56,48},{64,5... | collective-permute-start | bytes 294920 | tf_op jit(solution)/shard_map/rows_to_owners/ppermute | solution.py:129
  27.3 2.0 %copy-start.3 = (bf16[256,256]{1,0:T(8,128)(2,1)S(1)}, bf16[256,256]{1,0:T(8,128)(2,1)}, u32[]{:S(2)}) copy-start(bf16[256,256]{1,0:T(8,128)(2,1)} %get-tuple-element.38) | copy-start | bytes 393220
  29.3 33.6 %copy-start.1 = (bf16[256,512]{1,0:T(8,128)(2,1)S(1)}, bf16[256,512]{1,0:T(8,128)(2,1)}, u32[]{:S(2)}) copy-start(bf16[256,512]{1,0:T(8,128)(2,1)} %get-tuple-element.34.q_ref) | copy-start | bytes 786436
  29.3 33.6 %copy-start.2 = (s32[4]{0:T(128)S(1)}, s32[4]{0:T(128)}, u32[]{:S(2)}) copy-start(s32[4]{0:T(128)} %lengths.5) | copy-start | bytes 52
  29.3 6.6 %collective-permute-start.5 = (bf16[256,256]{1,0:T(8,128)(2,1)S(1)}, bf16[256,256]{1,0:T(8,128)(2,1)S(1)}, u32[]{:S(2)}, u32[]{:S(2)}) collective-permute-start(bf16[256,256]{1,0:T(8,128)(2,1)S(1)} %copy-done.3), channel_id=1, source_target_pairs={{0,16},{8,24},{16,32},{24,40},{32,48},{40,56},{48,0},{56,8},{1,17}... | collective-permute-start | bytes 393224 | tf_op jit(solution)/shard_map/keys_and_values/ppermute | solution.py:33
  29.5 9.9 %collective-permute-start.7 = (bf16[256,256]{1,0:T(8,128)(2,1)S(1)}, bf16[256,256]{1,0:T(8,128)(2,1)S(1)}, u32[]{:S(2)}, u32[]{:S(2)}) collective-permute-start(bf16[256,256]{1,0:T(8,128)(2,1)S(1)} %copy-done.3), channel_id=1, source_target_pairs={{0,8},{8,16},{16,24},{24,32},{32,40},{40,48},{48,56},{56,0},{1,9},... | collective-permute-start | bytes 393224 | tf_op jit(solution)/shard_map/keys_and_values/ppermute | solution.py:33
  32.4 7.0 %collective-permute-start.8 = (bf16[256,256]{1,0:T(8,128)(2,1)S(1)}, bf16[256,256]{1,0:T(8,128)(2,1)S(1)}, u32[]{:S(2)}, u32[]{:S(2)}) collective-permute-start(bf16[256,256]{1,0:T(8,128)(2,1)S(1)} %copy-done.3), channel_id=1, source_target_pairs={{0,56},{8,0},{16,8},{24,16},{32,24},{40,32},{48,40},{56,48},{1,57}... | collective-permute-start | bytes 393224 | tf_op jit(solution)/shard_map/keys_and_values/ppermute | solution.py:33
  32.4 8.8 %collective-permute-start.6 = (bf16[256,256]{1,0:T(8,128)(2,1)S(1)}, bf16[256,256]{1,0:T(8,128)(2,1)S(1)}, u32[]{:S(2)}, u32[]{:S(2)}) collective-permute-start(bf16[256,256]{1,0:T(8,128)(2,1)S(1)} %copy-done.3), channel_id=1, source_target_pairs={{0,48},{8,56},{16,0},{24,8},{32,16},{40,24},{48,32},{56,40},{1,49}... | collective-permute-start | bytes 393224 | tf_op jit(solution)/shard_map/keys_and_values/ppermute | solution.py:33
  41.2 19.0 %collective-permute-start.9 = (bf16[1280,256]{1,0:T(8,128)(2,1)S(1)}, bf16[1280,256]{1,0:T(8,128)(2,1)S(1)}, u32[]{:S(2)}, u32[]{:S(2)}) collective-permute-start(bf16[1280,256]{1,0:T(8,128)(2,1)S(1)} %constant_dynamic-update-slice_fusion.refs_0_), channel_id=1, source_target_pairs={{0,192},{64,0},{128,64},{192,128},{1,193},{65,1},{129,65},{193,129... | collective-permute-start | bytes 1966088 | tf_op jit(solution)/shard_map/keys_and_values/ppermute | solution.py:33
  42.5 7.2 %collective-permute-start.11 = (bf16[256,256]{1,0:T(8,128)(2,1)S(1)}, bf16[256,256]{1,0:T(8,128)(2,1)S(1)}, u32[]{:S(2)}, u32[]{:S(2)}) collective-permute-start(bf16[256,256]{1,0:T(8,128)(2,1)S(1)} %collective-permute-done.6), channel_id=1, source_target_pairs={{0,56},{8,0},{16,8},{24,16},{32,24},{40,32},{48,40},{56,48},{1,57}... | collective-permute-start | bytes 393224 | tf_op jit(solution)/shard_map/keys_and_values/ppermute | solution.py:33
  44.7 10.7 %collective-permute-start.12 = (bf16[256,256]{1,0:T(8,128)(2,1)S(1)}, bf16[256,256]{1,0:T(8,128)(2,1)S(1)}, u32[]{:S(2)}, u32[]{:S(2)}) collective-permute-start(bf16[256,256]{1,0:T(8,128)(2,1)S(1)} %collective-permute-done.5), channel_id=1, source_target_pairs={{0,16},{8,24},{16,32},{24,40},{32,48},{40,56},{48,0},{56,8},{1,17}... | collective-permute-start | bytes 393224 | tf_op jit(solution)/shard_map/keys_and_values/ppermute | solution.py:33
  44.7 15.2 %collective-permute-start.13 = (bf16[256,256]{1,0:T(8,128)(2,1)S(1)}, bf16[256,256]{1,0:T(8,128)(2,1)S(1)}, u32[]{:S(2)}, u32[]{:S(2)}) collective-permute-start(bf16[256,256]{1,0:T(8,128)(2,1)S(1)} %collective-permute-done.5), channel_id=1, source_target_pairs={{0,8},{8,16},{16,24},{24,32},{32,40},{40,48},{48,56},{56,0},{1,9},... | collective-permute-start | bytes 393224 | tf_op jit(solution)/shard_map/keys_and_values/ppermute | solution.py:33
  45.9 22.5 %collective-permute-start.15 = (bf16[1280,256]{1,0:T(8,128)(2,1)S(1)}, bf16[1280,256]{1,0:T(8,128)(2,1)S(1)}, u32[]{:S(2)}, u32[]{:S(2)}) collective-permute-start(bf16[1280,256]{1,0:T(8,128)(2,1)S(1)} %constant_dynamic-update-slice_fusion.refs_0_), channel_id=1, source_target_pairs={{0,64},{64,128},{128,192},{192,0},{1,65},{65,129},{129,193},{193,1... | collective-permute-start | bytes 1966088 | tf_op jit(solution)/shard_map/keys_and_values/ppermute | solution.py:33
  59.9 8.5 %collective-permute-start.14 = (bf16[768,256]{1,0:T(8,128)(2,1)S(1)}, bf16[768,256]{1,0:T(8,128)(2,1)S(1)}, u32[]{:S(2)}, u32[]{:S(2)}) collective-permute-start(bf16[768,256]{1,0:T(8,128)(2,1)S(1)} %constant_dynamic-update-slice_fusion.5.refs_1_), channel_id=1, source_target_pairs={{0,64},{64,128},{128,192},{192,0},{1,65},{65,129},{129,193},{193,1... | collective-permute-start | bytes 1179656 | tf_op jit(solution)/shard_map/keys_and_values/ppermute | solution.py:33
  60.3 18.1 %collective-permute-start.10 = (bf16[1280,256]{1,0:T(8,128)(2,1)S(1)}, bf16[1280,256]{1,0:T(8,128)(2,1)S(1)}, u32[]{:S(2)}, u32[]{:S(2)}) collective-permute-start(bf16[1280,256]{1,0:T(8,128)(2,1)S(1)} %collective-permute-done.9), channel_id=1, source_target_pairs={{0,192},{64,0},{128,64},{192,128},{1,193},{65,1},{129,65},{193,129... | collective-permute-start | bytes 1966088 | tf_op jit(solution)/shard_map/keys_and_values/ppermute | solution.py:33
  68.4 10.0 %collective-permute-start.16 = (bf16[768,256]{1,0:T(8,128)(2,1)S(1)}, bf16[768,256]{1,0:T(8,128)(2,1)S(1)}, u32[]{:S(2)}, u32[]{:S(2)}) collective-permute-start(bf16[768,256]{1,0:T(8,128)(2,1)S(1)} %collective-permute-done.14.refs_1_), channel_id=1, source_target_pairs={{0,64},{64,128},{128,192},{192,0},{1,65},{65,129},{129,193},{193,1... | collective-permute-start | bytes 1179656 | tf_op jit(solution)/shard_map/keys_and_values/ppermute | solution.py:33
  79.3 43.1 %copy-start = (f32[4096]{0:T(1024)S(1)}, f32[4096]{0:T(1024)}, u32[]{:S(2)}) copy-start(f32[4096]{0:T(1024)} %param.12) | copy-start | bytes 49156
  79.3 23.0 %collective-permute-start.20 = (bf16[256,512]{1,0:T(8,128)(2,1)S(1)}, bf16[256,512]{1,0:T(8,128)(2,1)S(1)}, u32[]{:S(2)}, u32[]{:S(2)}) collective-permute-start(bf16[256,512]{1,0:T(8,128)(2,1)S(1)} %attention.3), channel_id=1, source_target_pairs={{0,64},{2,66},{4,68},{6,70},{64,0},{66,2},{68,4},{70,6},{1,65},{3,... | collective-permute-start | bytes 786440 | tf_op jit(solution)/shard_map/features_of_the_pair/ppermute | solution.py:44
  79.4 22.9 %collective-permute-start.21 = (bf16[256,512]{1,0:T(8,128)(2,1)S(1)}, bf16[256,512]{1,0:T(8,128)(2,1)S(1)}, u32[]{:S(2)}, u32[]{:S(2)}) collective-permute-start(bf16[256,512]{1,0:T(8,128)(2,1)S(1)} %attention.3), channel_id=1, source_target_pairs={{0,66},{2,68},{4,70},{6,64},{64,2},{66,4},{68,6},{70,0},{1,67},{3,... | collective-permute-start | bytes 786440 | tf_op jit(solution)/shard_map/features_of_the_pair/ppermute | solution.py:44
  81.8 20.6 %collective-permute-start.22 = (bf16[256,512]{1,0:T(8,128)(2,1)S(1)}, bf16[256,512]{1,0:T(8,128)(2,1)S(1)}, u32[]{:S(2)}, u32[]{:S(2)}) collective-permute-start(bf16[256,512]{1,0:T(8,128)(2,1)S(1)} %attention.3), channel_id=1, source_target_pairs={{0,70},{2,64},{4,66},{6,68},{64,6},{66,0},{68,2},{70,4},{1,71},{3,... | collective-permute-start | bytes 786440 | tf_op jit(solution)/shard_map/features_of_the_pair/ppermute | solution.py:44
  83.1 19.3 %collective-permute-start.23 = (bf16[256,512]{1,0:T(8,128)(2,1)S(1)}, bf16[256,512]{1,0:T(8,128)(2,1)S(1)}, u32[]{:S(2)}, u32[]{:S(2)}) collective-permute-start(bf16[256,512]{1,0:T(8,128)(2,1)S(1)} %attention.3), channel_id=1, source_target_pairs={{0,68},{2,70},{4,64},{6,66},{64,4},{66,6},{68,0},{70,2},{1,69},{3,... | collective-permute-start | bytes 786440 | tf_op jit(solution)/shard_map/features_of_the_pair/ppermute | solution.py:44
  102.5 7.0 %collective-permute-start.24 = (bf16[1024,512]{1,0:T(8,128)(2,1)S(1)}, bf16[1024,512]{1,0:T(8,128)(2,1)S(1)}, u32[]{:S(2)}, u32[]{:S(2)}) collective-permute-start(bf16[1024,512]{1,0:T(8,128)(2,1)S(1)} %constant_dynamic-update-slice_fusion.8.mine), channel_id=1, source_target_pairs={{0,1},{1,0},{2,3},{3,2},{4,5},{5,4},{6,7},{7,6},{8,9},{9,8},{10,11... | collective-permute-start | bytes 3145736 | tf_op jit(solution)/shard_map/features_of_the_pair/ppermute | solution.py:33
  105.2 22.0 %collective-permute-start.17 = (bf16[256,512]{1,0:T(8,128)(2,1)S(1)}, bf16[256,512]{1,0:T(8,128)(2,1)S(1)}, u32[]{:S(2)}, u32[]{:S(2)}) collective-permute-start(bf16[256,512]{1,0:T(8,128)(2,1)S(1)} %attention.3), channel_id=1, source_target_pairs={{0,2},{2,4},{4,6},{6,0},{1,3},{3,5},{5,7},{7,1},{8,10},{10,12},{12... | collective-permute-start | bytes 786440 | tf_op jit(solution)/shard_map/features_of_the_pair/ppermute | solution.py:33
  106.4 20.8 %collective-permute-start.18 = (bf16[256,512]{1,0:T(8,128)(2,1)S(1)}, bf16[256,512]{1,0:T(8,128)(2,1)S(1)}, u32[]{:S(2)}, u32[]{:S(2)}) collective-permute-start(bf16[256,512]{1,0:T(8,128)(2,1)S(1)} %attention.3), channel_id=1, source_target_pairs={{0,6},{2,0},{4,2},{6,4},{1,7},{3,1},{5,3},{7,5},{8,14},{10,8},{12,... | collective-permute-start | bytes 786440 | tf_op jit(solution)/shard_map/features_of_the_pair/ppermute | solution.py:33
  107.9 19.4 %collective-permute-start.19 = (bf16[256,512]{1,0:T(8,128)(2,1)S(1)}, bf16[256,512]{1,0:T(8,128)(2,1)S(1)}, u32[]{:S(2)}, u32[]{:S(2)}) collective-permute-start(bf16[256,512]{1,0:T(8,128)(2,1)S(1)} %attention.3), channel_id=1, source_target_pairs={{0,4},{2,6},{4,0},{6,2},{1,5},{3,7},{5,1},{7,3},{8,12},{10,14},{12... | collective-permute-start | bytes 786440 | tf_op jit(solution)/shard_map/features_of_the_pair/ppermute | solution.py:33
  127.4 3.0 %collective-permute-start.25 = (bf16[1024,512]{1,0:T(8,128)(2,1)S(1)}, bf16[1024,512]{1,0:T(8,128)(2,1)S(1)}, u32[]{:S(2)}, u32[]{:S(2)}) collective-permute-start(bf16[1024,512]{1,0:T(8,128)(2,1)S(1)} %constant_dynamic-update-slice_fusion.12.mine), channel_id=1, source_target_pairs={{0,1},{1,0},{2,3},{3,2},{4,5},{5,4},{6,7},{7,6},{8,9},{9,8},{10,11... | collective-permute-start | bytes 3145736 | tf_op jit(solution)/shard_map/features/ppermute | solution.py:33
  128.1 12.1 %collective-permute-start.26 = (bf16[256,896]{1,0:T(8,128)(2,1)S(1)}, bf16[256,896]{1,0:T(8,128)(2,1)S(1)}, u32[]{:S(2)}, u32[]{:S(2)}) collective-permute-start(bf16[256,896]{1,0:T(8,128)(2,1)S(1)} %features_of_the_pair.1), channel_id=1, source_target_pairs={{0,64},{64,0},{1,65},{65,1},{2,66},{66,2},{3,67},{67,3},{4,68},{68... | collective-permute-start | bytes 1376264 | tf_op jit(solution)/shard_map/features/ppermute | solution.py:33
  (2 other events, 1.3 us)
Sparse Core Ops, SparseCore 0:
  29.4 92.9 all-gather.1

commit v2 on v1

--- a/solution.py
+++ b/solution.py
@@ -17,6 +17,7 @@
 HEADS_HERE = 4
 HERE = 2
 FAR = 5
+SENT_FIRST = 512
 PARTS = 4
 NORM_EPS = 1e-05
 MASKED = -1e30
@@ -38,6 +39,10 @@
     return y, lax.axis_index("z"), lax.axis_index("x"), lax.axis_index("c")
 
 
+def hop(block, *route, below=NZ):
+    return lax.ppermute(block, ROWS, [(a * NZ + z, b * NZ + z) for a, b in route for z in range(below)])
+
+
 def shift_both(block, across, distance):
     pairs = [(b, i) for b in range(2) for i in range(NX)]
     to = lambda b, i: (b ^ across) * NX + (i + distance) % NX
@@ -45,7 +50,8 @@
 
 
 def z_blocks(block):
-    up1, down1, up2, down2 = (shift(block, "z", d) for d in (1, -1, 2, -2))
+    up1, down1 = shift(block, "z", 1), shift(block, "z", -1)
+    up2, down2 = shift(up1, "z", 1), shift(down1, "z", -1)
     far = jnp.concatenate([up2, up1, block, down1, down2], axis=0)
     up2, down2, far = lax.optimization_barrier((up2, down2, far))
     return far, jnp.concatenate([shift(down2, "z", -1), shift(up2, "z", 2), shift(up2, "z", 1)], axis=0)
@@ -70,29 +76,35 @@
     return starts[mine] - mine * TOK, after - mine * TOK
 
 
-def open_kernel(starts, q, k, v, weight, up, down, theirs, mine, last, sems):
+def open_kernel(starts, q, k, v, weight, own, up, down, theirs, mine, sems):
     first, _ = extent(starts)
     half, odd = weight.shape[1] // 2, lax.rem(here()[0], 2)
     column = lambda side: weight.at[:, pl.ds(pl.multiple_of(side * half, HD), half)]
-    pairs = [(column(1 - odd), theirs), (column(odd), mine)]
-    at, ends = 0, []
+    at, pairs = 0, []
     for ref in (q, k, v):
-        wide = ref.shape[1]
-        pairs.append((ref.at[pl.ds(0, QUARTER)], down.at[:, pl.ds(at, wide)]))
-        pairs.append((ref.at[pl.ds(CAP - 3 * QUARTER, 3 * QUARTER)], last.at[:, pl.ds(at, wide)]))
-        at += wide
+        pairs.append((ref, own.at[:, pl.ds(at, ref.shape[1])]))
+        at += ref.shape[1]
+    pairs += [(column(1 - odd), theirs), (column(odd), mine)]
     copies = [pltpu.make_async_copy(a, b, sems.at[i]) for i, (a, b) in enumerate(pairs)]
     for copy in copies:
         copy.start()
     for copy in copies:
         copy.wait()
-    row = lax.broadcasted_iota(jnp.int32, (QUARTER, 3 * QUARTER), 0)
-    slot = lax.broadcasted_iota(jnp.int32, (QUARTER, 3 * QUARTER), 1) + CAP - 3 * QUARTER
+    row = lax.broadcasted_iota(jnp.int32, (QUARTER, CAP), 0)
+    slot = lax.broadcasted_iota(jnp.int32, (QUARTER, CAP), 1)
     picked = (slot == row + TOK - first).astype(jnp.bfloat16)
-    up[...] = jnp.dot(picked, last[...], preferred_element_type=jnp.float32).astype(jnp.bfloat16)
-
-
-def align_kernel(starts, q, k, v, low, high, q_out, kv_out):
+    up[...] = jnp.dot(picked, own[...], preferred_element_type=jnp.float32).astype(jnp.bfloat16)
+    down[...] = own[:QUARTER]
+
+
+def align_kernel(starts, rows, low, high, own_part, below, above, far_part, q_out, kv_out, pair, sems):
+    depth = own_part.shape[0]
+    copies = [
+        pltpu.make_async_copy(part, pair.at[pl.ds(i * depth, depth)], sems.at[i])
+        for i, part in enumerate((own_part, below, above, far_part))
+    ]
+    for copy in copies:
+        copy.start()
     first, end = extent(starts)
     row = lax.broadcasted_iota(jnp.int32, (TOK, 1), 0)
     slot = lax.broadcasted_iota(jnp.int32, (TOK, CAP), 1)
@@ -100,14 +112,18 @@
     own = ((slot == row - first) & (row >= first) & (row < end)).astype(jnp.bfloat16)
     from_low = ((near == row) & (row < first)).astype(jnp.bfloat16)
     from_high = ((near == row - end) & (row >= end)).astype(jnp.bfloat16)
-    at = 0
-    for ref, out, place in ((q, q_out, 0), (k, kv_out, 0), (v, kv_out, HD)):
-        wide = ref.shape[1]
-        total = jnp.dot(own, ref[...], preferred_element_type=jnp.float32)
-        total += jnp.dot(from_low, low[:, at : at + wide], preferred_element_type=jnp.float32)
-        total += jnp.dot(from_high, high[:, at : at + wide], preferred_element_type=jnp.float32)
-        out[:, place : place + wide] = total.astype(jnp.bfloat16)
-        at += wide
+    total = jnp.dot(own, rows[...], preferred_element_type=jnp.float32)
+    total += jnp.dot(from_low, low[...], preferred_element_type=jnp.float32)
+    total += jnp.dot(from_high, high[...], preferred_element_type=jnp.float32)
+    wide = q_out.shape[1]
+    q_out[...] = total[:, :wide].astype(jnp.bfloat16)
+    kv_out[...] = total[:, wide:].astype(jnp.bfloat16)
+    for copy in copies:
+        copy.wait()
+
+
+def in_hbm(array):
+    return pltpu.with_memory_space_constraint(array, pltpu.HBM)
 
 
 def opening(starts, q, k, v, weight):
@@ -115,25 +131,27 @@
     rows, half = weight.shape[0], weight.shape[1] // 2
     return pl.pallas_call(
         open_kernel,
-        out_shape=(bf16(QUARTER, wide),) * 2 + (bf16(rows, half),) * 2,
+        out_shape=(bf16(CAP, wide), *(bf16(QUARTER, wide),) * 2, *(bf16(rows, half),) * 2),
         in_specs=[SMEM] + [HBM] * 4,
-        out_specs=(VMEM,) * 4,
-        scratch_shapes=[pltpu.VMEM((3 * QUARTER, wide), jnp.bfloat16), pltpu.SemaphoreType.DMA((8,))],
-        compiler_params=limit(60),
-    )(starts, q, k, v, weight)
-
-
-def align(starts, q, k, v, up, down):
+        out_specs=(VMEM,) * 5,
+        scratch_shapes=[pltpu.SemaphoreType.DMA((5,))],
+        compiler_params=limit(16),
+    )(starts, *(in_hbm(a) for a in (q, k, v, weight)))
+
+
+def align(starts, own, up, down, parts):
     count = NY * NZ
     low = lax.ppermute(up, ROWS, [(i, (i + 1) % count) for i in range(count)])
     high = lax.ppermute(down, ROWS, [(i, (i - 1) % count) for i in range(count)])
+    depth, columns = parts[0].shape
     return pl.pallas_call(
         align_kernel,
-        out_shape=(bf16(TOK, q.shape[1]), bf16(TOK, 2 * HD)),
-        in_specs=[SMEM] + [VMEM] * 5,
-        out_specs=(VMEM,) * 2,
-        compiler_params=limit(60),
-    )(starts, q, k, v, low, high)
+        out_shape=(bf16(TOK, HEADS_HERE * HD), bf16(TOK, 2 * HD), bf16(NY * depth, columns)),
+        in_specs=[SMEM] + [VMEM] * 7,
+        out_specs=(VMEM, VMEM, HBM),
+        scratch_shapes=[pltpu.SemaphoreType.DMA((4,))],
+        compiler_params=limit(16),
+    )(starts, own, low, high, *parts)
 
 
 def attention_kernel(back, parts, place, lengths, q_ref, *refs):
@@ -244,12 +262,7 @@
     )(lengths, q, *blocks, *state)
 
 
-def gate_kernel(gain, mine, other, weight, out, rows, held, total, sems):
-    depth = FEATURES // PARTS
-    parts = [pl.ds(i * depth, depth) for i in range(PARTS)]
-    copies = [pltpu.make_async_copy(weight.at[p], held.at[p], sems.at[i]) for i, p in enumerate(parts)]
-    for copy in copies:
-        copy.start()
+def prepare_kernel(gain, mine, other, rows, inv):
     y, _, x, c = here()
     squares = jnp.zeros((TOK, HD), jnp.float32)
     for side, pieces in enumerate((mine, other)):
@@ -264,7 +277,27 @@
                 slot = jnp.where(away == 0, 0, jnp.where(away == 3, 1, away + 1))
                 place = lax.rem(head, NZ) * NY + slot
                 rows[:, pl.ds(pl.multiple_of(place * HD, HD), HD)] = scaled
-    inv = lax.rsqrt(jnp.sum(squares, axis=1, keepdims=True) / FEATURES + NORM_EPS)
+    mean = jnp.sum(squares, axis=1, keepdims=True) / FEATURES
+    inv[...] = jnp.broadcast_to(lax.rsqrt(mean + NORM_EPS), (TOK, HD))
+
+
+def prepare(gain, mine, other):
+    return pl.pallas_call(
+        prepare_kernel,
+        out_shape=(bf16(TOK, FEATURES), f32(TOK, HD)),
+        in_specs=[VMEM] * 3,
+        out_specs=(VMEM,) * 2,
+        compiler_params=limit(16),
+    )(gain, mine, other)
+
+
+def gate_kernel(first, rows, inv, weight, out, held, total, sems):
+    depth = FEATURES // PARTS
+    parts = [pl.ds(i * depth, depth) for i in range(PARTS)]
+    columns = pl.ds(first, out.shape[1])
+    copies = [pltpu.make_async_copy(weight.at[p, columns], held.at[p], sems.at[i]) for i, p in enumerate(parts)]
+    for copy in copies:
+        copy.start()
     for i, copy in enumerate(copies):
         copy.wait()
         term = jnp.dot(
@@ -277,20 +310,18 @@
         elif i < PARTS - 1:
             total[...] += term
         else:
-            value = (total[...] + term) * inv
+            value = (total[...] + term) * inv[:, :1]
             out[...] = (value / (1.0 + jnp.exp(-value))).astype(jnp.bfloat16)
 
 
-def gate(gain, mine, other, weight):
-    columns = weight.shape[1]
-    return pl.pallas_call(
-        gate_kernel,
+def gate(rows, inv, weight, first, columns):
+    return pl.pallas_call(
+        functools.partial(gate_kernel, first),
         out_shape=bf16(TOK, columns),
-        in_specs=[VMEM] * 3 + [HBM],
+        in_specs=[VMEM] * 2 + [HBM],
         out_specs=VMEM,
         scratch_shapes=[
-            pltpu.VMEM((TOK, FEATURES), jnp.bfloat16),
-            pltpu.VMEM(weight.shape, weight.dtype),
+            pltpu.VMEM((FEATURES, columns), weight.dtype),
             pltpu.VMEM((TOK, columns), jnp.float32),
             pltpu.SemaphoreType.DMA((PARTS,)),
         ],
@@ -298,60 +329,71 @@
         cost_estimate=pl.CostEstimate(
             flops=2 * TOK * FEATURES * columns, bytes_accessed=2 * FEATURES * columns, transcendentals=TOK * columns
         ),
-    )(gain, mine, other, pltpu.with_memory_space_constraint(weight, pltpu.HBM))
-
-
-def join_kernel(home, back, out):
-    columns = home.shape[1]
-    odd = lax.rem(here()[0], 2)
-    out[:, pl.ds(pl.multiple_of(odd * columns, HD), columns)] = home[...]
-    out[:, pl.ds(pl.multiple_of((1 - odd) * columns, HD), columns)] = back[...]
-
-
-def join(home, back):
+    )(rows, inv, in_hbm(weight))
+
+
+def join_kernel(*refs):
+    *parts, out = refs
+    half, odd = out.shape[1] // 2, lax.rem(here()[0], 2)
+    at = 0
+    for ref in parts:
+        side = odd if at < half else 1 - odd
+        place = side * half + at % half
+        out[:, pl.ds(pl.multiple_of(place, HD), ref.shape[1])] = ref[...]
+        at += ref.shape[1]
+
+
+def join(*parts):
     return pl.pallas_call(
         join_kernel,
-        out_shape=bf16(TOK, 2 * home.shape[1]),
-        in_specs=[VMEM] * 2,
+        out_shape=bf16(TOK, sum(part.shape[1] for part in parts)),
+        in_specs=[VMEM] * len(parts),
         out_specs=VMEM,
         compiler_params=limit(8),
-    )(home, back)
+    )(*parts)
 
 
 def on_device(queries, keys, values, doc_lengths, shard_starts, norm_gain, ffn_weight):
     with jax.named_scope("rows_to_owners"):
-        up, down, theirs, mine = opening(shard_starts, queries, keys, values, ffn_weight)
-        q, kv = align(shard_starts, queries, keys, values, up, down)
+        own, up, down, theirs, mine = opening(shard_starts, queries, keys, values, ffn_weight)
+        parts = [mine, shift(theirs, TALL, 1), shift(theirs, TALL, -1), shift(mine, TALL, 2)]
+        q, kv, pair = align(shard_starts, own, up, down, parts)
 
     with jax.named_scope("weight_rows"):
-        parts = [mine, shift(theirs, TALL, 1), shift(theirs, TALL, -1), shift(mine, TALL, 2)]
-        *parts, kv = lax.optimization_barrier((*parts, kv))
-        weight = lax.all_gather(jnp.concatenate(parts, axis=0), "z", axis=0, tiled=True)
+        weight = lax.all_gather(pair, "z", axis=0, tiled=True)
 
     with jax.named_scope("keys_and_values"):
         far, near = z_blocks(kv)
-        far1, far3 = shift(far, TALL, 1), shift(far, TALL, -1)
-        near1, far2 = shift(near, TALL, 1), shift(far3, TALL, -1)
+        far1, near1 = (hop(a, (0, 1), (1, 2), (2, 3)) for a in (far, near))
+        outer, inner = far[: HERE * TOK], far[HERE * TOK :]
+        inner2 = hop(hop(inner, (1, 0), (0, 3)), (3, 2), (0, 3))
+        outer2 = hop(hop(outer, (1, 0), (0, 3), below=HERE), (3, 2), (0, 3), below=HERE)
         state = attention(0, doc_lengths, q, [far, near], ())
         near1, far1, *state = lax.optimization_barrier((near1, far1, *state))
-        near2 = shift(near1, TALL, 1)
+        near2 = hop(near1, (1, 2), (2, 3), below=FAR)
 
     with jax.named_scope("attention"):
         state = attention(1, doc_lengths, q, [far1, near1], state)
-        (attended,) = attention(2, doc_lengths, q, [far2, near2], state)
+        (attended,) = attention(2, doc_lengths, q, [outer2, inner2, near2], state)
 
     gain = norm_gain.reshape(1, FEATURES)
-    with jax.named_scope("features_of_the_pair"):
-        pieces = [shift_both(attended, 1, d) for d in (0, 1, -1, 2)]
+    half = weight.shape[1]
+    with jax.named_scope("features"):
+        theirs = [shift_both(attended, 1, d) for d in (0, 1, -1, 2)]
         own = [attended] + [shift(attended, "x", d) for d in (1, -1, 2)]
-        mine = jnp.concatenate(pieces, axis=0)
-        away = gate(gain, mine, shift(mine, "c", 1), weight)
-
-    with jax.named_scope("features"):
-        *own, away = lax.optimization_barrier((*own, away))
-        mine = jnp.concatenate(own, axis=0)
-        home = gate(gain, mine, shift(mine, "c", 1), weight)
-        return join(home, shift(away, "yb", 1))
+        theirs, own = jnp.concatenate(theirs, axis=0), jnp.concatenate(own, axis=0)
+        their_rows, their_inv = prepare(gain, theirs, shift(theirs, "c", 1))
+        other = shift(own, "c", 1)
+
+    with jax.named_scope("gate"):
+        away = gate(their_rows, their_inv, weight, 0, SENT_FIRST)
+        back = [shift(away, "yb", 1)]
+        their_inv, away = lax.optimization_barrier((their_inv, away))
+        rest = gate(their_rows, their_inv, weight, SENT_FIRST, half - SENT_FIRST)
+        back.append(shift(rest, "yb", 1))
+        gain, rest = lax.optimization_barrier((gain, rest))
+        home = gate(*prepare(gain, own, other), weight, 0, half)
+        return join(home, *back)
 
 
 def solution(mesh):

time: 148 us -> 145 us (0.980)
  waiting for transfers between devices: 72.2 us -> 48.5 us
  starting transfers between devices: 39.9 us -> 59.8 us
  Pallas kernels: 18.9 us -> 21 us
  other arithmetic: 1.97 us -> 0.07 us
    ppermute x21 -> x17, waiting for transfers between devices: 39.6 us -> 18.1 us  [shift(): lax.ppermute(block, axis, [(i, (i + distance) % count) for i in range(cou...]
    ppermute x0 -> x7, starting transfers between devices: none -> 19.1 us  [hop(): lax.ppermute(block, ROWS, [(a * NZ + z, b * NZ + z) for a, b in route for...]
    all_gather x1, waiting for transfers between devices: 13 us -> 4.92 us  [on_device(): weight = lax.all_gather(pair, 'z', axis=0, tiled=True)]
    ppermute x0 -> x7, waiting for transfers between devices: none -> 7.7 us  [hop(): lax.ppermute(block, ROWS, [(a * NZ + z, b * NZ + z) for a, b in route for...]
    pallas_call x5 -> x8, Pallas kernels: 15.8 us -> 17.9 us  [the longest x3 10.1 us: gate(): pl.pallas_call(functools.partial(gate_kernel, first), out_shape=bf16(TOK,...]
    concatenate x1, other arithmetic: 1.97 us -> 0.07 us  [on_device(): jnp.concatenate(own, axis=0)]
    ppermute x4, waiting for transfers between devices: 16.6 us -> 15 us  [shift_both(): lax.ppermute(block, ('yb', 'x'), [(b * NX + i, to(b, i)) for b, i in pairs])]
    ppermute x21 -> x17, starting transfers between devices: 27.4 us -> 28.3 us  [shift(): lax.ppermute(block, axis, [(i, (i + distance) % count) for i in range(cou...]
  transfers between devices with their start and end apart: 28 -> 31, of which waited for: 13 -> 13; matrix products, arithmetic and copies ran while one was open for 0% -> 0% of each run, Pallas kernels for 10% -> 11%
where the time goes in v2:
time: 145 us; the launch traced here: 144 us
  starting transfers between devices  59.8 us (41%)
  waiting for transfers between devices  48.5 us (33%)
  Pallas kernels  21 us (14%)
  between operations  13.7 us (9%)
    ppermute x17, starting transfers between devices, shift(): lax.ppermute(block, axis, [(i, (i + distance) % count) for i in range(cou...  28.3 us
    ppermute x7, starting transfers between devices, hop(): lax.ppermute(block, ROWS, [(a * NZ + z, b * NZ + z) for a, b in route for...  19.1 us
    ppermute x17, waiting for transfers between devices, shift(): lax.ppermute(block, axis, [(i, (i + distance) % count) for i in range(cou...  18.1 us
    ppermute x4, waiting for transfers between devices, shift_both(): lax.ppermute(block, ('yb', 'x'), [(b * NX + i, to(b, i)) for b, i in pairs])  15 us
    pallas_call x3, Pallas kernels, gate(): pl.pallas_call(functools.partial(gate_kernel, first), out_shape=bf16(TOK,...  10.1 us
    ppermute x7, waiting for transfers between devices, hop(): lax.ppermute(block, ROWS, [(a * NZ + z, b * NZ + z) for a, b in route for...  7.7 us
    ppermute x4, starting transfers between devices, shift_both(): lax.ppermute(block, ('yb', 'x'), [(b * NX + i, to(b, i)) for b, i in pairs])  6.38 us
    all_gather x1, waiting for transfers between devices, on_device(): weight = lax.all_gather(pair, 'z', axis=0, tiled=True)  4.92 us
  transfers between devices with their start and end apart: 31, of which 13 were waited for; matrix products, arithmetic and copies ran while one was open for 0% of the time, Pallas kernels for 11%

profile of v2, /device:TPU:1, one launch (start us, length us, event | category | flops | bytes accessed | tf_op | source)
XLA Modules:
  0.0 144.0 jit_solution(10891719855186924718)
XLA Ops:
  7.2 2.0 %rows_to_owners.2 = (bf16[384,768]{1,0:T(8,128)(2,1)S(1)}, bf16[64,768]{1,0:T(8,128)(2,1)S(1)}, bf16[64,768]{1,0:T(8,128)(2,1)S(1)}, bf16[128,896]{1,0:T(8,128)(2,1)S(1)}, bf16[128,896]{1,0:T(8,128)(2,1)S(1)}) custom-call(s32[32]{0:T(128)S(1)} %copy-done.1, bf16[384,512]{1,0:T(8,128)(2,1)} %q.1, bf16[384,128]{1,0:T(8,128)(2,1)} %k.1, bf16[384,128]{1,0:T(8,128)(2,1)} %v.1, ...), custom_call_target="tpu_custom_call" | custom-call | tf_op jit(solution)/shard_map/rows_to_owners/pallas_call | solution.py:132
  9.2 2.2 %collective-permute-start.2 = (bf16[128,896]{1,0:T(8,128)(2,1)S(1)}, bf16[128,896]{1,0:T(8,128)(2,1)S(1)}, u32[]{:S(2)}, u32[]{:S(2)}) collective-permute-start(bf16[128,896]{1,0:T(8,128)(2,1)S(1)} %get-tuple-element.34), channel_id=1, source_target_pairs={{0,64},{64,128},{128,192},{192,0},{1,65},{65,129},{129,193},{193,1... | collective-permute-start | bytes 688136 | tf_op jit(solution)/shard_map/rows_to_owners/ppermute | solution.py:34
  16.2 4.4 %collective-permute-start.1 = (bf16[64,768]{1,0:T(8,128)(2,1)S(1)}, bf16[64,768]{1,0:T(8,128)(2,1)S(1)}, u32[]{:S(2)}, u32[]{:S(2)}) collective-permute-start(bf16[64,768]{1,0:T(8,128)(2,1)S(1)} %get-tuple-element.32), channel_id=1, source_target_pairs={{0,248},{8,0},{16,8},{24,16},{32,24},{40,32},{48,40},{56,48},{64,5... | collective-permute-start | bytes 294920 | tf_op jit(solution)/shard_map/rows_to_owners/ppermute | solution.py:145
  20.6 2.7 %collective-permute-done.low = bf16[64,768]{1,0:T(8,128)(2,1)S(1)} collective-permute-done((bf16[64,768]{1,0:T(8,128)(2,1)S(1)}, bf16[64,768]{1,0:T(8,128)(2,1)S(1)}, u32[]{:S(2)}, u32[]{:S(2)}) %collective-permute-start) | collective-permute-done | bytes 98336 | tf_op jit(solution)/shard_map/rows_to_owners/ppermute | solution.py:144
  23.4 2.7 %collective-permute-done.4.far_part = bf16[128,896]{1,0:T(8,128)(2,1)S(1)} collective-permute-done((bf16[128,896]{1,0:T(8,128)(2,1)S(1)}, bf16[128,896]{1,0:T(8,128)(2,1)S(1)}, u32[]{:S(2)}, u32[]{:S(2)}) %collective-permute-start.4) | collective-permute-done | bytes 229408 | tf_op jit(solution)/shard_map/rows_to_owners/ppermute | solution.py:34
  27.7 3.6 %collective-permute-start.7 = (bf16[256,256]{1,0:T(8,128)(2,1)S(1)}, bf16[256,256]{1,0:T(8,128)(2,1)S(1)}, u32[]{:S(2)}, u32[]{:S(2)}) collective-permute-start(bf16[256,256]{1,0:T(8,128)(2,1)S(1)} %get-tuple-element.36), channel_id=1, source_target_pairs={{0,56},{8,0},{16,8},{24,16},{32,24},{40,32},{48,40},{56,48},{1,57}... | collective-permute-start | bytes 393224 | tf_op jit(solution)/shard_map/keys_and_values/ppermute | solution.py:34
  31.3 2.3 %collective-permute-done.5 = bf16[256,256]{1,0:T(8,128)(2,1)S(1)} collective-permute-done((bf16[256,256]{1,0:T(8,128)(2,1)S(1)}, bf16[256,256]{1,0:T(8,128)(2,1)S(1)}, u32[]{:S(2)}, u32[]{:S(2)}) %collective-permute-start.5) | collective-permute-done | bytes 131104 | tf_op jit(solution)/shard_map/keys_and_values/ppermute | solution.py:34
  33.5 2.8 %collective-permute-start.8 = (bf16[256,256]{1,0:T(8,128)(2,1)S(1)}, bf16[256,256]{1,0:T(8,128)(2,1)S(1)}, u32[]{:S(2)}, u32[]{:S(2)}) collective-permute-start(bf16[256,256]{1,0:T(8,128)(2,1)S(1)} %collective-permute-done.7), channel_id=1, source_target_pairs={{0,56},{8,0},{16,8},{24,16},{32,24},{40,32},{48,40},{56,48},{1,57}... | collective-permute-start | bytes 393224 | tf_op jit(solution)/shard_map/keys_and_values/ppermute | solution.py:34
  36.3 2.3 %collective-permute-done.6 = bf16[256,256]{1,0:T(8,128)(2,1)S(1)} collective-permute-done((bf16[256,256]{1,0:T(8,128)(2,1)S(1)}, bf16[256,256]{1,0:T(8,128)(2,1)S(1)}, u32[]{:S(2)}, u32[]{:S(2)}) %collective-permute-start.6) | collective-permute-done | bytes 131104 | tf_op jit(solution)/shard_map/keys_and_values/ppermute | solution.py:34
  38.7 2.8 %collective-permute-start.13 = (bf16[256,256]{1,0:T(8,128)(2,1)S(1)}, bf16[256,256]{1,0:T(8,128)(2,1)S(1)}, u32[]{:S(2)}, u32[]{:S(2)}) collective-permute-start(bf16[256,256]{1,0:T(8,128)(2,1)S(1)} %collective-permute-done.8), channel_id=1, source_target_pairs={{0,56},{8,0},{16,8},{24,16},{32,24},{40,32},{48,40},{56,48},{1,57}... | collective-permute-start | bytes 393224 | tf_op jit(solution)/shard_map/keys_and_values/ppermute | solution.py:34
  41.4 1.9 %collective-permute-start.15 = (bf16[256,256]{1,0:T(8,128)(2,1)S(1)}, bf16[256,256]{1,0:T(8,128)(2,1)S(1)}, u32[]{:S(2)}, u32[]{:S(2)}) collective-permute-start(bf16[256,256]{1,0:T(8,128)(2,1)S(1)} %collective-permute-done.6), channel_id=1, source_target_pairs={{0,8},{8,16},{16,24},{24,32},{32,40},{40,48},{48,56},{56,0},{1,9},... | collective-permute-start | bytes 393224 | tf_op jit(solution)/shard_map/keys_and_values/ppermute | solution.py:34
  43.4 2.7 %collective-permute-start.17 = (bf16[1280,256]{1,0:T(8,128)(2,1)S(1)}, bf16[1280,256]{1,0:T(8,128)(2,1)S(1)}, u32[]{:S(2)}, u32[]{:S(2)}) collective-permute-start(bf16[1280,256]{1,0:T(8,128)(2,1)S(1)} %constant_dynamic-update-slice_fusion.refs_0_), channel_id=1, source_target_pairs={{0,64},{8,72},{16,80},{24,88},{32,96},{40,104},{48,112},{56,120},{... | collective-permute-start | bytes 1966088 | tf_op jit(solution)/shard_map/keys_and_values/ppermute | solution.py:43
  46.1 1.9 %collective-permute-start.11 = (bf16[768,256]{1,0:T(8,128)(2,1)S(1)}, bf16[768,256]{1,0:T(8,128)(2,1)S(1)}, u32[]{:S(2)}, u32[]{:S(2)}) collective-permute-start(bf16[768,256]{1,0:T(8,128)(2,1)S(1)} %slice.7), channel_id=1, source_target_pairs={{64,0},{72,8},{80,16},{88,24},{96,32},{104,40},{112,48},{120,56},{... | collective-permute-start | bytes 1179656 | tf_op jit(solution)/shard_map/keys_and_values/ppermute | solution.py:43
  48.0 2.3 %collective-permute-done.14 = bf16[256,256]{1,0:T(8,128)(2,1)S(1)} collective-permute-done((bf16[256,256]{1,0:T(8,128)(2,1)S(1)}, bf16[256,256]{1,0:T(8,128)(2,1)S(1)}, u32[]{:S(2)}, u32[]{:S(2)}) %collective-permute-start.14) | collective-permute-done | bytes 131104 | tf_op jit(solution)/shard_map/keys_and_values/ppermute | solution.py:34
  50.3 3.6 %collective-permute-done.15 = bf16[256,256]{1,0:T(8,128)(2,1)S(1)} collective-permute-done((bf16[256,256]{1,0:T(8,128)(2,1)S(1)}, bf16[256,256]{1,0:T(8,128)(2,1)S(1)}, u32[]{:S(2)}, u32[]{:S(2)}) %collective-permute-start.15) | collective-permute-done | bytes 131104 | tf_op jit(solution)/shard_map/keys_and_values/ppermute | solution.py:34
  53.9 4.9 %collective-permute-start.16 = (bf16[768,256]{1,0:T(8,128)(2,1)S(1)}, bf16[768,256]{1,0:T(8,128)(2,1)S(1)}, u32[]{:S(2)}, u32[]{:S(2)}) collective-permute-start(bf16[768,256]{1,0:T(8,128)(2,1)S(1)} %constant_dynamic-update-slice_fusion.5.refs_1_), channel_id=1, source_target_pairs={{0,64},{8,72},{16,80},{24,88},{32,96},{40,104},{48,112},{56,120},{... | collective-permute-start | bytes 1179656 | tf_op jit(solution)/shard_map/keys_and_values/ppermute | solution.py:43
  58.8 2.1 %collective-permute-start.9 = (bf16[512,256]{1,0:T(8,128)(2,1)S(1)}, bf16[512,256]{1,0:T(8,128)(2,1)S(1)}, u32[]{:S(2)}, u32[]{:S(2)}) collective-permute-start(bf16[512,256]{1,0:T(8,128)(2,1)S(1)} %slice.6), channel_id=1, source_target_pairs={{64,0},{72,8},{0,192},{8,200},{65,1},{73,9},{1,193},{9,201},{66,2}... | collective-permute-start | bytes 786440 | tf_op jit(solution)/shard_map/keys_and_values/ppermute | solution.py:43
  63.7 2.4 %collective-permute-done.16.refs_1_ = bf16[768,256]{1,0:T(8,128)(2,1)S(1)} collective-permute-done((bf16[768,256]{1,0:T(8,128)(2,1)S(1)}, bf16[768,256]{1,0:T(8,128)(2,1)S(1)}, u32[]{:S(2)}, u32[]{:S(2)}) %collective-permute-start.16) | collective-permute-done | bytes 393248 | tf_op jit(solution)/shard_map/keys_and_values/ppermute | solution.py:43
  66.7 5.5 %collective-permute-start.10 = (bf16[512,256]{1,0:T(8,128)(2,1)S(1)}, bf16[512,256]{1,0:T(8,128)(2,1)S(1)}, u32[]{:S(2)}, u32[]{:S(2)}) collective-permute-start(bf16[512,256]{1,0:T(8,128)(2,1)S(1)} %collective-permute-done.9), channel_id=1, source_target_pairs={{192,128},{200,136},{0,192},{8,200},{193,129},{201,137},{1,193},{9... | collective-permute-start | bytes 786440 | tf_op jit(solution)/shard_map/keys_and_values/ppermute | solution.py:43
  73.0 5.3 %collective-permute-done.10.refs_0_ = bf16[512,256]{1,0:T(8,128)(2,1)S(1)} collective-permute-done((bf16[512,256]{1,0:T(8,128)(2,1)S(1)}, bf16[512,256]{1,0:T(8,128)(2,1)S(1)}, u32[]{:S(2)}, u32[]{:S(2)}) %collective-permute-start.10) | collective-permute-done | bytes 262176 | tf_op jit(solution)/shard_map/keys_and_values/ppermute | solution.py:43
  79.3 2.4 %collective-permute-start.20 = (bf16[256,512]{1,0:T(8,128)(2,1)S(1)}, bf16[256,512]{1,0:T(8,128)(2,1)S(1)}, u32[]{:S(2)}, u32[]{:S(2)}) collective-permute-start(bf16[256,512]{1,0:T(8,128)(2,1)S(1)} %attention.3), channel_id=1, source_target_pairs={{0,66},{2,68},{4,70},{6,64},{64,2},{66,4},{68,6},{70,0},{1,67},{3,... | collective-permute-start | bytes 786440 | tf_op jit(solution)/shard_map/features/ppermute | solution.py:49
  83.0 2.6 %collective-permute-start.22 = (bf16[256,512]{1,0:T(8,128)(2,1)S(1)}, bf16[256,512]{1,0:T(8,128)(2,1)S(1)}, u32[]{:S(2)}, u32[]{:S(2)}) collective-permute-start(bf16[256,512]{1,0:T(8,128)(2,1)S(1)} %attention.3), channel_id=1, source_target_pairs={{0,68},{2,70},{4,64},{6,66},{64,4},{66,6},{68,0},{70,2},{1,69},{3,... | collective-permute-start | bytes 786440 | tf_op jit(solution)/shard_map/features/ppermute | solution.py:49
  87.1 15.0 %collective-permute-done.19 = bf16[256,512]{1,0:T(8,128)(2,1)S(1)} collective-permute-done((bf16[256,512]{1,0:T(8,128)(2,1)S(1)}, bf16[256,512]{1,0:T(8,128)(2,1)S(1)}, u32[]{:S(2)}, u32[]{:S(2)}) %collective-permute-start.19) | collective-permute-done | bytes 262176 | tf_op jit(solution)/shard_map/features/ppermute | solution.py:49
  102.1 3.4 %collective-permute-start.25 = (bf16[256,512]{1,0:T(8,128)(2,1)S(1)}, bf16[256,512]{1,0:T(8,128)(2,1)S(1)}, u32[]{:S(2)}, u32[]{:S(2)}) collective-permute-start(bf16[256,512]{1,0:T(8,128)(2,1)S(1)} %attention.3), channel_id=1, source_target_pairs={{0,6},{2,0},{4,2},{6,4},{1,7},{3,1},{5,3},{7,5},{8,14},{10,8},{12,... | collective-permute-start | bytes 786440 | tf_op jit(solution)/shard_map/features/ppermute | solution.py:34
  105.7 2.3 %collective-permute-start.23 = (bf16[1024,512]{1,0:T(8,128)(2,1)S(1)}, bf16[1024,512]{1,0:T(8,128)(2,1)S(1)}, u32[]{:S(2)}, u32[]{:S(2)}) collective-permute-start(bf16[1024,512]{1,0:T(8,128)(2,1)S(1)} %constant_dynamic-update-slice_fusion.8.mine), channel_id=1, source_target_pairs={{0,1},{1,0},{2,3},{3,2},{4,5},{5,4},{6,7},{7,6},{8,9},{9,8},{10,11... | collective-permute-start | bytes 3145736 | tf_op jit(solution)/shard_map/features/ppermute | solution.py:34
  109.1 3.3 %collective-permute-done.24 = bf16[256,512]{1,0:T(8,128)(2,1)S(1)} collective-permute-done((bf16[256,512]{1,0:T(8,128)(2,1)S(1)}, bf16[256,512]{1,0:T(8,128)(2,1)S(1)}, u32[]{:S(2)}, u32[]{:S(2)}) %collective-permute-start.24) | collective-permute-done | bytes 262176 | tf_op jit(solution)/shard_map/features/ppermute | solution.py:34
  112.5 3.1 %collective-permute-start.27 = (bf16[1024,512]{1,0:T(8,128)(2,1)S(1)}, bf16[1024,512]{1,0:T(8,128)(2,1)}, u32[]{:S(2)}, u32[]{:S(2)}) collective-permute-start(bf16[1024,512]{1,0:T(8,128)(2,1)S(1)} %pad_maximum_fusion.mine), channel_id=1, source_target_pairs={{0,1},{1,0},{2,3},{3,2},{4,5},{5,4},{6,7},{7,6},{8,9},{9,8},{10,11... | collective-permute-start | bytes 3145736 | tf_op jit(solution)/shard_map/features/ppermute | solution.py:34
  116.7 4.9 %all-gather.2.cloned.1.call-done.weight = bf16[4096,896]{1,0:T(8,128)(2,1)} async-done(((bf16[512,896]{1,0:T(8,128)(2,1)}), bf16[4096,896]{1,0:T(8,128)(2,1)}) %all-gather.2.cloned.1.call-update) | async-done | bytes 7340048 | tf_op jit(solution)/shard_map/weight_rows/all_gather | solution.py:363
  121.6 2.7 %gate.5 = bf16[256,512]{1,0:T(8,128)(2,1)S(1)} custom-call(bf16[256,4096]{1,0:T(8,128)(2,1)S(1)} %get-tuple-element.48.rows, f32[256,128]{1,0:T(8,128)S(1)} %get-tuple-element.51.inv, bf16[4096,896]{1,0:T(8,128)(2,1)} %all-gather.2.cloned.1.call-done.weight), custom_call_target="tpu_custom_call" | custom-call | flops 1073741824 | bytes 4194304 | tf_op jit(solution)/shard_map/gate/pallas_call | solution.py:318
  125.8 2.9 %gate.6 = bf16[256,384]{1,0:T(8,128)(2,1)S(1)} custom-call(bf16[256,4096]{1,0:T(8,128)(2,1)S(1)} %get-tuple-element.48.rows, f32[256,128]{1,0:T(8,128)S(1)} %get-tuple-element.51.inv, bf16[4096,896]{1,0:T(8,128)(2,1)} %all-gather.2.cloned.1.call-done.weight), custom_call_target="tpu_custom_call" | custom-call | flops 805306368 | bytes 3145728 | tf_op jit(solution)/shard_map/gate/pallas_call | solution.py:318
  128.9 2.3 %gate.7 = (bf16[256,4096]{1,0:T(8,128)(2,1)S(1)}, f32[256,128]{1,0:T(8,128)S(1)}) custom-call(f32[1,4096]{1,0:T(1,128)S(1)} %bitcast.2, bf16[1024,512]{1,0:T(8,128)(2,1)S(1)} %pad_maximum_fusion.mine, bf16[1024,512]{1,0:T(8,128)(2,1)} %collective-permute-done.27.other), custom_call_target="tpu_custom_call" | custom-call | tf_op jit(solution)/shard_map/gate/pallas_call | solution.py:285
  131.2 4.4 %gate.8.refs_0_ = bf16[256,896]{1,0:T(8,128)(2,1)S(1)} custom-call(bf16[256,4096]{1,0:T(8,128)(2,1)S(1)} %get-tuple-element.53.rows, f32[256,128]{1,0:T(8,128)S(1)} %get-tuple-element.54.inv, bf16[4096,896]{1,0:T(8,128)(2,1)} %all-gather.2.cloned.1.call-done.weight), custom_call_target="tpu_custom_call" | custom-call | flops 1879048192 | bytes 7340032 | tf_op jit(solution)/shard_map/gate/pallas_call | solution.py:318
  (63 shorter events, 20.5 us)
Async XLA Ops:
  6.5 115.1 %all-gather.2.cloned.1.call-start = ((), (), s32[]{:S(2)}) async-start(), calls=%async_computation | async-start | bytes 8257536 | tf_op jit(solution)/shard_map/weight_rows/all_gather | solution.py:363
  9.2 14.1 %collective-permute-start.2 = (bf16[128,896]{1,0:T(8,128)(2,1)S(1)}, bf16[128,896]{1,0:T(8,128)(2,1)S(1)}, u32[]{:S(2)}, u32[]{:S(2)}) collective-permute-start(bf16[128,896]{1,0:T(8,128)(2,1)S(1)} %get-tuple-element.34), channel_id=1, source_target_pairs={{0,64},{64,128},{128,192},{192,0},{1,65},{65,129},{129,193},{193,1... | collective-permute-start | bytes 688136 | tf_op jit(solution)/shard_map/rows_to_owners/ppermute | solution.py:34
  11.4 11.9 %collective-permute-start.3 = (bf16[128,896]{1,0:T(8,128)(2,1)S(1)}, bf16[128,896]{1,0:T(8,128)(2,1)S(1)}, u32[]{:S(2)}, u32[]{:S(2)}) collective-permute-start(bf16[128,896]{1,0:T(8,128)(2,1)S(1)} %get-tuple-element.34), channel_id=1, source_target_pairs={{0,192},{64,0},{128,64},{192,128},{1,193},{65,1},{129,65},{193,129... | collective-permute-start | bytes 688136 | tf_op jit(solution)/shard_map/rows_to_owners/ppermute | solution.py:34
  13.0 13.1 %collective-permute-start.4 = (bf16[128,896]{1,0:T(8,128)(2,1)S(1)}, bf16[128,896]{1,0:T(8,128)(2,1)S(1)}, u32[]{:S(2)}, u32[]{:S(2)}) collective-permute-start(bf16[128,896]{1,0:T(8,128)(2,1)S(1)} %get-tuple-element.33.own_part), channel_id=1, source_target_pairs={{0,128},{64,192},{128,0},{192,64},{1,129},{65,193},{129,1},{193,65... | collective-permute-start | bytes 688136 | tf_op jit(solution)/shard_map/rows_to_owners/ppermute | solution.py:34
  14.5 8.8 %collective-permute-start = (bf16[64,768]{1,0:T(8,128)(2,1)S(1)}, bf16[64,768]{1,0:T(8,128)(2,1)S(1)}, u32[]{:S(2)}, u32[]{:S(2)}) collective-permute-start(bf16[64,768]{1,0:T(8,128)(2,1)S(1)} %get-tuple-element.31), channel_id=1, source_target_pairs={{0,8},{8,16},{16,24},{24,32},{32,40},{40,48},{48,56},{56,64},{64,7... | collective-permute-start | bytes 294920 | tf_op jit(solution)/shard_map/rows_to_owners/ppermute | solution.py:144
  16.2 7.2 %collective-permute-start.1 = (bf16[64,768]{1,0:T(8,128)(2,1)S(1)}, bf16[64,768]{1,0:T(8,128)(2,1)S(1)}, u32[]{:S(2)}, u32[]{:S(2)}) collective-permute-start(bf16[64,768]{1,0:T(8,128)(2,1)S(1)} %get-tuple-element.32), channel_id=1, source_target_pairs={{0,248},{8,0},{16,8},{24,16},{32,24},{40,32},{48,40},{56,48},{64,5... | collective-permute-start | bytes 294920 | tf_op jit(solution)/shard_map/rows_to_owners/ppermute | solution.py:145
  27.6 5.9 %collective-permute-start.5 = (bf16[256,256]{1,0:T(8,128)(2,1)S(1)}, bf16[256,256]{1,0:T(8,128)(2,1)S(1)}, u32[]{:S(2)}, u32[]{:S(2)}) collective-permute-start(bf16[256,256]{1,0:T(8,128)(2,1)S(1)} %get-tuple-element.36), channel_id=1, source_target_pairs={{0,8},{8,16},{16,24},{24,32},{32,40},{40,48},{48,56},{56,0},{1,9},... | collective-permute-start | bytes 393224 | tf_op jit(solution)/shard_map/keys_and_values/ppermute | solution.py:34
  27.7 5.8 %collective-permute-start.7 = (bf16[256,256]{1,0:T(8,128)(2,1)S(1)}, bf16[256,256]{1,0:T(8,128)(2,1)S(1)}, u32[]{:S(2)}, u32[]{:S(2)}) collective-permute-start(bf16[256,256]{1,0:T(8,128)(2,1)S(1)} %get-tuple-element.36), channel_id=1, source_target_pairs={{0,56},{8,0},{16,8},{24,16},{32,24},{40,32},{48,40},{56,48},{1,57}... | collective-permute-start | bytes 393224 | tf_op jit(solution)/shard_map/keys_and_values/ppermute | solution.py:34
  33.5 5.0 %collective-permute-start.6 = (bf16[256,256]{1,0:T(8,128)(2,1)S(1)}, bf16[256,256]{1,0:T(8,128)(2,1)S(1)}, u32[]{:S(2)}, u32[]{:S(2)}) collective-permute-start(bf16[256,256]{1,0:T(8,128)(2,1)S(1)} %collective-permute-done.5), channel_id=1, source_target_pairs={{0,8},{8,16},{16,24},{24,32},{32,40},{40,48},{48,56},{56,0},{1,9},... | collective-permute-start | bytes 393224 | tf_op jit(solution)/shard_map/keys_and_values/ppermute | solution.py:34
  33.5 5.1 %collective-permute-start.8 = (bf16[256,256]{1,0:T(8,128)(2,1)S(1)}, bf16[256,256]{1,0:T(8,128)(2,1)S(1)}, u32[]{:S(2)}, u32[]{:S(2)}) collective-permute-start(bf16[256,256]{1,0:T(8,128)(2,1)S(1)} %collective-permute-done.7), channel_id=1, source_target_pairs={{0,56},{8,0},{16,8},{24,16},{32,24},{40,32},{48,40},{56,48},{1,57}... | collective-permute-start | bytes 393224 | tf_op jit(solution)/shard_map/keys_and_values/ppermute | solution.py:34
  38.7 9.3 %collective-permute-start.13 = (bf16[256,256]{1,0:T(8,128)(2,1)S(1)}, bf16[256,256]{1,0:T(8,128)(2,1)S(1)}, u32[]{:S(2)}, u32[]{:S(2)}) collective-permute-start(bf16[256,256]{1,0:T(8,128)(2,1)S(1)} %collective-permute-done.8), channel_id=1, source_target_pairs={{0,56},{8,0},{16,8},{24,16},{32,24},{40,32},{48,40},{56,48},{1,57}... | collective-permute-start | bytes 393224 | tf_op jit(solution)/shard_map/keys_and_values/ppermute | solution.py:34
  41.4 8.9 %collective-permute-start.14 = (bf16[256,256]{1,0:T(8,128)(2,1)S(1)}, bf16[256,256]{1,0:T(8,128)(2,1)S(1)}, u32[]{:S(2)}, u32[]{:S(2)}) collective-permute-start(bf16[256,256]{1,0:T(8,128)(2,1)S(1)} %collective-permute-done.6), channel_id=1, source_target_pairs={{0,16},{8,24},{16,32},{24,40},{32,48},{40,56},{48,0},{56,8},{1,17}... | collective-permute-start | bytes 393224 | tf_op jit(solution)/shard_map/keys_and_values/ppermute | solution.py:34
  41.4 12.5 %collective-permute-start.15 = (bf16[256,256]{1,0:T(8,128)(2,1)S(1)}, bf16[256,256]{1,0:T(8,128)(2,1)S(1)}, u32[]{:S(2)}, u32[]{:S(2)}) collective-permute-start(bf16[256,256]{1,0:T(8,128)(2,1)S(1)} %collective-permute-done.6), channel_id=1, source_target_pairs={{0,8},{8,16},{16,24},{24,32},{32,40},{40,48},{48,56},{56,0},{1,9},... | collective-permute-start | bytes 393224 | tf_op jit(solution)/shard_map/keys_and_values/ppermute | solution.py:34
  43.4 22.7 %collective-permute-start.17 = (bf16[1280,256]{1,0:T(8,128)(2,1)S(1)}, bf16[1280,256]{1,0:T(8,128)(2,1)S(1)}, u32[]{:S(2)}, u32[]{:S(2)}) collective-permute-start(bf16[1280,256]{1,0:T(8,128)(2,1)S(1)} %constant_dynamic-update-slice_fusion.refs_0_), channel_id=1, source_target_pairs={{0,64},{8,72},{16,80},{24,88},{32,96},{40,104},{48,112},{56,120},{... | collective-permute-start | bytes 1966088 | tf_op jit(solution)/shard_map/keys_and_values/ppermute | solution.py:43
  46.1 16.3 %collective-permute-start.11 = (bf16[768,256]{1,0:T(8,128)(2,1)S(1)}, bf16[768,256]{1,0:T(8,128)(2,1)S(1)}, u32[]{:S(2)}, u32[]{:S(2)}) collective-permute-start(bf16[768,256]{1,0:T(8,128)(2,1)S(1)} %slice.7), channel_id=1, source_target_pairs={{64,0},{72,8},{80,16},{88,24},{96,32},{104,40},{112,48},{120,56},{... | collective-permute-start | bytes 1179656 | tf_op jit(solution)/shard_map/keys_and_values/ppermute | solution.py:43
  53.9 12.1 %collective-permute-start.16 = (bf16[768,256]{1,0:T(8,128)(2,1)S(1)}, bf16[768,256]{1,0:T(8,128)(2,1)S(1)}, u32[]{:S(2)}, u32[]{:S(2)}) collective-permute-start(bf16[768,256]{1,0:T(8,128)(2,1)S(1)} %constant_dynamic-update-slice_fusion.5.refs_1_), channel_id=1, source_target_pairs={{0,64},{8,72},{16,80},{24,88},{32,96},{40,104},{48,112},{56,120},{... | collective-permute-start | bytes 1179656 | tf_op jit(solution)/shard_map/keys_and_values/ppermute | solution.py:43
  58.8 7.9 %collective-permute-start.9 = (bf16[512,256]{1,0:T(8,128)(2,1)S(1)}, bf16[512,256]{1,0:T(8,128)(2,1)S(1)}, u32[]{:S(2)}, u32[]{:S(2)}) collective-permute-start(bf16[512,256]{1,0:T(8,128)(2,1)S(1)} %slice.6), channel_id=1, source_target_pairs={{64,0},{72,8},{0,192},{8,200},{65,1},{73,9},{1,193},{9,201},{66,2}... | collective-permute-start | bytes 786440 | tf_op jit(solution)/shard_map/keys_and_values/ppermute | solution.py:43
  62.4 16.0 %collective-permute-start.12 = (bf16[768,256]{1,0:T(8,128)(2,1)S(1)}, bf16[768,256]{1,0:T(8,128)(2,1)S(1)}, u32[]{:S(2)}, u32[]{:S(2)}) collective-permute-start(bf16[768,256]{1,0:T(8,128)(2,1)S(1)} %collective-permute-done.11), channel_id=1, source_target_pairs={{192,128},{200,136},{208,144},{216,152},{224,160},{232,168},{240,1... | collective-permute-start | bytes 1179656 | tf_op jit(solution)/shard_map/keys_and_values/ppermute | solution.py:43
  66.0 12.3 %collective-permute-start.18 = (bf16[768,256]{1,0:T(8,128)(2,1)S(1)}, bf16[768,256]{1,0:T(8,128)(2,1)S(1)}, u32[]{:S(2)}, u32[]{:S(2)}) collective-permute-start(bf16[768,256]{1,0:T(8,128)(2,1)S(1)} %collective-permute-done.16.refs_1_), channel_id=1, source_target_pairs={{64,128},{72,136},{80,144},{88,152},{96,160},{128,192},{136,200},{... | collective-permute-start | bytes 1179656 | tf_op jit(solution)/shard_map/keys_and_values/ppermute | solution.py:43
  66.7 11.6 %collective-permute-start.10 = (bf16[512,256]{1,0:T(8,128)(2,1)S(1)}, bf16[512,256]{1,0:T(8,128)(2,1)S(1)}, u32[]{:S(2)}, u32[]{:S(2)}) collective-permute-start(bf16[512,256]{1,0:T(8,128)(2,1)S(1)} %collective-permute-done.9), channel_id=1, source_target_pairs={{192,128},{200,136},{0,192},{8,200},{193,129},{201,137},{1,193},{9... | collective-permute-start | bytes 786440 | tf_op jit(solution)/shard_map/keys_and_values/ppermute | solution.py:43
  79.2 36.4 %copy-start = (f32[4096]{0:T(1024)S(1)}, f32[4096]{0:T(1024)}, u32[]{:S(2)}) copy-start(f32[4096]{0:T(1024)} %param.12) | copy-start | bytes 49156
  79.2 22.8 %collective-permute-start.19 = (bf16[256,512]{1,0:T(8,128)(2,1)S(1)}, bf16[256,512]{1,0:T(8,128)(2,1)S(1)}, u32[]{:S(2)}, u32[]{:S(2)}) collective-permute-start(bf16[256,512]{1,0:T(8,128)(2,1)S(1)} %attention.3), channel_id=1, source_target_pairs={{0,64},{2,66},{4,68},{6,70},{64,0},{66,2},{68,4},{70,6},{1,65},{3,... | collective-permute-start | bytes 786440 | tf_op jit(solution)/shard_map/features/ppermute | solution.py:49
  79.3 26.1 %collective-permute-start.20 = (bf16[256,512]{1,0:T(8,128)(2,1)S(1)}, bf16[256,512]{1,0:T(8,128)(2,1)S(1)}, u32[]{:S(2)}, u32[]{:S(2)}) collective-permute-start(bf16[256,512]{1,0:T(8,128)(2,1)S(1)} %attention.3), channel_id=1, source_target_pairs={{0,66},{2,68},{4,70},{6,64},{64,2},{66,4},{68,6},{70,0},{1,67},{3,... | collective-permute-start | bytes 786440 | tf_op jit(solution)/shard_map/features/ppermute | solution.py:49
  81.7 23.9 %collective-permute-start.21 = (bf16[256,512]{1,0:T(8,128)(2,1)S(1)}, bf16[256,512]{1,0:T(8,128)(2,1)S(1)}, u32[]{:S(2)}, u32[]{:S(2)}) collective-permute-start(bf16[256,512]{1,0:T(8,128)(2,1)S(1)} %attention.3), channel_id=1, source_target_pairs={{0,70},{2,64},{4,66},{6,68},{64,6},{66,0},{68,2},{70,4},{1,71},{3,... | collective-permute-start | bytes 786440 | tf_op jit(solution)/shard_map/features/ppermute | solution.py:49
  83.0 22.6 %collective-permute-start.22 = (bf16[256,512]{1,0:T(8,128)(2,1)S(1)}, bf16[256,512]{1,0:T(8,128)(2,1)S(1)}, u32[]{:S(2)}, u32[]{:S(2)}) collective-permute-start(bf16[256,512]{1,0:T(8,128)(2,1)S(1)} %attention.3), channel_id=1, source_target_pairs={{0,68},{2,70},{4,64},{6,66},{64,4},{66,6},{68,0},{70,2},{1,69},{3,... | collective-permute-start | bytes 786440 | tf_op jit(solution)/shard_map/features/ppermute | solution.py:49
  85.6 22.4 %collective-permute-start.26 = (bf16[256,512]{1,0:T(8,128)(2,1)S(1)}, bf16[256,512]{1,0:T(8,128)(2,1)S(1)}, u32[]{:S(2)}, u32[]{:S(2)}) collective-permute-start(bf16[256,512]{1,0:T(8,128)(2,1)S(1)} %attention.3), channel_id=1, source_target_pairs={{0,4},{2,6},{4,0},{6,2},{1,5},{3,7},{5,1},{7,3},{8,12},{10,14},{12... | collective-permute-start | bytes 786440 | tf_op jit(solution)/shard_map/features/ppermute | solution.py:34
  102.1 7.0 %collective-permute-start.25 = (bf16[256,512]{1,0:T(8,128)(2,1)S(1)}, bf16[256,512]{1,0:T(8,128)(2,1)S(1)}, u32[]{:S(2)}, u32[]{:S(2)}) collective-permute-start(bf16[256,512]{1,0:T(8,128)(2,1)S(1)} %attention.3), channel_id=1, source_target_pairs={{0,6},{2,0},{4,2},{6,4},{1,7},{3,1},{5,3},{7,5},{8,14},{10,8},{12,... | collective-permute-start | bytes 786440 | tf_op jit(solution)/shard_map/features/ppermute | solution.py:34
  105.5 7.0 %collective-permute-start.24 = (bf16[256,512]{1,0:T(8,128)(2,1)S(1)}, bf16[256,512]{1,0:T(8,128)(2,1)S(1)}, u32[]{:S(2)}, u32[]{:S(2)}) collective-permute-start(bf16[256,512]{1,0:T(8,128)(2,1)S(1)} %attention.3), channel_id=1, source_target_pairs={{0,2},{2,4},{4,6},{6,0},{1,3},{3,5},{5,7},{7,1},{8,10},{10,12},{12... | collective-permute-start | bytes 786440 | tf_op jit(solution)/shard_map/features/ppermute | solution.py:34
  105.7 10.0 %collective-permute-start.23 = (bf16[1024,512]{1,0:T(8,128)(2,1)S(1)}, bf16[1024,512]{1,0:T(8,128)(2,1)S(1)}, u32[]{:S(2)}, u32[]{:S(2)}) collective-permute-start(bf16[1024,512]{1,0:T(8,128)(2,1)S(1)} %constant_dynamic-update-slice_fusion.8.mine), channel_id=1, source_target_pairs={{0,1},{1,0},{2,3},{3,2},{4,5},{5,4},{6,7},{7,6},{8,9},{9,8},{10,11... | collective-permute-start | bytes 3145736 | tf_op jit(solution)/shard_map/features/ppermute | solution.py:34
  112.5 16.4 %collective-permute-start.27 = (bf16[1024,512]{1,0:T(8,128)(2,1)S(1)}, bf16[1024,512]{1,0:T(8,128)(2,1)}, u32[]{:S(2)}, u32[]{:S(2)}) collective-permute-start(bf16[1024,512]{1,0:T(8,128)(2,1)S(1)} %pad_maximum_fusion.mine), channel_id=1, source_target_pairs={{0,1},{1,0},{2,3},{3,2},{4,5},{5,4},{6,7},{7,6},{8,9},{9,8},{10,11... | collective-permute-start | bytes 3145736 | tf_op jit(solution)/shard_map/features/ppermute | solution.py:34
  124.4 11.7 %collective-permute-start.28 = (bf16[256,512]{1,0:T(8,128)(2,1)S(1)}, bf16[256,512]{1,0:T(8,128)(2,1)S(1)}, u32[]{:S(2)}, u32[]{:S(2)}) collective-permute-start(bf16[256,512]{1,0:T(8,128)(2,1)S(1)} %gate.5), channel_id=1, source_target_pairs={{0,64},{64,0},{1,65},{65,1},{2,66},{66,2},{3,67},{67,3},{4,68},{68... | collective-permute-start | bytes 786440 | tf_op jit(solution)/shard_map/gate/ppermute | solution.py:34
  128.7 7.4 %collective-permute-start.29 = (bf16[256,384]{1,0:T(8,128)(2,1)S(1)}, bf16[256,384]{1,0:T(8,128)(2,1)S(1)}, u32[]{:S(2)}, u32[]{:S(2)}) collective-permute-start(bf16[256,384]{1,0:T(8,128)(2,1)S(1)} %gate.6), channel_id=1, source_target_pairs={{0,64},{64,0},{1,65},{65,1},{2,66},{66,2},{3,67},{67,3},{4,68},{68... | collective-permute-start | bytes 589832 | tf_op jit(solution)/shard_map/gate/ppermute | solution.py:34
  (2 other events, 34.0 us)
Sparse Core Ops, SparseCore 0:
  27.8 93.8 all-gather.1

commit v3 on v2

--- a/solution.py
+++ b/solution.py
@@ -136,7 +136,7 @@
         out_specs=(VMEM,) * 5,
         scratch_shapes=[pltpu.SemaphoreType.DMA((5,))],
         compiler_params=limit(16),
-    )(starts, *(in_hbm(a) for a in (q, k, v, weight)))
+    )(*(in_hbm(a) for a in (starts, q, k, v, weight)))
 
 
 def align(starts, own, up, down, parts):
@@ -151,7 +151,7 @@
         out_specs=(VMEM, VMEM, HBM),
         scratch_shapes=[pltpu.SemaphoreType.DMA((4,))],
         compiler_params=limit(16),
-    )(starts, own, low, high, *parts)
+    )(in_hbm(starts), own, low, high, *parts)
 
 
 def attention_kernel(back, parts, place, lengths, q_ref, *refs):
@@ -291,18 +291,23 @@
     )(gain, mine, other)
 
 
-def gate_kernel(first, rows, inv, weight, out, held, total, sems):
+def silu(value):
+    return (value / (1.0 + jnp.exp(-value))).astype(jnp.bfloat16)
+
+
+def first_gate_kernel(rows, inv, weight, out, held, total, sems):
     depth = FEATURES // PARTS
+    sent = out.shape[1]
     parts = [pl.ds(i * depth, depth) for i in range(PARTS)]
-    columns = pl.ds(first, out.shape[1])
-    copies = [pltpu.make_async_copy(weight.at[p, columns], held.at[p], sems.at[i]) for i, p in enumerate(parts)]
+    spots = [(p, c) for c in (pl.ds(0, sent), pl.ds(sent, held.shape[1] - sent)) for p in parts]
+    copies = [pltpu.make_async_copy(weight.at[s], held.at[s], sems.at[i]) for i, s in enumerate(spots)]
     for copy in copies:
         copy.start()
-    for i, copy in enumerate(copies):
-        copy.wait()
+    for i in range(PARTS):
+        copies[i].wait()
         term = jnp.dot(
             rows[:, i * depth : (i + 1) * depth],
-            held[i * depth : (i + 1) * depth],
+            held[i * depth : (i + 1) * depth, :sent],
             preferred_element_type=jnp.float32,
         )
         if i == 0:
@@ -310,26 +315,40 @@
         elif i < PARTS - 1:
             total[...] += term
         else:
-            value = (total[...] + term) * inv[:, :1]
-            out[...] = (value / (1.0 + jnp.exp(-value))).astype(jnp.bfloat16)
+            out[...] = silu((total[...] + term) * inv[:, :1])
+    for copy in copies[PARTS:]:
+        copy.wait()
+
+
+def first_gate(rows, inv, weight):
+    return pl.pallas_call(
+        first_gate_kernel,
+        out_shape=(bf16(TOK, SENT_FIRST), bf16(*weight.shape)),
+        in_specs=[VMEM] * 2 + [HBM],
+        out_specs=(VMEM,) * 2,
+        scratch_shapes=[pltpu.VMEM((TOK, SENT_FIRST), jnp.float32), pltpu.SemaphoreType.DMA((2 * PARTS,))],
+        compiler_params=limit(20),
+    )(rows, inv, in_hbm(weight))
+
+
+def gate_kernel(first, rows, inv, weight, out):
+    for at in range(0, out.shape[1], 2 * HD):
+        end = min(at + 2 * HD, out.shape[1])
+        value = jnp.dot(rows[...], weight[:, first + at : first + end], preferred_element_type=jnp.float32)
+        out[:, at:end] = silu(value * inv[:, :1])
 
 
 def gate(rows, inv, weight, first, columns):
     return pl.pallas_call(
         functools.partial(gate_kernel, first),
         out_shape=bf16(TOK, columns),
-        in_specs=[VMEM] * 2 + [HBM],
+        in_specs=[VMEM] * 3,
         out_specs=VMEM,
-        scratch_shapes=[
-            pltpu.VMEM((FEATURES, columns), weight.dtype),
-            pltpu.VMEM((TOK, columns), jnp.float32),
-            pltpu.SemaphoreType.DMA((PARTS,)),
-        ],
-        compiler_params=limit(28),
+        compiler_params=limit(20),
         cost_estimate=pl.CostEstimate(
             flops=2 * TOK * FEATURES * columns, bytes_accessed=2 * FEATURES * columns, transcendentals=TOK * columns
         ),
-    )(rows, inv, in_hbm(weight))
+    )(rows, inv, weight)
 
 
 def join_kernel(*refs):
@@ -356,7 +375,8 @@
 def on_device(queries, keys, values, doc_lengths, shard_starts, norm_gain, ffn_weight):
     with jax.named_scope("rows_to_owners"):
         own, up, down, theirs, mine = opening(shard_starts, queries, keys, values, ffn_weight)
-        parts = [mine, shift(theirs, TALL, 1), shift(theirs, TALL, -1), shift(mine, TALL, 2)]
+        far_part = shift(mine, TALL, 2)
+        parts = [mine, shift(theirs, TALL, 1), shift(theirs, TALL, -1), far_part]
         q, kv, pair = align(shard_starts, own, up, down, parts)
 
     with jax.named_scope("weight_rows"):
@@ -386,13 +406,13 @@
         other = shift(own, "c", 1)
 
     with jax.named_scope("gate"):
-        away = gate(their_rows, their_inv, weight, 0, SENT_FIRST)
+        away, held = first_gate(their_rows, their_inv, weight)
         back = [shift(away, "yb", 1)]
         their_inv, away = lax.optimization_barrier((their_inv, away))
-        rest = gate(their_rows, their_inv, weight, SENT_FIRST, half - SENT_FIRST)
+        rest = gate(their_rows, their_inv, held, SENT_FIRST, half - SENT_FIRST)
         back.append(shift(rest, "yb", 1))
         gain, rest = lax.optimization_barrier((gain, rest))
-        home = gate(*prepare(gain, own, other), weight, 0, half)
+        home = gate(*prepare(gain, own, other), held, 0, half)
         return join(home, *back)
 
 

time: 145 us -> 145 us (level)
  waiting for transfers between devices: 48.5 us -> 52 us
  Pallas kernels: 21 us -> 18.1 us
    pallas_call x3 -> x2, Pallas kernels: 10.1 us -> 3.77 us  [gate(): pl.pallas_call(functools.partial(gate_kernel, first), out_shape=bf16(TOK,...]
    ppermute x17, waiting for transfers between devices: 18.1 us -> 21.6 us  [shift(): lax.ppermute(block, axis, [(i, (i + distance) % count) for i in range(cou...]
    pallas_call x0 -> x1, Pallas kernels: none -> 3.18 us  [first_gate(): pl.pallas_call(first_gate_kernel, out_shape=(bf16(TOK, SENT_FIRST), bf16(...]
  transfers between devices with their start and end apart: 31 -> 31, of which waited for: 13 -> 13; matrix products, arithmetic and copies ran while one was open for 0% -> 0% of each run, Pallas kernels for 11% -> 9%
where the time goes in v3:
time: 145 us; the launch traced here: 144 us
  starting transfers between devices  59.8 us (41%)
  waiting for transfers between devices  52 us (36%)
  Pallas kernels  18.1 us (12%)
  between operations  13.7 us (9%)
    ppermute x17, starting transfers between devices, shift(): lax.ppermute(block, axis, [(i, (i + distance) % count) for i in range(cou...  28.3 us
    ppermute x17, waiting for transfers between devices, shift(): lax.ppermute(block, axis, [(i, (i + distance) % count) for i in range(cou...  21.6 us
    ppermute x7, starting transfers between devices, hop(): lax.ppermute(block, ROWS, [(a * NZ + z, b * NZ + z) for a, b in route for...  19.1 us
    ppermute x4, waiting for transfers between devices, shift_both(): lax.ppermute(block, ('yb', 'x'), [(b * NX + i, to(b, i)) for b, i in pairs])  15 us
    ppermute x7, waiting for transfers between devices, hop(): lax.ppermute(block, ROWS, [(a * NZ + z, b * NZ + z) for a, b in route for...  7.69 us
    ppermute x4, starting transfers between devices, shift_both(): lax.ppermute(block, ('yb', 'x'), [(b * NX + i, to(b, i)) for b, i in pairs])  6.41 us
    all_gather x1, waiting for transfers between devices, on_device(): weight = lax.all_gather(pair, 'z', axis=0, tiled=True)  4.92 us
    ppermute x1, starting transfers between devices, align(): lax.ppermute(down, ROWS, [(i, (i - 1) % count) for i in range(count)])  4.43 us
  transfers between devices with their start and end apart: 31, of which 13 were waited for; matrix products, arithmetic and copies ran while one was open for 0% of the time, Pallas kernels for 9%

profile of v3, /device:TPU:1, one launch (start us, length us, event | category | flops | bytes accessed | tf_op | source)
XLA Modules:
  0.0 144.0 jit_solution(6800950656333346552)
XLA Ops:
  6.5 2.2 %rows_to_owners.2 = (bf16[384,768]{1,0:T(8,128)(2,1)S(1)}, bf16[64,768]{1,0:T(8,128)(2,1)S(1)}, bf16[64,768]{1,0:T(8,128)(2,1)S(1)}, bf16[128,896]{1,0:T(8,128)(2,1)S(1)}, bf16[128,896]{1,0:T(8,128)(2,1)S(1)}) custom-call(s32[32]{0:T(128)} %starts.3, bf16[384,512]{1,0:T(8,128)(2,1)} %q.1, bf16[384,128]{1,0:T(8,128)(2,1)} %k.1, bf16[384,128]{1,0:T(8,128)(2,1)} %v.1, ...), custom_call_target="tpu_custom_call" | custom-call | tf_op jit(solution)/shard_map/rows_to_owners/pallas_call | solution.py:132
  8.7 2.2 %collective-permute-start.2 = (bf16[128,896]{1,0:T(8,128)(2,1)S(1)}, bf16[128,896]{1,0:T(8,128)(2,1)S(1)}, u32[]{:S(2)}, u32[]{:S(2)}) collective-permute-start(bf16[128,896]{1,0:T(8,128)(2,1)S(1)} %get-tuple-element.36), channel_id=1, source_target_pairs={{0,64},{64,128},{128,192},{192,0},{1,65},{65,129},{129,193},{193,1... | collective-permute-start | bytes 688136 | tf_op jit(solution)/shard_map/rows_to_owners/ppermute | solution.py:34
  15.6 4.4 %collective-permute-start.1 = (bf16[64,768]{1,0:T(8,128)(2,1)S(1)}, bf16[64,768]{1,0:T(8,128)(2,1)S(1)}, u32[]{:S(2)}, u32[]{:S(2)}) collective-permute-start(bf16[64,768]{1,0:T(8,128)(2,1)S(1)} %get-tuple-element.34), channel_id=1, source_target_pairs={{0,248},{8,0},{16,8},{24,16},{32,24},{40,32},{48,40},{56,48},{64,5... | collective-permute-start | bytes 294920 | tf_op jit(solution)/shard_map/rows_to_owners/ppermute | solution.py:145
  20.1 2.7 %collective-permute-done.low = bf16[64,768]{1,0:T(8,128)(2,1)S(1)} collective-permute-done((bf16[64,768]{1,0:T(8,128)(2,1)S(1)}, bf16[64,768]{1,0:T(8,128)(2,1)S(1)}, u32[]{:S(2)}, u32[]{:S(2)}) %collective-permute-start) | collective-permute-done | bytes 98336 | tf_op jit(solution)/shard_map/rows_to_owners/ppermute | solution.py:144
  22.8 2.7 %collective-permute-done.4.far_part = bf16[128,896]{1,0:T(8,128)(2,1)S(1)} collective-permute-done((bf16[128,896]{1,0:T(8,128)(2,1)S(1)}, bf16[128,896]{1,0:T(8,128)(2,1)S(1)}, u32[]{:S(2)}, u32[]{:S(2)}) %collective-permute-start.4) | collective-permute-done | bytes 229408 | tf_op jit(solution)/shard_map/rows_to_owners/ppermute | solution.py:34
  27.3 3.5 %collective-permute-start.7 = (bf16[256,256]{1,0:T(8,128)(2,1)S(1)}, bf16[256,256]{1,0:T(8,128)(2,1)S(1)}, u32[]{:S(2)}, u32[]{:S(2)}) collective-permute-start(bf16[256,256]{1,0:T(8,128)(2,1)S(1)} %get-tuple-element.38), channel_id=1, source_target_pairs={{0,56},{8,0},{16,8},{24,16},{32,24},{40,32},{48,40},{56,48},{1,57}... | collective-permute-start | bytes 393224 | tf_op jit(solution)/shard_map/keys_and_values/ppermute | solution.py:34
  30.9 2.3 %collective-permute-done.5 = bf16[256,256]{1,0:T(8,128)(2,1)S(1)} collective-permute-done((bf16[256,256]{1,0:T(8,128)(2,1)S(1)}, bf16[256,256]{1,0:T(8,128)(2,1)S(1)}, u32[]{:S(2)}, u32[]{:S(2)}) %collective-permute-start.5) | collective-permute-done | bytes 131104 | tf_op jit(solution)/shard_map/keys_and_values/ppermute | solution.py:34
  33.1 2.8 %collective-permute-start.8 = (bf16[256,256]{1,0:T(8,128)(2,1)S(1)}, bf16[256,256]{1,0:T(8,128)(2,1)S(1)}, u32[]{:S(2)}, u32[]{:S(2)}) collective-permute-start(bf16[256,256]{1,0:T(8,128)(2,1)S(1)} %collective-permute-done.7), channel_id=1, source_target_pairs={{0,56},{8,0},{16,8},{24,16},{32,24},{40,32},{48,40},{56,48},{1,57}... | collective-permute-start | bytes 393224 | tf_op jit(solution)/shard_map/keys_and_values/ppermute | solution.py:34
  35.9 2.3 %collective-permute-done.6 = bf16[256,256]{1,0:T(8,128)(2,1)S(1)} collective-permute-done((bf16[256,256]{1,0:T(8,128)(2,1)S(1)}, bf16[256,256]{1,0:T(8,128)(2,1)S(1)}, u32[]{:S(2)}, u32[]{:S(2)}) %collective-permute-start.6) | collective-permute-done | bytes 131104 | tf_op jit(solution)/shard_map/keys_and_values/ppermute | solution.py:34
  38.3 2.8 %collective-permute-start.13 = (bf16[256,256]{1,0:T(8,128)(2,1)S(1)}, bf16[256,256]{1,0:T(8,128)(2,1)S(1)}, u32[]{:S(2)}, u32[]{:S(2)}) collective-permute-start(bf16[256,256]{1,0:T(8,128)(2,1)S(1)} %collective-permute-done.8), channel_id=1, source_target_pairs={{0,56},{8,0},{16,8},{24,16},{32,24},{40,32},{48,40},{56,48},{1,57}... | collective-permute-start | bytes 393224 | tf_op jit(solution)/shard_map/keys_and_values/ppermute | solution.py:34
  41.0 1.9 %collective-permute-start.15 = (bf16[256,256]{1,0:T(8,128)(2,1)S(1)}, bf16[256,256]{1,0:T(8,128)(2,1)S(1)}, u32[]{:S(2)}, u32[]{:S(2)}) collective-permute-start(bf16[256,256]{1,0:T(8,128)(2,1)S(1)} %collective-permute-done.6), channel_id=1, source_target_pairs={{0,8},{8,16},{16,24},{24,32},{32,40},{40,48},{48,56},{56,0},{1,9},... | collective-permute-start | bytes 393224 | tf_op jit(solution)/shard_map/keys_and_values/ppermute | solution.py:34
  42.9 2.7 %collective-permute-start.17 = (bf16[1280,256]{1,0:T(8,128)(2,1)S(1)}, bf16[1280,256]{1,0:T(8,128)(2,1)S(1)}, u32[]{:S(2)}, u32[]{:S(2)}) collective-permute-start(bf16[1280,256]{1,0:T(8,128)(2,1)S(1)} %constant_dynamic-update-slice_fusion.refs_0_), channel_id=1, source_target_pairs={{0,64},{8,72},{16,80},{24,88},{32,96},{40,104},{48,112},{56,120},{... | collective-permute-start | bytes 1966088 | tf_op jit(solution)/shard_map/keys_and_values/ppermute | solution.py:43
  45.6 1.9 %collective-permute-start.11 = (bf16[768,256]{1,0:T(8,128)(2,1)S(1)}, bf16[768,256]{1,0:T(8,128)(2,1)S(1)}, u32[]{:S(2)}, u32[]{:S(2)}) collective-permute-start(bf16[768,256]{1,0:T(8,128)(2,1)S(1)} %slice.7), channel_id=1, source_target_pairs={{64,0},{72,8},{80,16},{88,24},{96,32},{104,40},{112,48},{120,56},{... | collective-permute-start | bytes 1179656 | tf_op jit(solution)/shard_map/keys_and_values/ppermute | solution.py:43
  47.6 2.3 %collective-permute-done.14 = bf16[256,256]{1,0:T(8,128)(2,1)S(1)} collective-permute-done((bf16[256,256]{1,0:T(8,128)(2,1)S(1)}, bf16[256,256]{1,0:T(8,128)(2,1)S(1)}, u32[]{:S(2)}, u32[]{:S(2)}) %collective-permute-start.14) | collective-permute-done | bytes 131104 | tf_op jit(solution)/shard_map/keys_and_values/ppermute | solution.py:34
  49.9 3.6 %collective-permute-done.15 = bf16[256,256]{1,0:T(8,128)(2,1)S(1)} collective-permute-done((bf16[256,256]{1,0:T(8,128)(2,1)S(1)}, bf16[256,256]{1,0:T(8,128)(2,1)S(1)}, u32[]{:S(2)}, u32[]{:S(2)}) %collective-permute-start.15) | collective-permute-done | bytes 131104 | tf_op jit(solution)/shard_map/keys_and_values/ppermute | solution.py:34
  53.5 4.9 %collective-permute-start.16 = (bf16[768,256]{1,0:T(8,128)(2,1)S(1)}, bf16[768,256]{1,0:T(8,128)(2,1)S(1)}, u32[]{:S(2)}, u32[]{:S(2)}) collective-permute-start(bf16[768,256]{1,0:T(8,128)(2,1)S(1)} %constant_dynamic-update-slice_fusion.5.refs_1_), channel_id=1, source_target_pairs={{0,64},{8,72},{16,80},{24,88},{32,96},{40,104},{48,112},{56,120},{... | collective-permute-start | bytes 1179656 | tf_op jit(solution)/shard_map/keys_and_values/ppermute | solution.py:43
  58.4 2.1 %collective-permute-start.9 = (bf16[512,256]{1,0:T(8,128)(2,1)S(1)}, bf16[512,256]{1,0:T(8,128)(2,1)S(1)}, u32[]{:S(2)}, u32[]{:S(2)}) collective-permute-start(bf16[512,256]{1,0:T(8,128)(2,1)S(1)} %slice.6), channel_id=1, source_target_pairs={{64,0},{72,8},{0,192},{8,200},{65,1},{73,9},{1,193},{9,201},{66,2}... | collective-permute-start | bytes 786440 | tf_op jit(solution)/shard_map/keys_and_values/ppermute | solution.py:43
  63.3 2.4 %collective-permute-done.16.refs_1_ = bf16[768,256]{1,0:T(8,128)(2,1)S(1)} collective-permute-done((bf16[768,256]{1,0:T(8,128)(2,1)S(1)}, bf16[768,256]{1,0:T(8,128)(2,1)S(1)}, u32[]{:S(2)}, u32[]{:S(2)}) %collective-permute-start.16) | collective-permute-done | bytes 393248 | tf_op jit(solution)/shard_map/keys_and_values/ppermute | solution.py:43
  66.3 5.5 %collective-permute-start.10 = (bf16[512,256]{1,0:T(8,128)(2,1)S(1)}, bf16[512,256]{1,0:T(8,128)(2,1)S(1)}, u32[]{:S(2)}, u32[]{:S(2)}) collective-permute-start(bf16[512,256]{1,0:T(8,128)(2,1)S(1)} %collective-permute-done.9), channel_id=1, source_target_pairs={{192,128},{200,136},{0,192},{8,200},{193,129},{201,137},{1,193},{9... | collective-permute-start | bytes 786440 | tf_op jit(solution)/shard_map/keys_and_values/ppermute | solution.py:43
  72.6 5.3 %collective-permute-done.10.refs_0_ = bf16[512,256]{1,0:T(8,128)(2,1)S(1)} collective-permute-done((bf16[512,256]{1,0:T(8,128)(2,1)S(1)}, bf16[512,256]{1,0:T(8,128)(2,1)S(1)}, u32[]{:S(2)}, u32[]{:S(2)}) %collective-permute-start.10) | collective-permute-done | bytes 262176 | tf_op jit(solution)/shard_map/keys_and_values/ppermute | solution.py:43
  78.9 2.4 %collective-permute-start.20 = (bf16[256,512]{1,0:T(8,128)(2,1)S(1)}, bf16[256,512]{1,0:T(8,128)(2,1)S(1)}, u32[]{:S(2)}, u32[]{:S(2)}) collective-permute-start(bf16[256,512]{1,0:T(8,128)(2,1)S(1)} %attention.3), channel_id=1, source_target_pairs={{0,66},{2,68},{4,70},{6,64},{64,2},{66,4},{68,6},{70,0},{1,67},{3,... | collective-permute-start | bytes 786440 | tf_op jit(solution)/shard_map/features/ppermute | solution.py:49
  82.6 2.6 %collective-permute-start.22 = (bf16[256,512]{1,0:T(8,128)(2,1)S(1)}, bf16[256,512]{1,0:T(8,128)(2,1)S(1)}, u32[]{:S(2)}, u32[]{:S(2)}) collective-permute-start(bf16[256,512]{1,0:T(8,128)(2,1)S(1)} %attention.3), channel_id=1, source_target_pairs={{0,68},{2,70},{4,64},{6,66},{64,4},{66,6},{68,0},{70,2},{1,69},{3,... | collective-permute-start | bytes 786440 | tf_op jit(solution)/shard_map/features/ppermute | solution.py:49
  86.6 15.0 %collective-permute-done.19 = bf16[256,512]{1,0:T(8,128)(2,1)S(1)} collective-permute-done((bf16[256,512]{1,0:T(8,128)(2,1)S(1)}, bf16[256,512]{1,0:T(8,128)(2,1)S(1)}, u32[]{:S(2)}, u32[]{:S(2)}) %collective-permute-start.19) | collective-permute-done | bytes 262176 | tf_op jit(solution)/shard_map/features/ppermute | solution.py:49
  101.6 3.4 %collective-permute-start.25 = (bf16[256,512]{1,0:T(8,128)(2,1)S(1)}, bf16[256,512]{1,0:T(8,128)(2,1)S(1)}, u32[]{:S(2)}, u32[]{:S(2)}) collective-permute-start(bf16[256,512]{1,0:T(8,128)(2,1)S(1)} %attention.3), channel_id=1, source_target_pairs={{0,6},{2,0},{4,2},{6,4},{1,7},{3,1},{5,3},{7,5},{8,14},{10,8},{12,... | collective-permute-start | bytes 786440 | tf_op jit(solution)/shard_map/features/ppermute | solution.py:34
  105.3 2.3 %collective-permute-start.23 = (bf16[1024,512]{1,0:T(8,128)(2,1)S(1)}, bf16[1024,512]{1,0:T(8,128)(2,1)S(1)}, u32[]{:S(2)}, u32[]{:S(2)}) collective-permute-start(bf16[1024,512]{1,0:T(8,128)(2,1)S(1)} %constant_dynamic-update-slice_fusion.8.mine), channel_id=1, source_target_pairs={{0,1},{1,0},{2,3},{3,2},{4,5},{5,4},{6,7},{7,6},{8,9},{9,8},{10,11... | collective-permute-start | bytes 3145736 | tf_op jit(solution)/shard_map/features/ppermute | solution.py:34
  108.7 3.3 %collective-permute-done.24 = bf16[256,512]{1,0:T(8,128)(2,1)S(1)} collective-permute-done((bf16[256,512]{1,0:T(8,128)(2,1)S(1)}, bf16[256,512]{1,0:T(8,128)(2,1)S(1)}, u32[]{:S(2)}, u32[]{:S(2)}) %collective-permute-start.24) | collective-permute-done | bytes 262176 | tf_op jit(solution)/shard_map/features/ppermute | solution.py:34
  112.1 3.1 %collective-permute-start.27 = (bf16[1024,512]{1,0:T(8,128)(2,1)S(1)}, bf16[1024,512]{1,0:T(8,128)(2,1)}, u32[]{:S(2)}, u32[]{:S(2)}) collective-permute-start(bf16[1024,512]{1,0:T(8,128)(2,1)S(1)} %pad_maximum_fusion.mine), channel_id=1, source_target_pairs={{0,1},{1,0},{2,3},{3,2},{4,5},{5,4},{6,7},{7,6},{8,9},{9,8},{10,11... | collective-permute-start | bytes 3145736 | tf_op jit(solution)/shard_map/features/ppermute | solution.py:34
  116.3 4.9 %all-gather.2.cloned.1.call-done.weight = bf16[4096,896]{1,0:T(8,128)(2,1)} async-done(((bf16[512,896]{1,0:T(8,128)(2,1)}), bf16[4096,896]{1,0:T(8,128)(2,1)}) %all-gather.2.cloned.1.call-update) | async-done | bytes 7340048 | tf_op jit(solution)/shard_map/weight_rows/all_gather | solution.py:383
  121.2 3.2 %gate.5 = (bf16[256,512]{1,0:T(8,128)(2,1)S(1)}, bf16[4096,896]{1,0:T(8,128)(2,1)S(1)}) custom-call(bf16[256,4096]{1,0:T(8,128)(2,1)S(1)} %get-tuple-element.50.rows, f32[256,128]{1,0:T(8,128)S(1)} %get-tuple-element.54.inv, bf16[4096,896]{1,0:T(8,128)(2,1)} %all-gather.2.cloned.1.call-done.weight), custom_call_target="tpu_custom_call" | custom-call | tf_op jit(solution)/shard_map/gate/pallas_call | solution.py:324
  127.4 2.3 %gate.7 = (bf16[256,4096]{1,0:T(8,128)(2,1)S(1)}, f32[256,128]{1,0:T(8,128)S(1)}) custom-call(f32[1,4096]{1,0:T(1,128)S(1)} %bitcast.2, bf16[1024,512]{1,0:T(8,128)(2,1)S(1)} %pad_maximum_fusion.mine, bf16[1024,512]{1,0:T(8,128)(2,1)} %collective-permute-done.27.other), custom_call_target="tpu_custom_call" | custom-call | tf_op jit(solution)/shard_map/gate/pallas_call | solution.py:285
  129.7 2.5 %gate.8.refs_0_ = bf16[256,896]{1,0:T(8,128)(2,1)S(1)} custom-call(bf16[256,4096]{1,0:T(8,128)(2,1)S(1)} %get-tuple-element.57.rows, f32[256,128]{1,0:T(8,128)S(1)} %get-tuple-element.58.inv, bf16[4096,896]{1,0:T(8,128)(2,1)S(1)} %get-tuple-element.55.weight), custom_call_target="tpu_custom_call" | custom-call | flops 1879048192 | bytes 7340032 | tf_op jit(solution)/shard_map/gate/pallas_call | solution.py:342
  132.1 4.0 %collective-permute-done.29.refs_2_ = bf16[256,384]{1,0:T(8,128)(2,1)S(1)} collective-permute-done((bf16[256,384]{1,0:T(8,128)(2,1)S(1)}, bf16[256,384]{1,0:T(8,128)(2,1)S(1)}, u32[]{:S(2)}, u32[]{:S(2)}) %collective-permute-start.29) | collective-permute-done | bytes 196640 | tf_op jit(solution)/shard_map/gate/ppermute | solution.py:34
  (61 shorter events, 20.8 us)
Async XLA Ops:
  6.5 114.7 %all-gather.2.cloned.1.call-start = ((), (), s32[]{:S(2)}) async-start(), calls=%async_computation | async-start | bytes 8257536 | tf_op jit(solution)/shard_map/weight_rows/all_gather | solution.py:383
  8.7 14.1 %collective-permute-start.2 = (bf16[128,896]{1,0:T(8,128)(2,1)S(1)}, bf16[128,896]{1,0:T(8,128)(2,1)S(1)}, u32[]{:S(2)}, u32[]{:S(2)}) collective-permute-start(bf16[128,896]{1,0:T(8,128)(2,1)S(1)} %get-tuple-element.36), channel_id=1, source_target_pairs={{0,64},{64,128},{128,192},{192,0},{1,65},{65,129},{129,193},{193,1... | collective-permute-start | bytes 688136 | tf_op jit(solution)/shard_map/rows_to_owners/ppermute | solution.py:34
  10.9 11.9 %collective-permute-start.3 = (bf16[128,896]{1,0:T(8,128)(2,1)S(1)}, bf16[128,896]{1,0:T(8,128)(2,1)S(1)}, u32[]{:S(2)}, u32[]{:S(2)}) collective-permute-start(bf16[128,896]{1,0:T(8,128)(2,1)S(1)} %get-tuple-element.36), channel_id=1, source_target_pairs={{0,192},{64,0},{128,64},{192,128},{1,193},{65,1},{129,65},{193,129... | collective-permute-start | bytes 688136 | tf_op jit(solution)/shard_map/rows_to_owners/ppermute | solution.py:34
  12.4 13.1 %collective-permute-start.4 = (bf16[128,896]{1,0:T(8,128)(2,1)S(1)}, bf16[128,896]{1,0:T(8,128)(2,1)S(1)}, u32[]{:S(2)}, u32[]{:S(2)}) collective-permute-start(bf16[128,896]{1,0:T(8,128)(2,1)S(1)} %get-tuple-element.35.own_part), channel_id=1, source_target_pairs={{0,128},{64,192},{128,0},{192,64},{1,129},{65,193},{129,1},{193,65... | collective-permute-start | bytes 688136 | tf_op jit(solution)/shard_map/rows_to_owners/ppermute | solution.py:34
  14.0 8.8 %collective-permute-start = (bf16[64,768]{1,0:T(8,128)(2,1)S(1)}, bf16[64,768]{1,0:T(8,128)(2,1)S(1)}, u32[]{:S(2)}, u32[]{:S(2)}) collective-permute-start(bf16[64,768]{1,0:T(8,128)(2,1)S(1)} %get-tuple-element.33), channel_id=1, source_target_pairs={{0,8},{8,16},{16,24},{24,32},{32,40},{40,48},{48,56},{56,64},{64,7... | collective-permute-start | bytes 294920 | tf_op jit(solution)/shard_map/rows_to_owners/ppermute | solution.py:144
  15.6 7.2 %collective-permute-start.1 = (bf16[64,768]{1,0:T(8,128)(2,1)S(1)}, bf16[64,768]{1,0:T(8,128)(2,1)S(1)}, u32[]{:S(2)}, u32[]{:S(2)}) collective-permute-start(bf16[64,768]{1,0:T(8,128)(2,1)S(1)} %get-tuple-element.34), channel_id=1, source_target_pairs={{0,248},{8,0},{16,8},{24,16},{32,24},{40,32},{48,40},{56,48},{64,5... | collective-permute-start | bytes 294920 | tf_op jit(solution)/shard_map/rows_to_owners/ppermute | solution.py:145
  27.2 5.9 %collective-permute-start.5 = (bf16[256,256]{1,0:T(8,128)(2,1)S(1)}, bf16[256,256]{1,0:T(8,128)(2,1)S(1)}, u32[]{:S(2)}, u32[]{:S(2)}) collective-permute-start(bf16[256,256]{1,0:T(8,128)(2,1)S(1)} %get-tuple-element.38), channel_id=1, source_target_pairs={{0,8},{8,16},{16,24},{24,32},{32,40},{40,48},{48,56},{56,0},{1,9},... | collective-permute-start | bytes 393224 | tf_op jit(solution)/shard_map/keys_and_values/ppermute | solution.py:34
  27.3 5.8 %collective-permute-start.7 = (bf16[256,256]{1,0:T(8,128)(2,1)S(1)}, bf16[256,256]{1,0:T(8,128)(2,1)S(1)}, u32[]{:S(2)}, u32[]{:S(2)}) collective-permute-start(bf16[256,256]{1,0:T(8,128)(2,1)S(1)} %get-tuple-element.38), channel_id=1, source_target_pairs={{0,56},{8,0},{16,8},{24,16},{32,24},{40,32},{48,40},{56,48},{1,57}... | collective-permute-start | bytes 393224 | tf_op jit(solution)/shard_map/keys_and_values/ppermute | solution.py:34
  33.1 5.0 %collective-permute-start.6 = (bf16[256,256]{1,0:T(8,128)(2,1)S(1)}, bf16[256,256]{1,0:T(8,128)(2,1)S(1)}, u32[]{:S(2)}, u32[]{:S(2)}) collective-permute-start(bf16[256,256]{1,0:T(8,128)(2,1)S(1)} %collective-permute-done.5), channel_id=1, source_target_pairs={{0,8},{8,16},{16,24},{24,32},{32,40},{40,48},{48,56},{56,0},{1,9},... | collective-permute-start | bytes 393224 | tf_op jit(solution)/shard_map/keys_and_values/ppermute | solution.py:34
  33.1 5.1 %collective-permute-start.8 = (bf16[256,256]{1,0:T(8,128)(2,1)S(1)}, bf16[256,256]{1,0:T(8,128)(2,1)S(1)}, u32[]{:S(2)}, u32[]{:S(2)}) collective-permute-start(bf16[256,256]{1,0:T(8,128)(2,1)S(1)} %collective-permute-done.7), channel_id=1, source_target_pairs={{0,56},{8,0},{16,8},{24,16},{32,24},{40,32},{48,40},{56,48},{1,57}... | collective-permute-start | bytes 393224 | tf_op jit(solution)/shard_map/keys_and_values/ppermute | solution.py:34
  38.3 9.3 %collective-permute-start.13 = (bf16[256,256]{1,0:T(8,128)(2,1)S(1)}, bf16[256,256]{1,0:T(8,128)(2,1)S(1)}, u32[]{:S(2)}, u32[]{:S(2)}) collective-permute-start(bf16[256,256]{1,0:T(8,128)(2,1)S(1)} %collective-permute-done.8), channel_id=1, source_target_pairs={{0,56},{8,0},{16,8},{24,16},{32,24},{40,32},{48,40},{56,48},{1,57}... | collective-permute-start | bytes 393224 | tf_op jit(solution)/shard_map/keys_and_values/ppermute | solution.py:34
  41.0 8.9 %collective-permute-start.14 = (bf16[256,256]{1,0:T(8,128)(2,1)S(1)}, bf16[256,256]{1,0:T(8,128)(2,1)S(1)}, u32[]{:S(2)}, u32[]{:S(2)}) collective-permute-start(bf16[256,256]{1,0:T(8,128)(2,1)S(1)} %collective-permute-done.6), channel_id=1, source_target_pairs={{0,16},{8,24},{16,32},{24,40},{32,48},{40,56},{48,0},{56,8},{1,17}... | collective-permute-start | bytes 393224 | tf_op jit(solution)/shard_map/keys_and_values/ppermute | solution.py:34
  41.0 12.5 %collective-permute-start.15 = (bf16[256,256]{1,0:T(8,128)(2,1)S(1)}, bf16[256,256]{1,0:T(8,128)(2,1)S(1)}, u32[]{:S(2)}, u32[]{:S(2)}) collective-permute-start(bf16[256,256]{1,0:T(8,128)(2,1)S(1)} %collective-permute-done.6), channel_id=1, source_target_pairs={{0,8},{8,16},{16,24},{24,32},{32,40},{40,48},{48,56},{56,0},{1,9},... | collective-permute-start | bytes 393224 | tf_op jit(solution)/shard_map/keys_and_values/ppermute | solution.py:34
  42.9 22.7 %collective-permute-start.17 = (bf16[1280,256]{1,0:T(8,128)(2,1)S(1)}, bf16[1280,256]{1,0:T(8,128)(2,1)S(1)}, u32[]{:S(2)}, u32[]{:S(2)}) collective-permute-start(bf16[1280,256]{1,0:T(8,128)(2,1)S(1)} %constant_dynamic-update-slice_fusion.refs_0_), channel_id=1, source_target_pairs={{0,64},{8,72},{16,80},{24,88},{32,96},{40,104},{48,112},{56,120},{... | collective-permute-start | bytes 1966088 | tf_op jit(solution)/shard_map/keys_and_values/ppermute | solution.py:43
  45.6 16.3 %collective-permute-start.11 = (bf16[768,256]{1,0:T(8,128)(2,1)S(1)}, bf16[768,256]{1,0:T(8,128)(2,1)S(1)}, u32[]{:S(2)}, u32[]{:S(2)}) collective-permute-start(bf16[768,256]{1,0:T(8,128)(2,1)S(1)} %slice.7), channel_id=1, source_target_pairs={{64,0},{72,8},{80,16},{88,24},{96,32},{104,40},{112,48},{120,56},{... | collective-permute-start | bytes 1179656 | tf_op jit(solution)/shard_map/keys_and_values/ppermute | solution.py:43
  53.5 12.1 %collective-permute-start.16 = (bf16[768,256]{1,0:T(8,128)(2,1)S(1)}, bf16[768,256]{1,0:T(8,128)(2,1)S(1)}, u32[]{:S(2)}, u32[]{:S(2)}) collective-permute-start(bf16[768,256]{1,0:T(8,128)(2,1)S(1)} %constant_dynamic-update-slice_fusion.5.refs_1_), channel_id=1, source_target_pairs={{0,64},{8,72},{16,80},{24,88},{32,96},{40,104},{48,112},{56,120},{... | collective-permute-start | bytes 1179656 | tf_op jit(solution)/shard_map/keys_and_values/ppermute | solution.py:43
  58.4 7.9 %collective-permute-start.9 = (bf16[512,256]{1,0:T(8,128)(2,1)S(1)}, bf16[512,256]{1,0:T(8,128)(2,1)S(1)}, u32[]{:S(2)}, u32[]{:S(2)}) collective-permute-start(bf16[512,256]{1,0:T(8,128)(2,1)S(1)} %slice.6), channel_id=1, source_target_pairs={{64,0},{72,8},{0,192},{8,200},{65,1},{73,9},{1,193},{9,201},{66,2}... | collective-permute-start | bytes 786440 | tf_op jit(solution)/shard_map/keys_and_values/ppermute | solution.py:43
  61.9 15.9 %collective-permute-start.12 = (bf16[768,256]{1,0:T(8,128)(2,1)S(1)}, bf16[768,256]{1,0:T(8,128)(2,1)S(1)}, u32[]{:S(2)}, u32[]{:S(2)}) collective-permute-start(bf16[768,256]{1,0:T(8,128)(2,1)S(1)} %collective-permute-done.11), channel_id=1, source_target_pairs={{192,128},{200,136},{208,144},{216,152},{224,160},{232,168},{240,1... | collective-permute-start | bytes 1179656 | tf_op jit(solution)/shard_map/keys_and_values/ppermute | solution.py:43
  65.6 12.3 %collective-permute-start.18 = (bf16[768,256]{1,0:T(8,128)(2,1)S(1)}, bf16[768,256]{1,0:T(8,128)(2,1)S(1)}, u32[]{:S(2)}, u32[]{:S(2)}) collective-permute-start(bf16[768,256]{1,0:T(8,128)(2,1)S(1)} %collective-permute-done.16.refs_1_), channel_id=1, source_target_pairs={{64,128},{72,136},{80,144},{88,152},{96,160},{128,192},{136,200},{... | collective-permute-start | bytes 1179656 | tf_op jit(solution)/shard_map/keys_and_values/ppermute | solution.py:43
  66.3 11.6 %collective-permute-start.10 = (bf16[512,256]{1,0:T(8,128)(2,1)S(1)}, bf16[512,256]{1,0:T(8,128)(2,1)S(1)}, u32[]{:S(2)}, u32[]{:S(2)}) collective-permute-start(bf16[512,256]{1,0:T(8,128)(2,1)S(1)} %collective-permute-done.9), channel_id=1, source_target_pairs={{192,128},{200,136},{0,192},{8,200},{193,129},{201,137},{1,193},{9... | collective-permute-start | bytes 786440 | tf_op jit(solution)/shard_map/keys_and_values/ppermute | solution.py:43
  78.8 36.5 %copy-start = (f32[4096]{0:T(1024)S(1)}, f32[4096]{0:T(1024)}, u32[]{:S(2)}) copy-start(f32[4096]{0:T(1024)} %param.12) | copy-start | bytes 49156
  78.8 22.8 %collective-permute-start.19 = (bf16[256,512]{1,0:T(8,128)(2,1)S(1)}, bf16[256,512]{1,0:T(8,128)(2,1)S(1)}, u32[]{:S(2)}, u32[]{:S(2)}) collective-permute-start(bf16[256,512]{1,0:T(8,128)(2,1)S(1)} %attention.3), channel_id=1, source_target_pairs={{0,64},{2,66},{4,68},{6,70},{64,0},{66,2},{68,4},{70,6},{1,65},{3,... | collective-permute-start | bytes 786440 | tf_op jit(solution)/shard_map/features/ppermute | solution.py:49
  78.9 26.2 %collective-permute-start.20 = (bf16[256,512]{1,0:T(8,128)(2,1)S(1)}, bf16[256,512]{1,0:T(8,128)(2,1)S(1)}, u32[]{:S(2)}, u32[]{:S(2)}) collective-permute-start(bf16[256,512]{1,0:T(8,128)(2,1)S(1)} %attention.3), channel_id=1, source_target_pairs={{0,66},{2,68},{4,70},{6,64},{64,2},{66,4},{68,6},{70,0},{1,67},{3,... | collective-permute-start | bytes 786440 | tf_op jit(solution)/shard_map/features/ppermute | solution.py:49
  81.3 23.9 %collective-permute-start.21 = (bf16[256,512]{1,0:T(8,128)(2,1)S(1)}, bf16[256,512]{1,0:T(8,128)(2,1)S(1)}, u32[]{:S(2)}, u32[]{:S(2)}) collective-permute-start(bf16[256,512]{1,0:T(8,128)(2,1)S(1)} %attention.3), channel_id=1, source_target_pairs={{0,70},{2,64},{4,66},{6,68},{64,6},{66,0},{68,2},{70,4},{1,71},{3,... | collective-permute-start | bytes 786440 | tf_op jit(solution)/shard_map/features/ppermute | solution.py:49
  82.6 22.6 %collective-permute-start.22 = (bf16[256,512]{1,0:T(8,128)(2,1)S(1)}, bf16[256,512]{1,0:T(8,128)(2,1)S(1)}, u32[]{:S(2)}, u32[]{:S(2)}) collective-permute-start(bf16[256,512]{1,0:T(8,128)(2,1)S(1)} %attention.3), channel_id=1, source_target_pairs={{0,68},{2,70},{4,64},{6,66},{64,4},{66,6},{68,0},{70,2},{1,69},{3,... | collective-permute-start | bytes 786440 | tf_op jit(solution)/shard_map/features/ppermute | solution.py:49
  85.2 22.4 %collective-permute-start.26 = (bf16[256,512]{1,0:T(8,128)(2,1)S(1)}, bf16[256,512]{1,0:T(8,128)(2,1)S(1)}, u32[]{:S(2)}, u32[]{:S(2)}) collective-permute-start(bf16[256,512]{1,0:T(8,128)(2,1)S(1)} %attention.3), channel_id=1, source_target_pairs={{0,4},{2,6},{4,0},{6,2},{1,5},{3,7},{5,1},{7,3},{8,12},{10,14},{12... | collective-permute-start | bytes 786440 | tf_op jit(solution)/shard_map/features/ppermute | solution.py:34
  101.6 7.1 %collective-permute-start.25 = (bf16[256,512]{1,0:T(8,128)(2,1)S(1)}, bf16[256,512]{1,0:T(8,128)(2,1)S(1)}, u32[]{:S(2)}, u32[]{:S(2)}) collective-permute-start(bf16[256,512]{1,0:T(8,128)(2,1)S(1)} %attention.3), channel_id=1, source_target_pairs={{0,6},{2,0},{4,2},{6,4},{1,7},{3,1},{5,3},{7,5},{8,14},{10,8},{12,... | collective-permute-start | bytes 786440 | tf_op jit(solution)/shard_map/features/ppermute | solution.py:34
  105.1 7.0 %collective-permute-start.24 = (bf16[256,512]{1,0:T(8,128)(2,1)S(1)}, bf16[256,512]{1,0:T(8,128)(2,1)S(1)}, u32[]{:S(2)}, u32[]{:S(2)}) collective-permute-start(bf16[256,512]{1,0:T(8,128)(2,1)S(1)} %attention.3), channel_id=1, source_target_pairs={{0,2},{2,4},{4,6},{6,0},{1,3},{3,5},{5,7},{7,1},{8,10},{10,12},{12... | collective-permute-start | bytes 786440 | tf_op jit(solution)/shard_map/features/ppermute | solution.py:34
  105.3 10.0 %collective-permute-start.23 = (bf16[1024,512]{1,0:T(8,128)(2,1)S(1)}, bf16[1024,512]{1,0:T(8,128)(2,1)S(1)}, u32[]{:S(2)}, u32[]{:S(2)}) collective-permute-start(bf16[1024,512]{1,0:T(8,128)(2,1)S(1)} %constant_dynamic-update-slice_fusion.8.mine), channel_id=1, source_target_pairs={{0,1},{1,0},{2,3},{3,2},{4,5},{5,4},{6,7},{7,6},{8,9},{9,8},{10,11... | collective-permute-start | bytes 3145736 | tf_op jit(solution)/shard_map/features/ppermute | solution.py:34
  112.1 15.2 %collective-permute-start.27 = (bf16[1024,512]{1,0:T(8,128)(2,1)S(1)}, bf16[1024,512]{1,0:T(8,128)(2,1)}, u32[]{:S(2)}, u32[]{:S(2)}) collective-permute-start(bf16[1024,512]{1,0:T(8,128)(2,1)S(1)} %pad_maximum_fusion.mine), channel_id=1, source_target_pairs={{0,1},{1,0},{2,3},{3,2},{4,5},{5,4},{6,7},{7,6},{8,9},{9,8},{10,11... | collective-permute-start | bytes 3145736 | tf_op jit(solution)/shard_map/features/ppermute | solution.py:34
  124.4 11.7 %collective-permute-start.28 = (bf16[256,512]{1,0:T(8,128)(2,1)S(1)}, bf16[256,512]{1,0:T(8,128)(2,1)S(1)}, u32[]{:S(2)}, u32[]{:S(2)}) collective-permute-start(bf16[256,512]{1,0:T(8,128)(2,1)S(1)} %get-tuple-element.53), channel_id=1, source_target_pairs={{0,64},{64,0},{1,65},{65,1},{2,66},{66,2},{3,67},{67,3},{4,68},{68... | collective-permute-start | bytes 786440 | tf_op jit(solution)/shard_map/gate/ppermute | solution.py:34
  127.1 9.0 %collective-permute-start.29 = (bf16[256,384]{1,0:T(8,128)(2,1)S(1)}, bf16[256,384]{1,0:T(8,128)(2,1)S(1)}, u32[]{:S(2)}, u32[]{:S(2)}) collective-permute-start(bf16[256,384]{1,0:T(8,128)(2,1)S(1)} %gate.6), channel_id=1, source_target_pairs={{0,64},{64,0},{1,65},{65,1},{2,66},{66,2},{3,67},{67,3},{4,68},{68... | collective-permute-start | bytes 589832 | tf_op jit(solution)/shard_map/gate/ppermute | solution.py:34
  (1 other events, 33.3 us)
Sparse Core Ops, SparseCore 0:
  27.3 93.8 all-gather.1

commit v4 on v3

--- a/solution.py
+++ b/solution.py
@@ -17,7 +17,7 @@
 HEADS_HERE = 4
 HERE = 2
 FAR = 5
-SENT_FIRST = 512
+SENT_FIRST = 640
 PARTS = 4
 NORM_EPS = 1e-05
 MASKED = -1e30
@@ -351,25 +351,53 @@
     )(rows, inv, weight)
 
 
-def join_kernel(*refs):
-    *parts, out = refs
-    half, odd = out.shape[1] // 2, lax.rem(here()[0], 2)
-    at = 0
-    for ref in parts:
-        side = odd if at < half else 1 - odd
-        place = side * half + at % half
-        out[:, pl.ds(pl.multiple_of(place, HD), ref.shape[1])] = ref[...]
-        at += ref.shape[1]
-
-
-def join(*parts):
+def home_kernel(rows, inv, weight, out):
+    half = weight.shape[1]
+    side = lax.rem(here()[0], 2) * half
+    for at in range(0, half, 2 * HD):
+        end = min(at + 2 * HD, half)
+        value = jnp.dot(rows[...], weight[:, at:end], preferred_element_type=jnp.float32)
+        out[:, pl.ds(pl.multiple_of(side + at, HD), end - at)] = silu(value * inv[:, :1])
+
+
+def home_gate(rows, inv, weight):
+    columns = weight.shape[1]
+    return pl.pallas_call(
+        home_kernel,
+        out_shape=bf16(TOK, 2 * columns),
+        in_specs=[VMEM] * 3,
+        out_specs=VMEM,
+        compiler_params=limit(20),
+        cost_estimate=pl.CostEstimate(
+            flops=2 * TOK * FEATURES * columns, bytes_accessed=2 * FEATURES * columns, transcendentals=TOK * columns
+        ),
+    )(rows, inv, weight)
+
+
+def join_kernel(first, rest, _, out, sems):
+    half = out.shape[1] // 2
+    at = (1 - lax.rem(here()[0], 2)) * half
+    copies = []
+    for i, part in enumerate((first, rest)):
+        place = out.at[:, pl.ds(pl.multiple_of(at, HD), part.shape[1])]
+        copies.append(pltpu.make_async_copy(part, place, sems.at[i]))
+        at += part.shape[1]
+    for copy in copies:
+        copy.start()
+    for copy in copies:
+        copy.wait()
+
+
+def join(out, first, rest):
     return pl.pallas_call(
         join_kernel,
-        out_shape=bf16(TOK, sum(part.shape[1] for part in parts)),
-        in_specs=[VMEM] * len(parts),
-        out_specs=VMEM,
+        out_shape=bf16(*out.shape),
+        in_specs=[VMEM] * 2 + [HBM],
+        out_specs=HBM,
+        scratch_shapes=[pltpu.SemaphoreType.DMA((2,))],
+        input_output_aliases={2: 0},
         compiler_params=limit(8),
-    )(*parts)
+    )(first, rest, out)
 
 
 def on_device(queries, keys, values, doc_lengths, shard_starts, norm_gain, ffn_weight):
@@ -412,8 +440,7 @@
         rest = gate(their_rows, their_inv, held, SENT_FIRST, half - SENT_FIRST)
         back.append(shift(rest, "yb", 1))
         gain, rest = lax.optimization_barrier((gain, rest))
-        home = gate(*prepare(gain, own, other), held, 0, half)
-        return join(home, *back)
+        return join(home_gate(*prepare(gain, own, other), held), *back)
 
 
 def solution(mesh):

time: 145 us -> 145 us (level)
    pallas_call x1 -> x2, Pallas kernels: 1 us -> 4.18 us  [the longest x1 3.4 us: home_gate(): pl.pallas_call(home_kernel, out_shape=bf16(TOK, 2 * columns), in_specs=[V...]
    pallas_call x2 -> x1, Pallas kernels: 3.77 us -> 0.73 us  [gate(): pl.pallas_call(functools.partial(gate_kernel, first), out_shape=bf16(TOK,...]
  transfers between devices with their start and end apart: 31 -> 31, of which waited for: 13 -> 13; matrix products, arithmetic and copies ran while one was open for 0% -> 0% of each run, Pallas kernels for 9% -> 10%
where the time goes in v4:
time: 145 us; the launch traced here: 144 us
  starting transfers between devices  59.9 us (41%)
  waiting for transfers between devices  51.6 us (36%)
  Pallas kernels  18.8 us (13%)
  between operations  13.8 us (10%)
    ppermute x17, starting transfers between devices, shift(): lax.ppermute(block, axis, [(i, (i + distance) % count) for i in range(cou...  28.3 us
    ppermute x17, waiting for transfers between devices, shift(): lax.ppermute(block, axis, [(i, (i + distance) % count) for i in range(cou...  21.3 us
    ppermute x7, starting transfers between devices, hop(): lax.ppermute(block, ROWS, [(a * NZ + z, b * NZ + z) for a, b in route for...  19.1 us
    ppermute x4, waiting for transfers between devices, shift_both(): lax.ppermute(block, ('yb', 'x'), [(b * NX + i, to(b, i)) for b, i in pairs])  15 us
    ppermute x7, waiting for transfers between devices, hop(): lax.ppermute(block, ROWS, [(a * NZ + z, b * NZ + z) for a, b in route for...  7.69 us
    ppermute x4, starting transfers between devices, shift_both(): lax.ppermute(block, ('yb', 'x'), [(b * NX + i, to(b, i)) for b, i in pairs])  6.41 us
    all_gather x1, waiting for transfers between devices, on_device(): weight = lax.all_gather(pair, 'z', axis=0, tiled=True)  4.92 us
    ppermute x1, starting transfers between devices, align(): lax.ppermute(down, ROWS, [(i, (i - 1) % count) for i in range(count)])  4.43 us
  transfers between devices with their start and end apart: 31, of which 13 were waited for; matrix products, arithmetic and copies ran while one was open for 0% of the time, Pallas kernels for 10%

profile of v4, /device:TPU:1, one launch (start us, length us, event | category | flops | bytes accessed | tf_op | source)
XLA Modules:
  0.0 144.3 jit_solution(14167165323374856626)
XLA Ops:
  6.5 2.2 %rows_to_owners.2 = (bf16[384,768]{1,0:T(8,128)(2,1)S(1)}, bf16[64,768]{1,0:T(8,128)(2,1)S(1)}, bf16[64,768]{1,0:T(8,128)(2,1)S(1)}, bf16[128,896]{1,0:T(8,128)(2,1)S(1)}, bf16[128,896]{1,0:T(8,128)(2,1)S(1)}) custom-call(s32[32]{0:T(128)} %starts.3, bf16[384,512]{1,0:T(8,128)(2,1)} %q.1, bf16[384,128]{1,0:T(8,128)(2,1)} %k.1, bf16[384,128]{1,0:T(8,128)(2,1)} %v.1, ...), custom_call_target="tpu_custom_call" | custom-call | tf_op jit(solution)/shard_map/rows_to_owners/pallas_call | solution.py:132
  8.7 2.2 %collective-permute-start.2 = (bf16[128,896]{1,0:T(8,128)(2,1)S(1)}, bf16[128,896]{1,0:T(8,128)(2,1)S(1)}, u32[]{:S(2)}, u32[]{:S(2)}) collective-permute-start(bf16[128,896]{1,0:T(8,128)(2,1)S(1)} %get-tuple-element.36), channel_id=1, source_target_pairs={{0,64},{64,128},{128,192},{192,0},{1,65},{65,129},{129,193},{193,1... | collective-permute-start | bytes 688136 | tf_op jit(solution)/shard_map/rows_to_owners/ppermute | solution.py:34
  15.6 4.4 %collective-permute-start.1 = (bf16[64,768]{1,0:T(8,128)(2,1)S(1)}, bf16[64,768]{1,0:T(8,128)(2,1)S(1)}, u32[]{:S(2)}, u32[]{:S(2)}) collective-permute-start(bf16[64,768]{1,0:T(8,128)(2,1)S(1)} %get-tuple-element.34), channel_id=1, source_target_pairs={{0,248},{8,0},{16,8},{24,16},{32,24},{40,32},{48,40},{56,48},{64,5... | collective-permute-start | bytes 294920 | tf_op jit(solution)/shard_map/rows_to_owners/ppermute | solution.py:145
  20.1 2.7 %collective-permute-done.low = bf16[64,768]{1,0:T(8,128)(2,1)S(1)} collective-permute-done((bf16[64,768]{1,0:T(8,128)(2,1)S(1)}, bf16[64,768]{1,0:T(8,128)(2,1)S(1)}, u32[]{:S(2)}, u32[]{:S(2)}) %collective-permute-start) | collective-permute-done | bytes 98336 | tf_op jit(solution)/shard_map/rows_to_owners/ppermute | solution.py:144
  22.8 2.7 %collective-permute-done.4.far_part = bf16[128,896]{1,0:T(8,128)(2,1)S(1)} collective-permute-done((bf16[128,896]{1,0:T(8,128)(2,1)S(1)}, bf16[128,896]{1,0:T(8,128)(2,1)S(1)}, u32[]{:S(2)}, u32[]{:S(2)}) %collective-permute-start.4) | collective-permute-done | bytes 229408 | tf_op jit(solution)/shard_map/rows_to_owners/ppermute | solution.py:34
  27.3 3.5 %collective-permute-start.7 = (bf16[256,256]{1,0:T(8,128)(2,1)S(1)}, bf16[256,256]{1,0:T(8,128)(2,1)S(1)}, u32[]{:S(2)}, u32[]{:S(2)}) collective-permute-start(bf16[256,256]{1,0:T(8,128)(2,1)S(1)} %get-tuple-element.38), channel_id=1, source_target_pairs={{0,56},{8,0},{16,8},{24,16},{32,24},{40,32},{48,40},{56,48},{1,57}... | collective-permute-start | bytes 393224 | tf_op jit(solution)/shard_map/keys_and_values/ppermute | solution.py:34
  30.9 2.3 %collective-permute-done.5 = bf16[256,256]{1,0:T(8,128)(2,1)S(1)} collective-permute-done((bf16[256,256]{1,0:T(8,128)(2,1)S(1)}, bf16[256,256]{1,0:T(8,128)(2,1)S(1)}, u32[]{:S(2)}, u32[]{:S(2)}) %collective-permute-start.5) | collective-permute-done | bytes 131104 | tf_op jit(solution)/shard_map/keys_and_values/ppermute | solution.py:34
  33.1 2.8 %collective-permute-start.8 = (bf16[256,256]{1,0:T(8,128)(2,1)S(1)}, bf16[256,256]{1,0:T(8,128)(2,1)S(1)}, u32[]{:S(2)}, u32[]{:S(2)}) collective-permute-start(bf16[256,256]{1,0:T(8,128)(2,1)S(1)} %collective-permute-done.7), channel_id=1, source_target_pairs={{0,56},{8,0},{16,8},{24,16},{32,24},{40,32},{48,40},{56,48},{1,57}... | collective-permute-start | bytes 393224 | tf_op jit(solution)/shard_map/keys_and_values/ppermute | solution.py:34
  35.9 2.3 %collective-permute-done.6 = bf16[256,256]{1,0:T(8,128)(2,1)S(1)} collective-permute-done((bf16[256,256]{1,0:T(8,128)(2,1)S(1)}, bf16[256,256]{1,0:T(8,128)(2,1)S(1)}, u32[]{:S(2)}, u32[]{:S(2)}) %collective-permute-start.6) | collective-permute-done | bytes 131104 | tf_op jit(solution)/shard_map/keys_and_values/ppermute | solution.py:34
  38.3 2.8 %collective-permute-start.13 = (bf16[256,256]{1,0:T(8,128)(2,1)S(1)}, bf16[256,256]{1,0:T(8,128)(2,1)S(1)}, u32[]{:S(2)}, u32[]{:S(2)}) collective-permute-start(bf16[256,256]{1,0:T(8,128)(2,1)S(1)} %collective-permute-done.8), channel_id=1, source_target_pairs={{0,56},{8,0},{16,8},{24,16},{32,24},{40,32},{48,40},{56,48},{1,57}... | collective-permute-start | bytes 393224 | tf_op jit(solution)/shard_map/keys_and_values/ppermute | solution.py:34
  41.0 1.9 %collective-permute-start.15 = (bf16[256,256]{1,0:T(8,128)(2,1)S(1)}, bf16[256,256]{1,0:T(8,128)(2,1)S(1)}, u32[]{:S(2)}, u32[]{:S(2)}) collective-permute-start(bf16[256,256]{1,0:T(8,128)(2,1)S(1)} %collective-permute-done.6), channel_id=1, source_target_pairs={{0,8},{8,16},{16,24},{24,32},{32,40},{40,48},{48,56},{56,0},{1,9},... | collective-permute-start | bytes 393224 | tf_op jit(solution)/shard_map/keys_and_values/ppermute | solution.py:34
  42.9 2.7 %collective-permute-start.17 = (bf16[1280,256]{1,0:T(8,128)(2,1)S(1)}, bf16[1280,256]{1,0:T(8,128)(2,1)S(1)}, u32[]{:S(2)}, u32[]{:S(2)}) collective-permute-start(bf16[1280,256]{1,0:T(8,128)(2,1)S(1)} %constant_dynamic-update-slice_fusion.refs_0_), channel_id=1, source_target_pairs={{0,64},{8,72},{16,80},{24,88},{32,96},{40,104},{48,112},{56,120},{... | collective-permute-start | bytes 1966088 | tf_op jit(solution)/shard_map/keys_and_values/ppermute | solution.py:43
  45.6 1.9 %collective-permute-start.11 = (bf16[768,256]{1,0:T(8,128)(2,1)S(1)}, bf16[768,256]{1,0:T(8,128)(2,1)S(1)}, u32[]{:S(2)}, u32[]{:S(2)}) collective-permute-start(bf16[768,256]{1,0:T(8,128)(2,1)S(1)} %slice.7), channel_id=1, source_target_pairs={{64,0},{72,8},{80,16},{88,24},{96,32},{104,40},{112,48},{120,56},{... | collective-permute-start | bytes 1179656 | tf_op jit(solution)/shard_map/keys_and_values/ppermute | solution.py:43
  47.6 2.3 %collective-permute-done.14 = bf16[256,256]{1,0:T(8,128)(2,1)S(1)} collective-permute-done((bf16[256,256]{1,0:T(8,128)(2,1)S(1)}, bf16[256,256]{1,0:T(8,128)(2,1)S(1)}, u32[]{:S(2)}, u32[]{:S(2)}) %collective-permute-start.14) | collective-permute-done | bytes 131104 | tf_op jit(solution)/shard_map/keys_and_values/ppermute | solution.py:34
  49.9 3.6 %collective-permute-done.15 = bf16[256,256]{1,0:T(8,128)(2,1)S(1)} collective-permute-done((bf16[256,256]{1,0:T(8,128)(2,1)S(1)}, bf16[256,256]{1,0:T(8,128)(2,1)S(1)}, u32[]{:S(2)}, u32[]{:S(2)}) %collective-permute-start.15) | collective-permute-done | bytes 131104 | tf_op jit(solution)/shard_map/keys_and_values/ppermute | solution.py:34
  53.5 4.9 %collective-permute-start.16 = (bf16[768,256]{1,0:T(8,128)(2,1)S(1)}, bf16[768,256]{1,0:T(8,128)(2,1)S(1)}, u32[]{:S(2)}, u32[]{:S(2)}) collective-permute-start(bf16[768,256]{1,0:T(8,128)(2,1)S(1)} %constant_dynamic-update-slice_fusion.5.refs_1_), channel_id=1, source_target_pairs={{0,64},{8,72},{16,80},{24,88},{32,96},{40,104},{48,112},{56,120},{... | collective-permute-start | bytes 1179656 | tf_op jit(solution)/shard_map/keys_and_values/ppermute | solution.py:43
  58.4 2.1 %collective-permute-start.9 = (bf16[512,256]{1,0:T(8,128)(2,1)S(1)}, bf16[512,256]{1,0:T(8,128)(2,1)S(1)}, u32[]{:S(2)}, u32[]{:S(2)}) collective-permute-start(bf16[512,256]{1,0:T(8,128)(2,1)S(1)} %slice.6), channel_id=1, source_target_pairs={{64,0},{72,8},{0,192},{8,200},{65,1},{73,9},{1,193},{9,201},{66,2}... | collective-permute-start | bytes 786440 | tf_op jit(solution)/shard_map/keys_and_values/ppermute | solution.py:43
  63.3 2.4 %collective-permute-done.16.refs_1_ = bf16[768,256]{1,0:T(8,128)(2,1)S(1)} collective-permute-done((bf16[768,256]{1,0:T(8,128)(2,1)S(1)}, bf16[768,256]{1,0:T(8,128)(2,1)S(1)}, u32[]{:S(2)}, u32[]{:S(2)}) %collective-permute-start.16) | collective-permute-done | bytes 393248 | tf_op jit(solution)/shard_map/keys_and_values/ppermute | solution.py:43
  66.3 5.5 %collective-permute-start.10 = (bf16[512,256]{1,0:T(8,128)(2,1)S(1)}, bf16[512,256]{1,0:T(8,128)(2,1)S(1)}, u32[]{:S(2)}, u32[]{:S(2)}) collective-permute-start(bf16[512,256]{1,0:T(8,128)(2,1)S(1)} %collective-permute-done.9), channel_id=1, source_target_pairs={{192,128},{200,136},{0,192},{8,200},{193,129},{201,137},{1,193},{9... | collective-permute-start | bytes 786440 | tf_op jit(solution)/shard_map/keys_and_values/ppermute | solution.py:43
  72.6 5.3 %collective-permute-done.10.refs_0_ = bf16[512,256]{1,0:T(8,128)(2,1)S(1)} collective-permute-done((bf16[512,256]{1,0:T(8,128)(2,1)S(1)}, bf16[512,256]{1,0:T(8,128)(2,1)S(1)}, u32[]{:S(2)}, u32[]{:S(2)}) %collective-permute-start.10) | collective-permute-done | bytes 262176 | tf_op jit(solution)/shard_map/keys_and_values/ppermute | solution.py:43
  78.9 2.4 %collective-permute-start.20 = (bf16[256,512]{1,0:T(8,128)(2,1)S(1)}, bf16[256,512]{1,0:T(8,128)(2,1)S(1)}, u32[]{:S(2)}, u32[]{:S(2)}) collective-permute-start(bf16[256,512]{1,0:T(8,128)(2,1)S(1)} %attention.3), channel_id=1, source_target_pairs={{0,66},{2,68},{4,70},{6,64},{64,2},{66,4},{68,6},{70,0},{1,67},{3,... | collective-permute-start | bytes 786440 | tf_op jit(solution)/shard_map/features/ppermute | solution.py:49
  82.6 2.6 %collective-permute-start.22 = (bf16[256,512]{1,0:T(8,128)(2,1)S(1)}, bf16[256,512]{1,0:T(8,128)(2,1)S(1)}, u32[]{:S(2)}, u32[]{:S(2)}) collective-permute-start(bf16[256,512]{1,0:T(8,128)(2,1)S(1)} %attention.3), channel_id=1, source_target_pairs={{0,68},{2,70},{4,64},{6,66},{64,4},{66,6},{68,0},{70,2},{1,69},{3,... | collective-permute-start | bytes 786440 | tf_op jit(solution)/shard_map/features/ppermute | solution.py:49
  86.6 15.0 %collective-permute-done.19 = bf16[256,512]{1,0:T(8,128)(2,1)S(1)} collective-permute-done((bf16[256,512]{1,0:T(8,128)(2,1)S(1)}, bf16[256,512]{1,0:T(8,128)(2,1)S(1)}, u32[]{:S(2)}, u32[]{:S(2)}) %collective-permute-start.19) | collective-permute-done | bytes 262176 | tf_op jit(solution)/shard_map/features/ppermute | solution.py:49
  101.6 3.4 %collective-permute-start.27 = (bf16[256,512]{1,0:T(8,128)(2,1)S(1)}, bf16[256,512]{1,0:T(8,128)(2,1)S(1)}, u32[]{:S(2)}, u32[]{:S(2)}) collective-permute-start(bf16[256,512]{1,0:T(8,128)(2,1)S(1)} %attention.3), channel_id=1, source_target_pairs={{0,6},{2,0},{4,2},{6,4},{1,7},{3,1},{5,3},{7,5},{8,14},{10,8},{12,... | collective-permute-start | bytes 786440 | tf_op jit(solution)/shard_map/features/ppermute | solution.py:34
  105.3 2.3 %collective-permute-start.23 = (bf16[1024,512]{1,0:T(8,128)(2,1)S(1)}, bf16[1024,512]{1,0:T(8,128)(2,1)S(1)}, u32[]{:S(2)}, u32[]{:S(2)}) collective-permute-start(bf16[1024,512]{1,0:T(8,128)(2,1)S(1)} %constant_dynamic-update-slice_fusion.8.mine), channel_id=1, source_target_pairs={{0,1},{1,0},{2,3},{3,2},{4,5},{5,4},{6,7},{7,6},{8,9},{9,8},{10,11... | collective-permute-start | bytes 3145736 | tf_op jit(solution)/shard_map/features/ppermute | solution.py:34
  108.7 3.3 %collective-permute-done.26 = bf16[256,512]{1,0:T(8,128)(2,1)S(1)} collective-permute-done((bf16[256,512]{1,0:T(8,128)(2,1)S(1)}, bf16[256,512]{1,0:T(8,128)(2,1)S(1)}, u32[]{:S(2)}, u32[]{:S(2)}) %collective-permute-start.26) | collective-permute-done | bytes 262176 | tf_op jit(solution)/shard_map/features/ppermute | solution.py:34
  112.1 3.1 %collective-permute-start.29 = (bf16[1024,512]{1,0:T(8,128)(2,1)S(1)}, bf16[1024,512]{1,0:T(8,128)(2,1)}, u32[]{:S(2)}, u32[]{:S(2)}) collective-permute-start(bf16[1024,512]{1,0:T(8,128)(2,1)S(1)} %pad_maximum_fusion.mine), channel_id=1, source_target_pairs={{0,1},{1,0},{2,3},{3,2},{4,5},{5,4},{6,7},{7,6},{8,9},{9,8},{10,11... | collective-permute-start | bytes 3145736 | tf_op jit(solution)/shard_map/features/ppermute | solution.py:34
  116.3 4.9 %all-gather.2.cloned.1.call-done.weight = bf16[4096,896]{1,0:T(8,128)(2,1)} async-done(((bf16[512,896]{1,0:T(8,128)(2,1)}), bf16[4096,896]{1,0:T(8,128)(2,1)}) %all-gather.2.cloned.1.call-update) | async-done | bytes 7340048 | tf_op jit(solution)/shard_map/weight_rows/all_gather | solution.py:411
  121.2 3.7 %gate.5 = (bf16[256,640]{1,0:T(8,128)(2,1)S(1)}, bf16[4096,896]{1,0:T(8,128)(2,1)S(1)}) custom-call(bf16[256,4096]{1,0:T(8,128)(2,1)S(1)} %get-tuple-element.50.rows, f32[256,128]{1,0:T(8,128)S(1)} %get-tuple-element.54.inv, bf16[4096,896]{1,0:T(8,128)(2,1)} %all-gather.2.cloned.1.call-done.weight), custom_call_target="tpu_custom_call" | custom-call | tf_op jit(solution)/shard_map/gate/pallas_call | solution.py:324
  127.4 2.3 %gate.7 = (bf16[256,4096]{1,0:T(8,128)(2,1)S(1)}, f32[256,128]{1,0:T(8,128)S(1)}) custom-call(f32[1,4096]{1,0:T(1,128)S(1)} %bitcast.2, bf16[1024,512]{1,0:T(8,128)(2,1)S(1)} %pad_maximum_fusion.mine, bf16[1024,512]{1,0:T(8,128)(2,1)} %collective-permute-done.29.other), custom_call_target="tpu_custom_call" | custom-call | tf_op jit(solution)/shard_map/gate/pallas_call | solution.py:285
  129.6 3.4 %gate.8._ = bf16[256,1792]{1,0:T(8,128)(2,1)} custom-call(bf16[256,4096]{1,0:T(8,128)(2,1)S(1)} %get-tuple-element.57.rows, f32[256,128]{1,0:T(8,128)S(1)} %get-tuple-element.58.inv, bf16[4096,896]{1,0:T(8,128)(2,1)S(1)} %get-tuple-element.55.weight), custom_call_target="tpu_custom_call" | custom-call | flops 1879048192 | bytes 7340032 | tf_op jit(solution)/shard_map/gate/pallas_call | solution.py:365
  133.0 3.6 %collective-permute-done.25.rest = bf16[256,256]{1,0:T(8,128)(2,1)S(1)} collective-permute-done((bf16[256,256]{1,0:T(8,128)(2,1)S(1)}, bf16[256,256]{1,0:T(8,128)(2,1)S(1)}, u32[]{:S(2)}, u32[]{:S(2)}) %collective-permute-start.25) | collective-permute-done | bytes 131104 | tf_op jit(solution)/shard_map/gate/ppermute | solution.py:34
  (61 shorter events, 20.0 us)
Async XLA Ops:
  6.5 114.7 %all-gather.2.cloned.1.call-start = ((), (), s32[]{:S(2)}) async-start(), calls=%async_computation | async-start | bytes 8257536 | tf_op jit(solution)/shard_map/weight_rows/all_gather | solution.py:411
  8.7 14.1 %collective-permute-start.2 = (bf16[128,896]{1,0:T(8,128)(2,1)S(1)}, bf16[128,896]{1,0:T(8,128)(2,1)S(1)}, u32[]{:S(2)}, u32[]{:S(2)}) collective-permute-start(bf16[128,896]{1,0:T(8,128)(2,1)S(1)} %get-tuple-element.36), channel_id=1, source_target_pairs={{0,64},{64,128},{128,192},{192,0},{1,65},{65,129},{129,193},{193,1... | collective-permute-start | bytes 688136 | tf_op jit(solution)/shard_map/rows_to_owners/ppermute | solution.py:34
  10.9 11.9 %collective-permute-start.3 = (bf16[128,896]{1,0:T(8,128)(2,1)S(1)}, bf16[128,896]{1,0:T(8,128)(2,1)S(1)}, u32[]{:S(2)}, u32[]{:S(2)}) collective-permute-start(bf16[128,896]{1,0:T(8,128)(2,1)S(1)} %get-tuple-element.36), channel_id=1, source_target_pairs={{0,192},{64,0},{128,64},{192,128},{1,193},{65,1},{129,65},{193,129... | collective-permute-start | bytes 688136 | tf_op jit(solution)/shard_map/rows_to_owners/ppermute | solution.py:34
  12.4 13.1 %collective-permute-start.4 = (bf16[128,896]{1,0:T(8,128)(2,1)S(1)}, bf16[128,896]{1,0:T(8,128)(2,1)S(1)}, u32[]{:S(2)}, u32[]{:S(2)}) collective-permute-start(bf16[128,896]{1,0:T(8,128)(2,1)S(1)} %get-tuple-element.35.own_part), channel_id=1, source_target_pairs={{0,128},{64,192},{128,0},{192,64},{1,129},{65,193},{129,1},{193,65... | collective-permute-start | bytes 688136 | tf_op jit(solution)/shard_map/rows_to_owners/ppermute | solution.py:34
  14.0 8.8 %collective-permute-start = (bf16[64,768]{1,0:T(8,128)(2,1)S(1)}, bf16[64,768]{1,0:T(8,128)(2,1)S(1)}, u32[]{:S(2)}, u32[]{:S(2)}) collective-permute-start(bf16[64,768]{1,0:T(8,128)(2,1)S(1)} %get-tuple-element.33), channel_id=1, source_target_pairs={{0,8},{8,16},{16,24},{24,32},{32,40},{40,48},{48,56},{56,64},{64,7... | collective-permute-start | bytes 294920 | tf_op jit(solution)/shard_map/rows_to_owners/ppermute | solution.py:144
  15.6 7.2 %collective-permute-start.1 = (bf16[64,768]{1,0:T(8,128)(2,1)S(1)}, bf16[64,768]{1,0:T(8,128)(2,1)S(1)}, u32[]{:S(2)}, u32[]{:S(2)}) collective-permute-start(bf16[64,768]{1,0:T(8,128)(2,1)S(1)} %get-tuple-element.34), channel_id=1, source_target_pairs={{0,248},{8,0},{16,8},{24,16},{32,24},{40,32},{48,40},{56,48},{64,5... | collective-permute-start | bytes 294920 | tf_op jit(solution)/shard_map/rows_to_owners/ppermute | solution.py:145
  27.2 5.9 %collective-permute-start.5 = (bf16[256,256]{1,0:T(8,128)(2,1)S(1)}, bf16[256,256]{1,0:T(8,128)(2,1)S(1)}, u32[]{:S(2)}, u32[]{:S(2)}) collective-permute-start(bf16[256,256]{1,0:T(8,128)(2,1)S(1)} %get-tuple-element.38), channel_id=1, source_target_pairs={{0,8},{8,16},{16,24},{24,32},{32,40},{40,48},{48,56},{56,0},{1,9},... | collective-permute-start | bytes 393224 | tf_op jit(solution)/shard_map/keys_and_values/ppermute | solution.py:34
  27.3 5.8 %collective-permute-start.7 = (bf16[256,256]{1,0:T(8,128)(2,1)S(1)}, bf16[256,256]{1,0:T(8,128)(2,1)S(1)}, u32[]{:S(2)}, u32[]{:S(2)}) collective-permute-start(bf16[256,256]{1,0:T(8,128)(2,1)S(1)} %get-tuple-element.38), channel_id=1, source_target_pairs={{0,56},{8,0},{16,8},{24,16},{32,24},{40,32},{48,40},{56,48},{1,57}... | collective-permute-start | bytes 393224 | tf_op jit(solution)/shard_map/keys_and_values/ppermute | solution.py:34
  33.1 5.0 %collective-permute-start.6 = (bf16[256,256]{1,0:T(8,128)(2,1)S(1)}, bf16[256,256]{1,0:T(8,128)(2,1)S(1)}, u32[]{:S(2)}, u32[]{:S(2)}) collective-permute-start(bf16[256,256]{1,0:T(8,128)(2,1)S(1)} %collective-permute-done.5), channel_id=1, source_target_pairs={{0,8},{8,16},{16,24},{24,32},{32,40},{40,48},{48,56},{56,0},{1,9},... | collective-permute-start | bytes 393224 | tf_op jit(solution)/shard_map/keys_and_values/ppermute | solution.py:34
  33.1 5.1 %collective-permute-start.8 = (bf16[256,256]{1,0:T(8,128)(2,1)S(1)}, bf16[256,256]{1,0:T(8,128)(2,1)S(1)}, u32[]{:S(2)}, u32[]{:S(2)}) collective-permute-start(bf16[256,256]{1,0:T(8,128)(2,1)S(1)} %collective-permute-done.7), channel_id=1, source_target_pairs={{0,56},{8,0},{16,8},{24,16},{32,24},{40,32},{48,40},{56,48},{1,57}... | collective-permute-start | bytes 393224 | tf_op jit(solution)/shard_map/keys_and_values/ppermute | solution.py:34
  38.3 9.3 %collective-permute-start.13 = (bf16[256,256]{1,0:T(8,128)(2,1)S(1)}, bf16[256,256]{1,0:T(8,128)(2,1)S(1)}, u32[]{:S(2)}, u32[]{:S(2)}) collective-permute-start(bf16[256,256]{1,0:T(8,128)(2,1)S(1)} %collective-permute-done.8), channel_id=1, source_target_pairs={{0,56},{8,0},{16,8},{24,16},{32,24},{40,32},{48,40},{56,48},{1,57}... | collective-permute-start | bytes 393224 | tf_op jit(solution)/shard_map/keys_and_values/ppermute | solution.py:34
  41.0 8.9 %collective-permute-start.14 = (bf16[256,256]{1,0:T(8,128)(2,1)S(1)}, bf16[256,256]{1,0:T(8,128)(2,1)S(1)}, u32[]{:S(2)}, u32[]{:S(2)}) collective-permute-start(bf16[256,256]{1,0:T(8,128)(2,1)S(1)} %collective-permute-done.6), channel_id=1, source_target_pairs={{0,16},{8,24},{16,32},{24,40},{32,48},{40,56},{48,0},{56,8},{1,17}... | collective-permute-start | bytes 393224 | tf_op jit(solution)/shard_map/keys_and_values/ppermute | solution.py:34
  41.0 12.5 %collective-permute-start.15 = (bf16[256,256]{1,0:T(8,128)(2,1)S(1)}, bf16[256,256]{1,0:T(8,128)(2,1)S(1)}, u32[]{:S(2)}, u32[]{:S(2)}) collective-permute-start(bf16[256,256]{1,0:T(8,128)(2,1)S(1)} %collective-permute-done.6), channel_id=1, source_target_pairs={{0,8},{8,16},{16,24},{24,32},{32,40},{40,48},{48,56},{56,0},{1,9},... | collective-permute-start | bytes 393224 | tf_op jit(solution)/shard_map/keys_and_values/ppermute | solution.py:34
  42.9 22.7 %collective-permute-start.17 = (bf16[1280,256]{1,0:T(8,128)(2,1)S(1)}, bf16[1280,256]{1,0:T(8,128)(2,1)S(1)}, u32[]{:S(2)}, u32[]{:S(2)}) collective-permute-start(bf16[1280,256]{1,0:T(8,128)(2,1)S(1)} %constant_dynamic-update-slice_fusion.refs_0_), channel_id=1, source_target_pairs={{0,64},{8,72},{16,80},{24,88},{32,96},{40,104},{48,112},{56,120},{... | collective-permute-start | bytes 1966088 | tf_op jit(solution)/shard_map/keys_and_values/ppermute | solution.py:43
  45.6 16.3 %collective-permute-start.11 = (bf16[768,256]{1,0:T(8,128)(2,1)S(1)}, bf16[768,256]{1,0:T(8,128)(2,1)S(1)}, u32[]{:S(2)}, u32[]{:S(2)}) collective-permute-start(bf16[768,256]{1,0:T(8,128)(2,1)S(1)} %slice.7), channel_id=1, source_target_pairs={{64,0},{72,8},{80,16},{88,24},{96,32},{104,40},{112,48},{120,56},{... | collective-permute-start | bytes 1179656 | tf_op jit(solution)/shard_map/keys_and_values/ppermute | solution.py:43
  53.5 12.1 %collective-permute-start.16 = (bf16[768,256]{1,0:T(8,128)(2,1)S(1)}, bf16[768,256]{1,0:T(8,128)(2,1)S(1)}, u32[]{:S(2)}, u32[]{:S(2)}) collective-permute-start(bf16[768,256]{1,0:T(8,128)(2,1)S(1)} %constant_dynamic-update-slice_fusion.5.refs_1_), channel_id=1, source_target_pairs={{0,64},{8,72},{16,80},{24,88},{32,96},{40,104},{48,112},{56,120},{... | collective-permute-start | bytes 1179656 | tf_op jit(solution)/shard_map/keys_and_values/ppermute | solution.py:43
  58.4 7.9 %collective-permute-start.9 = (bf16[512,256]{1,0:T(8,128)(2,1)S(1)}, bf16[512,256]{1,0:T(8,128)(2,1)S(1)}, u32[]{:S(2)}, u32[]{:S(2)}) collective-permute-start(bf16[512,256]{1,0:T(8,128)(2,1)S(1)} %slice.6), channel_id=1, source_target_pairs={{64,0},{72,8},{0,192},{8,200},{65,1},{73,9},{1,193},{9,201},{66,2}... | collective-permute-start | bytes 786440 | tf_op jit(solution)/shard_map/keys_and_values/ppermute | solution.py:43
  61.9 15.9 %collective-permute-start.12 = (bf16[768,256]{1,0:T(8,128)(2,1)S(1)}, bf16[768,256]{1,0:T(8,128)(2,1)S(1)}, u32[]{:S(2)}, u32[]{:S(2)}) collective-permute-start(bf16[768,256]{1,0:T(8,128)(2,1)S(1)} %collective-permute-done.11), channel_id=1, source_target_pairs={{192,128},{200,136},{208,144},{216,152},{224,160},{232,168},{240,1... | collective-permute-start | bytes 1179656 | tf_op jit(solution)/shard_map/keys_and_values/ppermute | solution.py:43
  65.6 12.3 %collective-permute-start.18 = (bf16[768,256]{1,0:T(8,128)(2,1)S(1)}, bf16[768,256]{1,0:T(8,128)(2,1)S(1)}, u32[]{:S(2)}, u32[]{:S(2)}) collective-permute-start(bf16[768,256]{1,0:T(8,128)(2,1)S(1)} %collective-permute-done.16.refs_1_), channel_id=1, source_target_pairs={{64,128},{72,136},{80,144},{88,152},{96,160},{128,192},{136,200},{... | collective-permute-start | bytes 1179656 | tf_op jit(solution)/shard_map/keys_and_values/ppermute | solution.py:43
  66.3 11.6 %collective-permute-start.10 = (bf16[512,256]{1,0:T(8,128)(2,1)S(1)}, bf16[512,256]{1,0:T(8,128)(2,1)S(1)}, u32[]{:S(2)}, u32[]{:S(2)}) collective-permute-start(bf16[512,256]{1,0:T(8,128)(2,1)S(1)} %collective-permute-done.9), channel_id=1, source_target_pairs={{192,128},{200,136},{0,192},{8,200},{193,129},{201,137},{1,193},{9... | collective-permute-start | bytes 786440 | tf_op jit(solution)/shard_map/keys_and_values/ppermute | solution.py:43
  78.8 36.5 %copy-start = (f32[4096]{0:T(1024)S(1)}, f32[4096]{0:T(1024)}, u32[]{:S(2)}) copy-start(f32[4096]{0:T(1024)} %param.12) | copy-start | bytes 49156
  78.8 22.8 %collective-permute-start.19 = (bf16[256,512]{1,0:T(8,128)(2,1)S(1)}, bf16[256,512]{1,0:T(8,128)(2,1)S(1)}, u32[]{:S(2)}, u32[]{:S(2)}) collective-permute-start(bf16[256,512]{1,0:T(8,128)(2,1)S(1)} %attention.3), channel_id=1, source_target_pairs={{0,64},{2,66},{4,68},{6,70},{64,0},{66,2},{68,4},{70,6},{1,65},{3,... | collective-permute-start | bytes 786440 | tf_op jit(solution)/shard_map/features/ppermute | solution.py:49
  78.9 26.2 %collective-permute-start.20 = (bf16[256,512]{1,0:T(8,128)(2,1)S(1)}, bf16[256,512]{1,0:T(8,128)(2,1)S(1)}, u32[]{:S(2)}, u32[]{:S(2)}) collective-permute-start(bf16[256,512]{1,0:T(8,128)(2,1)S(1)} %attention.3), channel_id=1, source_target_pairs={{0,66},{2,68},{4,70},{6,64},{64,2},{66,4},{68,6},{70,0},{1,67},{3,... | collective-permute-start | bytes 786440 | tf_op jit(solution)/shard_map/features/ppermute | solution.py:49
  81.3 23.9 %collective-permute-start.21 = (bf16[256,512]{1,0:T(8,128)(2,1)S(1)}, bf16[256,512]{1,0:T(8,128)(2,1)S(1)}, u32[]{:S(2)}, u32[]{:S(2)}) collective-permute-start(bf16[256,512]{1,0:T(8,128)(2,1)S(1)} %attention.3), channel_id=1, source_target_pairs={{0,70},{2,64},{4,66},{6,68},{64,6},{66,0},{68,2},{70,4},{1,71},{3,... | collective-permute-start | bytes 786440 | tf_op jit(solution)/shard_map/features/ppermute | solution.py:49
  82.6 22.6 %collective-permute-start.22 = (bf16[256,512]{1,0:T(8,128)(2,1)S(1)}, bf16[256,512]{1,0:T(8,128)(2,1)S(1)}, u32[]{:S(2)}, u32[]{:S(2)}) collective-permute-start(bf16[256,512]{1,0:T(8,128)(2,1)S(1)} %attention.3), channel_id=1, source_target_pairs={{0,68},{2,70},{4,64},{6,66},{64,4},{66,6},{68,0},{70,2},{1,69},{3,... | collective-permute-start | bytes 786440 | tf_op jit(solution)/shard_map/features/ppermute | solution.py:49
  85.2 22.4 %collective-permute-start.28 = (bf16[256,512]{1,0:T(8,128)(2,1)S(1)}, bf16[256,512]{1,0:T(8,128)(2,1)S(1)}, u32[]{:S(2)}, u32[]{:S(2)}) collective-permute-start(bf16[256,512]{1,0:T(8,128)(2,1)S(1)} %attention.3), channel_id=1, source_target_pairs={{0,4},{2,6},{4,0},{6,2},{1,5},{3,7},{5,1},{7,3},{8,12},{10,14},{12... | collective-permute-start | bytes 786440 | tf_op jit(solution)/shard_map/features/ppermute | solution.py:34
  101.6 7.1 %collective-permute-start.27 = (bf16[256,512]{1,0:T(8,128)(2,1)S(1)}, bf16[256,512]{1,0:T(8,128)(2,1)S(1)}, u32[]{:S(2)}, u32[]{:S(2)}) collective-permute-start(bf16[256,512]{1,0:T(8,128)(2,1)S(1)} %attention.3), channel_id=1, source_target_pairs={{0,6},{2,0},{4,2},{6,4},{1,7},{3,1},{5,3},{7,5},{8,14},{10,8},{12,... | collective-permute-start | bytes 786440 | tf_op jit(solution)/shard_map/features/ppermute | solution.py:34
  105.1 7.0 %collective-permute-start.26 = (bf16[256,512]{1,0:T(8,128)(2,1)S(1)}, bf16[256,512]{1,0:T(8,128)(2,1)S(1)}, u32[]{:S(2)}, u32[]{:S(2)}) collective-permute-start(bf16[256,512]{1,0:T(8,128)(2,1)S(1)} %attention.3), channel_id=1, source_target_pairs={{0,2},{2,4},{4,6},{6,0},{1,3},{3,5},{5,7},{7,1},{8,10},{10,12},{12... | collective-permute-start | bytes 786440 | tf_op jit(solution)/shard_map/features/ppermute | solution.py:34
  105.3 10.0 %collective-permute-start.23 = (bf16[1024,512]{1,0:T(8,128)(2,1)S(1)}, bf16[1024,512]{1,0:T(8,128)(2,1)S(1)}, u32[]{:S(2)}, u32[]{:S(2)}) collective-permute-start(bf16[1024,512]{1,0:T(8,128)(2,1)S(1)} %constant_dynamic-update-slice_fusion.8.mine), channel_id=1, source_target_pairs={{0,1},{1,0},{2,3},{3,2},{4,5},{5,4},{6,7},{7,6},{8,9},{9,8},{10,11... | collective-permute-start | bytes 3145736 | tf_op jit(solution)/shard_map/features/ppermute | solution.py:34
  112.1 15.2 %collective-permute-start.29 = (bf16[1024,512]{1,0:T(8,128)(2,1)S(1)}, bf16[1024,512]{1,0:T(8,128)(2,1)}, u32[]{:S(2)}, u32[]{:S(2)}) collective-permute-start(bf16[1024,512]{1,0:T(8,128)(2,1)S(1)} %pad_maximum_fusion.mine), channel_id=1, source_target_pairs={{0,1},{1,0},{2,3},{3,2},{4,5},{5,4},{6,7},{7,6},{8,9},{9,8},{10,11... | collective-permute-start | bytes 3145736 | tf_op jit(solution)/shard_map/features/ppermute | solution.py:34
  125.0 11.7 %collective-permute-start.24 = (bf16[256,640]{1,0:T(8,128)(2,1)S(1)}, bf16[256,640]{1,0:T(8,128)(2,1)S(1)}, u32[]{:S(2)}, u32[]{:S(2)}) collective-permute-start(bf16[256,640]{1,0:T(8,128)(2,1)S(1)} %get-tuple-element.53), channel_id=1, source_target_pairs={{0,64},{64,0},{1,65},{65,1},{2,66},{66,2},{3,67},{67,3},{4,68},{68... | collective-permute-start | bytes 983048 | tf_op jit(solution)/shard_map/gate/ppermute | solution.py:34
  127.1 9.6 %collective-permute-start.25 = (bf16[256,256]{1,0:T(8,128)(2,1)S(1)}, bf16[256,256]{1,0:T(8,128)(2,1)S(1)}, u32[]{:S(2)}, u32[]{:S(2)}) collective-permute-start(bf16[256,256]{1,0:T(8,128)(2,1)S(1)} %gate.6), channel_id=1, source_target_pairs={{0,64},{64,0},{1,65},{65,1},{2,66},{66,2},{3,67},{67,3},{4,68},{68... | collective-permute-start | bytes 393224 | tf_op jit(solution)/shard_map/gate/ppermute | solution.py:34
  (1 other events, 33.3 us)
Sparse Core Ops, SparseCore 0:
  27.3 93.8 all-gather.1

commit v5 on v3

--- a/solution.py
+++ b/solution.py
@@ -18,7 +18,7 @@
 HERE = 2
 FAR = 5
 SENT_FIRST = 512
-PARTS = 4
+PARTS = 2
 NORM_EPS = 1e-05
 MASKED = -1e30
 LOG2E = 1.4426950408889634

time: 145 us -> 145 us (level)
  no operation moved by 1% of the time
where the time goes in v5:
time: 145 us; the launch traced here: 144 us
  starting transfers between devices  59.8 us (41%)
  waiting for transfers between devices  52 us (36%)
  Pallas kernels  18.1 us (12%)
  between operations  13.7 us (9%)
    ppermute x17, starting transfers between devices, shift(): lax.ppermute(block, axis, [(i, (i + distance) % count) for i in range(cou...  28.3 us
    ppermute x17, waiting for transfers between devices, shift(): lax.ppermute(block, axis, [(i, (i + distance) % count) for i in range(cou...  21.6 us
    ppermute x7, starting transfers between devices, hop(): lax.ppermute(block, ROWS, [(a * NZ + z, b * NZ + z) for a, b in route for...  19.1 us
    ppermute x4, waiting for transfers between devices, shift_both(): lax.ppermute(block, ('yb', 'x'), [(b * NX + i, to(b, i)) for b, i in pairs])  15 us
    ppermute x7, waiting for transfers between devices, hop(): lax.ppermute(block, ROWS, [(a * NZ + z, b * NZ + z) for a, b in route for...  7.69 us
    ppermute x4, starting transfers between devices, shift_both(): lax.ppermute(block, ('yb', 'x'), [(b * NX + i, to(b, i)) for b, i in pairs])  6.41 us
    all_gather x1, waiting for transfers between devices, on_device(): weight = lax.all_gather(pair, 'z', axis=0, tiled=True)  4.92 us
    ppermute x1, starting transfers between devices, align(): lax.ppermute(down, ROWS, [(i, (i - 1) % count) for i in range(count)])  4.43 us
  transfers between devices with their start and end apart: 31, of which 13 were waited for; matrix products, arithmetic and copies ran while one was open for 0% of the time, Pallas kernels for 9%

profile of v5, /device:TPU:1, one launch (start us, length us, event | category | flops | bytes accessed | tf_op | source)
XLA Modules:
  0.0 144.0 jit_solution(9418130589064273823)
XLA Ops:
  6.5 2.2 %rows_to_owners.2 = (bf16[384,768]{1,0:T(8,128)(2,1)S(1)}, bf16[64,768]{1,0:T(8,128)(2,1)S(1)}, bf16[64,768]{1,0:T(8,128)(2,1)S(1)}, bf16[128,896]{1,0:T(8,128)(2,1)S(1)}, bf16[128,896]{1,0:T(8,128)(2,1)S(1)}) custom-call(s32[32]{0:T(128)} %starts.3, bf16[384,512]{1,0:T(8,128)(2,1)} %q.1, bf16[384,128]{1,0:T(8,128)(2,1)} %k.1, bf16[384,128]{1,0:T(8,128)(2,1)} %v.1, ...), custom_call_target="tpu_custom_call" | custom-call | tf_op jit(solution)/shard_map/rows_to_owners/pallas_call | solution.py:132
  8.7 2.2 %collective-permute-start.2 = (bf16[128,896]{1,0:T(8,128)(2,1)S(1)}, bf16[128,896]{1,0:T(8,128)(2,1)S(1)}, u32[]{:S(2)}, u32[]{:S(2)}) collective-permute-start(bf16[128,896]{1,0:T(8,128)(2,1)S(1)} %get-tuple-element.36), channel_id=1, source_target_pairs={{0,64},{64,128},{128,192},{192,0},{1,65},{65,129},{129,193},{193,1... | collective-permute-start | bytes 688136 | tf_op jit(solution)/shard_map/rows_to_owners/ppermute | solution.py:34
  15.6 4.4 %collective-permute-start.1 = (bf16[64,768]{1,0:T(8,128)(2,1)S(1)}, bf16[64,768]{1,0:T(8,128)(2,1)S(1)}, u32[]{:S(2)}, u32[]{:S(2)}) collective-permute-start(bf16[64,768]{1,0:T(8,128)(2,1)S(1)} %get-tuple-element.34), channel_id=1, source_target_pairs={{0,248},{8,0},{16,8},{24,16},{32,24},{40,32},{48,40},{56,48},{64,5... | collective-permute-start | bytes 294920 | tf_op jit(solution)/shard_map/rows_to_owners/ppermute | solution.py:145
  20.1 2.7 %collective-permute-done.low = bf16[64,768]{1,0:T(8,128)(2,1)S(1)} collective-permute-done((bf16[64,768]{1,0:T(8,128)(2,1)S(1)}, bf16[64,768]{1,0:T(8,128)(2,1)S(1)}, u32[]{:S(2)}, u32[]{:S(2)}) %collective-permute-start) | collective-permute-done | bytes 98336 | tf_op jit(solution)/shard_map/rows_to_owners/ppermute | solution.py:144
  22.8 2.7 %collective-permute-done.4.far_part = bf16[128,896]{1,0:T(8,128)(2,1)S(1)} collective-permute-done((bf16[128,896]{1,0:T(8,128)(2,1)S(1)}, bf16[128,896]{1,0:T(8,128)(2,1)S(1)}, u32[]{:S(2)}, u32[]{:S(2)}) %collective-permute-start.4) | collective-permute-done | bytes 229408 | tf_op jit(solution)/shard_map/rows_to_owners/ppermute | solution.py:34
  27.3 3.5 %collective-permute-start.7 = (bf16[256,256]{1,0:T(8,128)(2,1)S(1)}, bf16[256,256]{1,0:T(8,128)(2,1)S(1)}, u32[]{:S(2)}, u32[]{:S(2)}) collective-permute-start(bf16[256,256]{1,0:T(8,128)(2,1)S(1)} %get-tuple-element.38), channel_id=1, source_target_pairs={{0,56},{8,0},{16,8},{24,16},{32,24},{40,32},{48,40},{56,48},{1,57}... | collective-permute-start | bytes 393224 | tf_op jit(solution)/shard_map/keys_and_values/ppermute | solution.py:34
  30.9 2.3 %collective-permute-done.5 = bf16[256,256]{1,0:T(8,128)(2,1)S(1)} collective-permute-done((bf16[256,256]{1,0:T(8,128)(2,1)S(1)}, bf16[256,256]{1,0:T(8,128)(2,1)S(1)}, u32[]{:S(2)}, u32[]{:S(2)}) %collective-permute-start.5) | collective-permute-done | bytes 131104 | tf_op jit(solution)/shard_map/keys_and_values/ppermute | solution.py:34
  33.1 2.8 %collective-permute-start.8 = (bf16[256,256]{1,0:T(8,128)(2,1)S(1)}, bf16[256,256]{1,0:T(8,128)(2,1)S(1)}, u32[]{:S(2)}, u32[]{:S(2)}) collective-permute-start(bf16[256,256]{1,0:T(8,128)(2,1)S(1)} %collective-permute-done.7), channel_id=1, source_target_pairs={{0,56},{8,0},{16,8},{24,16},{32,24},{40,32},{48,40},{56,48},{1,57}... | collective-permute-start | bytes 393224 | tf_op jit(solution)/shard_map/keys_and_values/ppermute | solution.py:34
  35.9 2.3 %collective-permute-done.6 = bf16[256,256]{1,0:T(8,128)(2,1)S(1)} collective-permute-done((bf16[256,256]{1,0:T(8,128)(2,1)S(1)}, bf16[256,256]{1,0:T(8,128)(2,1)S(1)}, u32[]{:S(2)}, u32[]{:S(2)}) %collective-permute-start.6) | collective-permute-done | bytes 131104 | tf_op jit(solution)/shard_map/keys_and_values/ppermute | solution.py:34
  38.3 2.8 %collective-permute-start.13 = (bf16[256,256]{1,0:T(8,128)(2,1)S(1)}, bf16[256,256]{1,0:T(8,128)(2,1)S(1)}, u32[]{:S(2)}, u32[]{:S(2)}) collective-permute-start(bf16[256,256]{1,0:T(8,128)(2,1)S(1)} %collective-permute-done.8), channel_id=1, source_target_pairs={{0,56},{8,0},{16,8},{24,16},{32,24},{40,32},{48,40},{56,48},{1,57}... | collective-permute-start | bytes 393224 | tf_op jit(solution)/shard_map/keys_and_values/ppermute | solution.py:34
  41.0 1.9 %collective-permute-start.15 = (bf16[256,256]{1,0:T(8,128)(2,1)S(1)}, bf16[256,256]{1,0:T(8,128)(2,1)S(1)}, u32[]{:S(2)}, u32[]{:S(2)}) collective-permute-start(bf16[256,256]{1,0:T(8,128)(2,1)S(1)} %collective-permute-done.6), channel_id=1, source_target_pairs={{0,8},{8,16},{16,24},{24,32},{32,40},{40,48},{48,56},{56,0},{1,9},... | collective-permute-start | bytes 393224 | tf_op jit(solution)/shard_map/keys_and_values/ppermute | solution.py:34
  42.9 2.7 %collective-permute-start.17 = (bf16[1280,256]{1,0:T(8,128)(2,1)S(1)}, bf16[1280,256]{1,0:T(8,128)(2,1)S(1)}, u32[]{:S(2)}, u32[]{:S(2)}) collective-permute-start(bf16[1280,256]{1,0:T(8,128)(2,1)S(1)} %constant_dynamic-update-slice_fusion.refs_0_), channel_id=1, source_target_pairs={{0,64},{8,72},{16,80},{24,88},{32,96},{40,104},{48,112},{56,120},{... | collective-permute-start | bytes 1966088 | tf_op jit(solution)/shard_map/keys_and_values/ppermute | solution.py:43
  45.6 1.9 %collective-permute-start.11 = (bf16[768,256]{1,0:T(8,128)(2,1)S(1)}, bf16[768,256]{1,0:T(8,128)(2,1)S(1)}, u32[]{:S(2)}, u32[]{:S(2)}) collective-permute-start(bf16[768,256]{1,0:T(8,128)(2,1)S(1)} %slice.7), channel_id=1, source_target_pairs={{64,0},{72,8},{80,16},{88,24},{96,32},{104,40},{112,48},{120,56},{... | collective-permute-start | bytes 1179656 | tf_op jit(solution)/shard_map/keys_and_values/ppermute | solution.py:43
  47.6 2.3 %collective-permute-done.14 = bf16[256,256]{1,0:T(8,128)(2,1)S(1)} collective-permute-done((bf16[256,256]{1,0:T(8,128)(2,1)S(1)}, bf16[256,256]{1,0:T(8,128)(2,1)S(1)}, u32[]{:S(2)}, u32[]{:S(2)}) %collective-permute-start.14) | collective-permute-done | bytes 131104 | tf_op jit(solution)/shard_map/keys_and_values/ppermute | solution.py:34
  49.9 3.6 %collective-permute-done.15 = bf16[256,256]{1,0:T(8,128)(2,1)S(1)} collective-permute-done((bf16[256,256]{1,0:T(8,128)(2,1)S(1)}, bf16[256,256]{1,0:T(8,128)(2,1)S(1)}, u32[]{:S(2)}, u32[]{:S(2)}) %collective-permute-start.15) | collective-permute-done | bytes 131104 | tf_op jit(solution)/shard_map/keys_and_values/ppermute | solution.py:34
  53.5 4.9 %collective-permute-start.16 = (bf16[768,256]{1,0:T(8,128)(2,1)S(1)}, bf16[768,256]{1,0:T(8,128)(2,1)S(1)}, u32[]{:S(2)}, u32[]{:S(2)}) collective-permute-start(bf16[768,256]{1,0:T(8,128)(2,1)S(1)} %constant_dynamic-update-slice_fusion.5.refs_1_), channel_id=1, source_target_pairs={{0,64},{8,72},{16,80},{24,88},{32,96},{40,104},{48,112},{56,120},{... | collective-permute-start | bytes 1179656 | tf_op jit(solution)/shard_map/keys_and_values/ppermute | solution.py:43
  58.4 2.1 %collective-permute-start.9 = (bf16[512,256]{1,0:T(8,128)(2,1)S(1)}, bf16[512,256]{1,0:T(8,128)(2,1)S(1)}, u32[]{:S(2)}, u32[]{:S(2)}) collective-permute-start(bf16[512,256]{1,0:T(8,128)(2,1)S(1)} %slice.6), channel_id=1, source_target_pairs={{64,0},{72,8},{0,192},{8,200},{65,1},{73,9},{1,193},{9,201},{66,2}... | collective-permute-start | bytes 786440 | tf_op jit(solution)/shard_map/keys_and_values/ppermute | solution.py:43
  63.3 2.4 %collective-permute-done.16.refs_1_ = bf16[768,256]{1,0:T(8,128)(2,1)S(1)} collective-permute-done((bf16[768,256]{1,0:T(8,128)(2,1)S(1)}, bf16[768,256]{1,0:T(8,128)(2,1)S(1)}, u32[]{:S(2)}, u32[]{:S(2)}) %collective-permute-start.16) | collective-permute-done | bytes 393248 | tf_op jit(solution)/shard_map/keys_and_values/ppermute | solution.py:43
  66.3 5.5 %collective-permute-start.10 = (bf16[512,256]{1,0:T(8,128)(2,1)S(1)}, bf16[512,256]{1,0:T(8,128)(2,1)S(1)}, u32[]{:S(2)}, u32[]{:S(2)}) collective-permute-start(bf16[512,256]{1,0:T(8,128)(2,1)S(1)} %collective-permute-done.9), channel_id=1, source_target_pairs={{192,128},{200,136},{0,192},{8,200},{193,129},{201,137},{1,193},{9... | collective-permute-start | bytes 786440 | tf_op jit(solution)/shard_map/keys_and_values/ppermute | solution.py:43
  72.6 5.3 %collective-permute-done.10.refs_0_ = bf16[512,256]{1,0:T(8,128)(2,1)S(1)} collective-permute-done((bf16[512,256]{1,0:T(8,128)(2,1)S(1)}, bf16[512,256]{1,0:T(8,128)(2,1)S(1)}, u32[]{:S(2)}, u32[]{:S(2)}) %collective-permute-start.10) | collective-permute-done | bytes 262176 | tf_op jit(solution)/shard_map/keys_and_values/ppermute | solution.py:43
  78.9 2.4 %collective-permute-start.20 = (bf16[256,512]{1,0:T(8,128)(2,1)S(1)}, bf16[256,512]{1,0:T(8,128)(2,1)S(1)}, u32[]{:S(2)}, u32[]{:S(2)}) collective-permute-start(bf16[256,512]{1,0:T(8,128)(2,1)S(1)} %attention.3), channel_id=1, source_target_pairs={{0,66},{2,68},{4,70},{6,64},{64,2},{66,4},{68,6},{70,0},{1,67},{3,... | collective-permute-start | bytes 786440 | tf_op jit(solution)/shard_map/features/ppermute | solution.py:49
  82.6 2.6 %collective-permute-start.22 = (bf16[256,512]{1,0:T(8,128)(2,1)S(1)}, bf16[256,512]{1,0:T(8,128)(2,1)S(1)}, u32[]{:S(2)}, u32[]{:S(2)}) collective-permute-start(bf16[256,512]{1,0:T(8,128)(2,1)S(1)} %attention.3), channel_id=1, source_target_pairs={{0,68},{2,70},{4,64},{6,66},{64,4},{66,6},{68,0},{70,2},{1,69},{3,... | collective-permute-start | bytes 786440 | tf_op jit(solution)/shard_map/features/ppermute | solution.py:49
  86.6 15.0 %collective-permute-done.19 = bf16[256,512]{1,0:T(8,128)(2,1)S(1)} collective-permute-done((bf16[256,512]{1,0:T(8,128)(2,1)S(1)}, bf16[256,512]{1,0:T(8,128)(2,1)S(1)}, u32[]{:S(2)}, u32[]{:S(2)}) %collective-permute-start.19) | collective-permute-done | bytes 262176 | tf_op jit(solution)/shard_map/features/ppermute | solution.py:49
  101.6 3.4 %collective-permute-start.25 = (bf16[256,512]{1,0:T(8,128)(2,1)S(1)}, bf16[256,512]{1,0:T(8,128)(2,1)S(1)}, u32[]{:S(2)}, u32[]{:S(2)}) collective-permute-start(bf16[256,512]{1,0:T(8,128)(2,1)S(1)} %attention.3), channel_id=1, source_target_pairs={{0,6},{2,0},{4,2},{6,4},{1,7},{3,1},{5,3},{7,5},{8,14},{10,8},{12,... | collective-permute-start | bytes 786440 | tf_op jit(solution)/shard_map/features/ppermute | solution.py:34
  105.3 2.3 %collective-permute-start.23 = (bf16[1024,512]{1,0:T(8,128)(2,1)S(1)}, bf16[1024,512]{1,0:T(8,128)(2,1)S(1)}, u32[]{:S(2)}, u32[]{:S(2)}) collective-permute-start(bf16[1024,512]{1,0:T(8,128)(2,1)S(1)} %constant_dynamic-update-slice_fusion.8.mine), channel_id=1, source_target_pairs={{0,1},{1,0},{2,3},{3,2},{4,5},{5,4},{6,7},{7,6},{8,9},{9,8},{10,11... | collective-permute-start | bytes 3145736 | tf_op jit(solution)/shard_map/features/ppermute | solution.py:34
  108.7 3.3 %collective-permute-done.24 = bf16[256,512]{1,0:T(8,128)(2,1)S(1)} collective-permute-done((bf16[256,512]{1,0:T(8,128)(2,1)S(1)}, bf16[256,512]{1,0:T(8,128)(2,1)S(1)}, u32[]{:S(2)}, u32[]{:S(2)}) %collective-permute-start.24) | collective-permute-done | bytes 262176 | tf_op jit(solution)/shard_map/features/ppermute | solution.py:34
  112.1 3.1 %collective-permute-start.27 = (bf16[1024,512]{1,0:T(8,128)(2,1)S(1)}, bf16[1024,512]{1,0:T(8,128)(2,1)}, u32[]{:S(2)}, u32[]{:S(2)}) collective-permute-start(bf16[1024,512]{1,0:T(8,128)(2,1)S(1)} %pad_maximum_fusion.mine), channel_id=1, source_target_pairs={{0,1},{1,0},{2,3},{3,2},{4,5},{5,4},{6,7},{7,6},{8,9},{9,8},{10,11... | collective-permute-start | bytes 3145736 | tf_op jit(solution)/shard_map/features/ppermute | solution.py:34
  116.3 4.9 %all-gather.2.cloned.1.call-done.weight = bf16[4096,896]{1,0:T(8,128)(2,1)} async-done(((bf16[512,896]{1,0:T(8,128)(2,1)}), bf16[4096,896]{1,0:T(8,128)(2,1)}) %all-gather.2.cloned.1.call-update) | async-done | bytes 7340048 | tf_op jit(solution)/shard_map/weight_rows/all_gather | solution.py:383
  121.2 3.2 %gate.5 = (bf16[256,512]{1,0:T(8,128)(2,1)S(1)}, bf16[4096,896]{1,0:T(8,128)(2,1)S(1)}) custom-call(bf16[256,4096]{1,0:T(8,128)(2,1)S(1)} %get-tuple-element.50.rows, f32[256,128]{1,0:T(8,128)S(1)} %get-tuple-element.54.inv, bf16[4096,896]{1,0:T(8,128)(2,1)} %all-gather.2.cloned.1.call-done.weight), custom_call_target="tpu_custom_call" | custom-call | tf_op jit(solution)/shard_map/gate/pallas_call | solution.py:324
  127.4 2.3 %gate.7 = (bf16[256,4096]{1,0:T(8,128)(2,1)S(1)}, f32[256,128]{1,0:T(8,128)S(1)}) custom-call(f32[1,4096]{1,0:T(1,128)S(1)} %bitcast.2, bf16[1024,512]{1,0:T(8,128)(2,1)S(1)} %pad_maximum_fusion.mine, bf16[1024,512]{1,0:T(8,128)(2,1)} %collective-permute-done.27.other), custom_call_target="tpu_custom_call" | custom-call | tf_op jit(solution)/shard_map/gate/pallas_call | solution.py:285
  129.7 2.5 %gate.8.refs_0_ = bf16[256,896]{1,0:T(8,128)(2,1)S(1)} custom-call(bf16[256,4096]{1,0:T(8,128)(2,1)S(1)} %get-tuple-element.57.rows, f32[256,128]{1,0:T(8,128)S(1)} %get-tuple-element.58.inv, bf16[4096,896]{1,0:T(8,128)(2,1)S(1)} %get-tuple-element.55.weight), custom_call_target="tpu_custom_call" | custom-call | flops 1879048192 | bytes 7340032 | tf_op jit(solution)/shard_map/gate/pallas_call | solution.py:342
  132.1 4.0 %collective-permute-done.29.refs_2_ = bf16[256,384]{1,0:T(8,128)(2,1)S(1)} collective-permute-done((bf16[256,384]{1,0:T(8,128)(2,1)S(1)}, bf16[256,384]{1,0:T(8,128)(2,1)S(1)}, u32[]{:S(2)}, u32[]{:S(2)}) %collective-permute-start.29) | collective-permute-done | bytes 196640 | tf_op jit(solution)/shard_map/gate/ppermute | solution.py:34
  (61 shorter events, 20.8 us)
Async XLA Ops:
  6.5 114.7 %all-gather.2.cloned.1.call-start = ((), (), s32[]{:S(2)}) async-start(), calls=%async_computation | async-start | bytes 8257536 | tf_op jit(solution)/shard_map/weight_rows/all_gather | solution.py:383
  8.7 14.1 %collective-permute-start.2 = (bf16[128,896]{1,0:T(8,128)(2,1)S(1)}, bf16[128,896]{1,0:T(8,128)(2,1)S(1)}, u32[]{:S(2)}, u32[]{:S(2)}) collective-permute-start(bf16[128,896]{1,0:T(8,128)(2,1)S(1)} %get-tuple-element.36), channel_id=1, source_target_pairs={{0,64},{64,128},{128,192},{192,0},{1,65},{65,129},{129,193},{193,1... | collective-permute-start | bytes 688136 | tf_op jit(solution)/shard_map/rows_to_owners/ppermute | solution.py:34
  10.9 11.9 %collective-permute-start.3 = (bf16[128,896]{1,0:T(8,128)(2,1)S(1)}, bf16[128,896]{1,0:T(8,128)(2,1)S(1)}, u32[]{:S(2)}, u32[]{:S(2)}) collective-permute-start(bf16[128,896]{1,0:T(8,128)(2,1)S(1)} %get-tuple-element.36), channel_id=1, source_target_pairs={{0,192},{64,0},{128,64},{192,128},{1,193},{65,1},{129,65},{193,129... | collective-permute-start | bytes 688136 | tf_op jit(solution)/shard_map/rows_to_owners/ppermute | solution.py:34
  12.4 13.1 %collective-permute-start.4 = (bf16[128,896]{1,0:T(8,128)(2,1)S(1)}, bf16[128,896]{1,0:T(8,128)(2,1)S(1)}, u32[]{:S(2)}, u32[]{:S(2)}) collective-permute-start(bf16[128,896]{1,0:T(8,128)(2,1)S(1)} %get-tuple-element.35.own_part), channel_id=1, source_target_pairs={{0,128},{64,192},{128,0},{192,64},{1,129},{65,193},{129,1},{193,65... | collective-permute-start | bytes 688136 | tf_op jit(solution)/shard_map/rows_to_owners/ppermute | solution.py:34
  14.0 8.8 %collective-permute-start = (bf16[64,768]{1,0:T(8,128)(2,1)S(1)}, bf16[64,768]{1,0:T(8,128)(2,1)S(1)}, u32[]{:S(2)}, u32[]{:S(2)}) collective-permute-start(bf16[64,768]{1,0:T(8,128)(2,1)S(1)} %get-tuple-element.33), channel_id=1, source_target_pairs={{0,8},{8,16},{16,24},{24,32},{32,40},{40,48},{48,56},{56,64},{64,7... | collective-permute-start | bytes 294920 | tf_op jit(solution)/shard_map/rows_to_owners/ppermute | solution.py:144
  15.6 7.2 %collective-permute-start.1 = (bf16[64,768]{1,0:T(8,128)(2,1)S(1)}, bf16[64,768]{1,0:T(8,128)(2,1)S(1)}, u32[]{:S(2)}, u32[]{:S(2)}) collective-permute-start(bf16[64,768]{1,0:T(8,128)(2,1)S(1)} %get-tuple-element.34), channel_id=1, source_target_pairs={{0,248},{8,0},{16,8},{24,16},{32,24},{40,32},{48,40},{56,48},{64,5... | collective-permute-start | bytes 294920 | tf_op jit(solution)/shard_map/rows_to_owners/ppermute | solution.py:145
  27.2 5.9 %collective-permute-start.5 = (bf16[256,256]{1,0:T(8,128)(2,1)S(1)}, bf16[256,256]{1,0:T(8,128)(2,1)S(1)}, u32[]{:S(2)}, u32[]{:S(2)}) collective-permute-start(bf16[256,256]{1,0:T(8,128)(2,1)S(1)} %get-tuple-element.38), channel_id=1, source_target_pairs={{0,8},{8,16},{16,24},{24,32},{32,40},{40,48},{48,56},{56,0},{1,9},... | collective-permute-start | bytes 393224 | tf_op jit(solution)/shard_map/keys_and_values/ppermute | solution.py:34
  27.3 5.8 %collective-permute-start.7 = (bf16[256,256]{1,0:T(8,128)(2,1)S(1)}, bf16[256,256]{1,0:T(8,128)(2,1)S(1)}, u32[]{:S(2)}, u32[]{:S(2)}) collective-permute-start(bf16[256,256]{1,0:T(8,128)(2,1)S(1)} %get-tuple-element.38), channel_id=1, source_target_pairs={{0,56},{8,0},{16,8},{24,16},{32,24},{40,32},{48,40},{56,48},{1,57}... | collective-permute-start | bytes 393224 | tf_op jit(solution)/shard_map/keys_and_values/ppermute | solution.py:34
  33.1 5.0 %collective-permute-start.6 = (bf16[256,256]{1,0:T(8,128)(2,1)S(1)}, bf16[256,256]{1,0:T(8,128)(2,1)S(1)}, u32[]{:S(2)}, u32[]{:S(2)}) collective-permute-start(bf16[256,256]{1,0:T(8,128)(2,1)S(1)} %collective-permute-done.5), channel_id=1, source_target_pairs={{0,8},{8,16},{16,24},{24,32},{32,40},{40,48},{48,56},{56,0},{1,9},... | collective-permute-start | bytes 393224 | tf_op jit(solution)/shard_map/keys_and_values/ppermute | solution.py:34
  33.1 5.1 %collective-permute-start.8 = (bf16[256,256]{1,0:T(8,128)(2,1)S(1)}, bf16[256,256]{1,0:T(8,128)(2,1)S(1)}, u32[]{:S(2)}, u32[]{:S(2)}) collective-permute-start(bf16[256,256]{1,0:T(8,128)(2,1)S(1)} %collective-permute-done.7), channel_id=1, source_target_pairs={{0,56},{8,0},{16,8},{24,16},{32,24},{40,32},{48,40},{56,48},{1,57}... | collective-permute-start | bytes 393224 | tf_op jit(solution)/shard_map/keys_and_values/ppermute | solution.py:34
  38.3 9.3 %collective-permute-start.13 = (bf16[256,256]{1,0:T(8,128)(2,1)S(1)}, bf16[256,256]{1,0:T(8,128)(2,1)S(1)}, u32[]{:S(2)}, u32[]{:S(2)}) collective-permute-start(bf16[256,256]{1,0:T(8,128)(2,1)S(1)} %collective-permute-done.8), channel_id=1, source_target_pairs={{0,56},{8,0},{16,8},{24,16},{32,24},{40,32},{48,40},{56,48},{1,57}... | collective-permute-start | bytes 393224 | tf_op jit(solution)/shard_map/keys_and_values/ppermute | solution.py:34
  41.0 8.9 %collective-permute-start.14 = (bf16[256,256]{1,0:T(8,128)(2,1)S(1)}, bf16[256,256]{1,0:T(8,128)(2,1)S(1)}, u32[]{:S(2)}, u32[]{:S(2)}) collective-permute-start(bf16[256,256]{1,0:T(8,128)(2,1)S(1)} %collective-permute-done.6), channel_id=1, source_target_pairs={{0,16},{8,24},{16,32},{24,40},{32,48},{40,56},{48,0},{56,8},{1,17}... | collective-permute-start | bytes 393224 | tf_op jit(solution)/shard_map/keys_and_values/ppermute | solution.py:34
  41.0 12.5 %collective-permute-start.15 = (bf16[256,256]{1,0:T(8,128)(2,1)S(1)}, bf16[256,256]{1,0:T(8,128)(2,1)S(1)}, u32[]{:S(2)}, u32[]{:S(2)}) collective-permute-start(bf16[256,256]{1,0:T(8,128)(2,1)S(1)} %collective-permute-done.6), channel_id=1, source_target_pairs={{0,8},{8,16},{16,24},{24,32},{32,40},{40,48},{48,56},{56,0},{1,9},... | collective-permute-start | bytes 393224 | tf_op jit(solution)/shard_map/keys_and_values/ppermute | solution.py:34
  42.9 22.7 %collective-permute-start.17 = (bf16[1280,256]{1,0:T(8,128)(2,1)S(1)}, bf16[1280,256]{1,0:T(8,128)(2,1)S(1)}, u32[]{:S(2)}, u32[]{:S(2)}) collective-permute-start(bf16[1280,256]{1,0:T(8,128)(2,1)S(1)} %constant_dynamic-update-slice_fusion.refs_0_), channel_id=1, source_target_pairs={{0,64},{8,72},{16,80},{24,88},{32,96},{40,104},{48,112},{56,120},{... | collective-permute-start | bytes 1966088 | tf_op jit(solution)/shard_map/keys_and_values/ppermute | solution.py:43
  45.6 16.3 %collective-permute-start.11 = (bf16[768,256]{1,0:T(8,128)(2,1)S(1)}, bf16[768,256]{1,0:T(8,128)(2,1)S(1)}, u32[]{:S(2)}, u32[]{:S(2)}) collective-permute-start(bf16[768,256]{1,0:T(8,128)(2,1)S(1)} %slice.7), channel_id=1, source_target_pairs={{64,0},{72,8},{80,16},{88,24},{96,32},{104,40},{112,48},{120,56},{... | collective-permute-start | bytes 1179656 | tf_op jit(solution)/shard_map/keys_and_values/ppermute | solution.py:43
  53.5 12.1 %collective-permute-start.16 = (bf16[768,256]{1,0:T(8,128)(2,1)S(1)}, bf16[768,256]{1,0:T(8,128)(2,1)S(1)}, u32[]{:S(2)}, u32[]{:S(2)}) collective-permute-start(bf16[768,256]{1,0:T(8,128)(2,1)S(1)} %constant_dynamic-update-slice_fusion.5.refs_1_), channel_id=1, source_target_pairs={{0,64},{8,72},{16,80},{24,88},{32,96},{40,104},{48,112},{56,120},{... | collective-permute-start | bytes 1179656 | tf_op jit(solution)/shard_map/keys_and_values/ppermute | solution.py:43
  58.4 7.9 %collective-permute-start.9 = (bf16[512,256]{1,0:T(8,128)(2,1)S(1)}, bf16[512,256]{1,0:T(8,128)(2,1)S(1)}, u32[]{:S(2)}, u32[]{:S(2)}) collective-permute-start(bf16[512,256]{1,0:T(8,128)(2,1)S(1)} %slice.6), channel_id=1, source_target_pairs={{64,0},{72,8},{0,192},{8,200},{65,1},{73,9},{1,193},{9,201},{66,2}... | collective-permute-start | bytes 786440 | tf_op jit(solution)/shard_map/keys_and_values/ppermute | solution.py:43
  61.9 15.9 %collective-permute-start.12 = (bf16[768,256]{1,0:T(8,128)(2,1)S(1)}, bf16[768,256]{1,0:T(8,128)(2,1)S(1)}, u32[]{:S(2)}, u32[]{:S(2)}) collective-permute-start(bf16[768,256]{1,0:T(8,128)(2,1)S(1)} %collective-permute-done.11), channel_id=1, source_target_pairs={{192,128},{200,136},{208,144},{216,152},{224,160},{232,168},{240,1... | collective-permute-start | bytes 1179656 | tf_op jit(solution)/shard_map/keys_and_values/ppermute | solution.py:43
  65.6 12.3 %collective-permute-start.18 = (bf16[768,256]{1,0:T(8,128)(2,1)S(1)}, bf16[768,256]{1,0:T(8,128)(2,1)S(1)}, u32[]{:S(2)}, u32[]{:S(2)}) collective-permute-start(bf16[768,256]{1,0:T(8,128)(2,1)S(1)} %collective-permute-done.16.refs_1_), channel_id=1, source_target_pairs={{64,128},{72,136},{80,144},{88,152},{96,160},{128,192},{136,200},{... | collective-permute-start | bytes 1179656 | tf_op jit(solution)/shard_map/keys_and_values/ppermute | solution.py:43
  66.3 11.6 %collective-permute-start.10 = (bf16[512,256]{1,0:T(8,128)(2,1)S(1)}, bf16[512,256]{1,0:T(8,128)(2,1)S(1)}, u32[]{:S(2)}, u32[]{:S(2)}) collective-permute-start(bf16[512,256]{1,0:T(8,128)(2,1)S(1)} %collective-permute-done.9), channel_id=1, source_target_pairs={{192,128},{200,136},{0,192},{8,200},{193,129},{201,137},{1,193},{9... | collective-permute-start | bytes 786440 | tf_op jit(solution)/shard_map/keys_and_values/ppermute | solution.py:43
  78.8 36.5 %copy-start = (f32[4096]{0:T(1024)S(1)}, f32[4096]{0:T(1024)}, u32[]{:S(2)}) copy-start(f32[4096]{0:T(1024)} %param.12) | copy-start | bytes 49156
  78.8 22.8 %collective-permute-start.19 = (bf16[256,512]{1,0:T(8,128)(2,1)S(1)}, bf16[256,512]{1,0:T(8,128)(2,1)S(1)}, u32[]{:S(2)}, u32[]{:S(2)}) collective-permute-start(bf16[256,512]{1,0:T(8,128)(2,1)S(1)} %attention.3), channel_id=1, source_target_pairs={{0,64},{2,66},{4,68},{6,70},{64,0},{66,2},{68,4},{70,6},{1,65},{3,... | collective-permute-start | bytes 786440 | tf_op jit(solution)/shard_map/features/ppermute | solution.py:49
  78.9 26.2 %collective-permute-start.20 = (bf16[256,512]{1,0:T(8,128)(2,1)S(1)}, bf16[256,512]{1,0:T(8,128)(2,1)S(1)}, u32[]{:S(2)}, u32[]{:S(2)}) collective-permute-start(bf16[256,512]{1,0:T(8,128)(2,1)S(1)} %attention.3), channel_id=1, source_target_pairs={{0,66},{2,68},{4,70},{6,64},{64,2},{66,4},{68,6},{70,0},{1,67},{3,... | collective-permute-start | bytes 786440 | tf_op jit(solution)/shard_map/features/ppermute | solution.py:49
  81.3 23.9 %collective-permute-start.21 = (bf16[256,512]{1,0:T(8,128)(2,1)S(1)}, bf16[256,512]{1,0:T(8,128)(2,1)S(1)}, u32[]{:S(2)}, u32[]{:S(2)}) collective-permute-start(bf16[256,512]{1,0:T(8,128)(2,1)S(1)} %attention.3), channel_id=1, source_target_pairs={{0,70},{2,64},{4,66},{6,68},{64,6},{66,0},{68,2},{70,4},{1,71},{3,... | collective-permute-start | bytes 786440 | tf_op jit(solution)/shard_map/features/ppermute | solution.py:49
  82.6 22.6 %collective-permute-start.22 = (bf16[256,512]{1,0:T(8,128)(2,1)S(1)}, bf16[256,512]{1,0:T(8,128)(2,1)S(1)}, u32[]{:S(2)}, u32[]{:S(2)}) collective-permute-start(bf16[256,512]{1,0:T(8,128)(2,1)S(1)} %attention.3), channel_id=1, source_target_pairs={{0,68},{2,70},{4,64},{6,66},{64,4},{66,6},{68,0},{70,2},{1,69},{3,... | collective-permute-start | bytes 786440 | tf_op jit(solution)/shard_map/features/ppermute | solution.py:49
  85.2 22.4 %collective-permute-start.26 = (bf16[256,512]{1,0:T(8,128)(2,1)S(1)}, bf16[256,512]{1,0:T(8,128)(2,1)S(1)}, u32[]{:S(2)}, u32[]{:S(2)}) collective-permute-start(bf16[256,512]{1,0:T(8,128)(2,1)S(1)} %attention.3), channel_id=1, source_target_pairs={{0,4},{2,6},{4,0},{6,2},{1,5},{3,7},{5,1},{7,3},{8,12},{10,14},{12... | collective-permute-start | bytes 786440 | tf_op jit(solution)/shard_map/features/ppermute | solution.py:34
  101.6 7.1 %collective-permute-start.25 = (bf16[256,512]{1,0:T(8,128)(2,1)S(1)}, bf16[256,512]{1,0:T(8,128)(2,1)S(1)}, u32[]{:S(2)}, u32[]{:S(2)}) collective-permute-start(bf16[256,512]{1,0:T(8,128)(2,1)S(1)} %attention.3), channel_id=1, source_target_pairs={{0,6},{2,0},{4,2},{6,4},{1,7},{3,1},{5,3},{7,5},{8,14},{10,8},{12,... | collective-permute-start | bytes 786440 | tf_op jit(solution)/shard_map/features/ppermute | solution.py:34
  105.1 7.0 %collective-permute-start.24 = (bf16[256,512]{1,0:T(8,128)(2,1)S(1)}, bf16[256,512]{1,0:T(8,128)(2,1)S(1)}, u32[]{:S(2)}, u32[]{:S(2)}) collective-permute-start(bf16[256,512]{1,0:T(8,128)(2,1)S(1)} %attention.3), channel_id=1, source_target_pairs={{0,2},{2,4},{4,6},{6,0},{1,3},{3,5},{5,7},{7,1},{8,10},{10,12},{12... | collective-permute-start | bytes 786440 | tf_op jit(solution)/shard_map/features/ppermute | solution.py:34
  105.3 10.0 %collective-permute-start.23 = (bf16[1024,512]{1,0:T(8,128)(2,1)S(1)}, bf16[1024,512]{1,0:T(8,128)(2,1)S(1)}, u32[]{:S(2)}, u32[]{:S(2)}) collective-permute-start(bf16[1024,512]{1,0:T(8,128)(2,1)S(1)} %constant_dynamic-update-slice_fusion.8.mine), channel_id=1, source_target_pairs={{0,1},{1,0},{2,3},{3,2},{4,5},{5,4},{6,7},{7,6},{8,9},{9,8},{10,11... | collective-permute-start | bytes 3145736 | tf_op jit(solution)/shard_map/features/ppermute | solution.py:34
  112.1 15.2 %collective-permute-start.27 = (bf16[1024,512]{1,0:T(8,128)(2,1)S(1)}, bf16[1024,512]{1,0:T(8,128)(2,1)}, u32[]{:S(2)}, u32[]{:S(2)}) collective-permute-start(bf16[1024,512]{1,0:T(8,128)(2,1)S(1)} %pad_maximum_fusion.mine), channel_id=1, source_target_pairs={{0,1},{1,0},{2,3},{3,2},{4,5},{5,4},{6,7},{7,6},{8,9},{9,8},{10,11... | collective-permute-start | bytes 3145736 | tf_op jit(solution)/shard_map/features/ppermute | solution.py:34
  124.4 11.7 %collective-permute-start.28 = (bf16[256,512]{1,0:T(8,128)(2,1)S(1)}, bf16[256,512]{1,0:T(8,128)(2,1)S(1)}, u32[]{:S(2)}, u32[]{:S(2)}) collective-permute-start(bf16[256,512]{1,0:T(8,128)(2,1)S(1)} %get-tuple-element.53), channel_id=1, source_target_pairs={{0,64},{64,0},{1,65},{65,1},{2,66},{66,2},{3,67},{67,3},{4,68},{68... | collective-permute-start | bytes 786440 | tf_op jit(solution)/shard_map/gate/ppermute | solution.py:34
  127.1 9.0 %collective-permute-start.29 = (bf16[256,384]{1,0:T(8,128)(2,1)S(1)}, bf16[256,384]{1,0:T(8,128)(2,1)S(1)}, u32[]{:S(2)}, u32[]{:S(2)}) collective-permute-start(bf16[256,384]{1,0:T(8,128)(2,1)S(1)} %gate.6), channel_id=1, source_target_pairs={{0,64},{64,0},{1,65},{65,1},{2,66},{66,2},{3,67},{67,3},{4,68},{68... | collective-permute-start | bytes 589832 | tf_op jit(solution)/shard_map/gate/ppermute | solution.py:34
  (1 other events, 33.3 us)
Sparse Core Ops, SparseCore 0:
  27.3 93.8 all-gather.1
